TPU v7x, 128 devices: a whole 4x4x4 slice. The times are simulated.
128 devices in a mesh: leaf: 16 (over z, x_lo, core), head: 8 (over x_hi, y).
Axes of the slice: x: 4 (x_hi: 2, x_lo: 2; x = x_hi * 2 + x_lo), y: 4, z: 4, core: 2. Of those that a mesh axis runs over, the one named last changes fastest.
Arguments:
- query_rows: bfloat16 [12288, 4096], P('leaf', 'head')
- key_rows: bfloat16 [12288, 256], P('leaf')
- value_rows: bfloat16 [12288, 256], P('leaf'), may hold values from -6 to 6
- out_weight: bfloat16 [4096, 4096], P('head'), may hold values from -0.09375 to 0.09375
- out_grad: bfloat16 [12288, 4096], P(('leaf', 'head')), may hold values from -6 to 6
- seg_owner: int32 [42], replicated, may hold values from 0 to 15, as said below
- seg_parent: int32 [42], replicated, may hold values from -1 to 25, as said below
- seg_offset: int32 [42], replicated, may hold values from 0 to 640, as said below
- seg_length: int32 [42], replicated, may hold values from 1 to 512, as said below
Outputs:
- layer_out: bfloat16 [12288, 4096], P(('leaf', 'head'))
- query_grads: bfloat16 [12288, 4096], P('leaf', 'head')
- key_grads: bfloat16 [12288, 256], P(('leaf', 'head'))
- value_grads: bfloat16 [12288, 256], P(('leaf', 'head'))
- weight_grad: bfloat16 [4096, 4096], P('head', 'leaf')
Inputs may be any that keep to these rules, and one draw needn't show every extreme that they name: seg_owner[i] is the leaf device of segment i; each device holds 2 leaves and at most one prompt or branch, never more than 768 live slots, and some device has all 768 slots live. `seg_parent`: segment 21 t is tree t's prompt (parent -1); 21 t + 1 to 21 t + 4 are its branches (parent 21 t); 21 t + 5 to 21 t + 20 are its leaves, four under each branch. Segment i fills slots seg_offset[i] to seg_offset[i] + seg_length[i] - 1 of its device, and no slot has two segments; every offset is a multiple of 128; a leaf's offset is at most 640, a branch's at most 512, a prompt's at most 256, and in every draw some leaf, some branch and some prompt sit at these latest offsets. `seg_length`: prompts have 512 tokens, branches 256, leaves at most 128, and one leaf of each tree exactly 128.
All inputs are finite; a program needn't handle non-finite values.
Results may differ from a plain program's by a relative error of at most 0.025.
Values may be sent and summed in bfloat16 or wider, within the bound.
No kernel may reach another device: no remote copies, remote signals or barrier semaphores. Data moves between devices by JAX's collectives and lax.ppermute only.
A program may use at most 192 MiB of HBM per device.

v0:
```python
import jax
import jax.numpy as jnp
from jax import lax
from jax.sharding import PartitionSpec as P

KV_HEADS = 2
HD = 128
GROUP = 16


NEG = -1e30
HIGH = lax.Precision.HIGHEST


def slot_table(first, count, row_count, seg_owner, seg_offset, seg_length):
    slot_index = first + jnp.arange(count, dtype=jnp.int32)
    device = slot_index // row_count
    place = slot_index % row_count
    inside = (
        (seg_owner[None, :] == device[:, None])
        & (seg_offset[None, :] <= place[:, None])
        & (place[:, None] < (seg_offset + seg_length)[None, :])
    )
    position = place - jnp.sum(jnp.where(inside, seg_offset[None, :], 0), axis=1)
    return (inside.astype(jnp.float32), position)


def visible(query_table, key_table, lineage):
    query_hot, query_pos = query_table
    key_hot, key_pos = key_table
    same = jnp.dot(query_hot, key_hot.T, precision=HIGH)
    elder = jnp.dot(jnp.dot(query_hot, lineage, precision=HIGH), key_hot.T, precision=HIGH)
    return (elder > 0.5) | (same > 0.5) & (key_pos[None, :] <= query_pos[:, None])


def head_scores(query_heads, key_block):
    return jnp.einsum(
        "qhd,kd->hqk", query_heads, key_block, preferred_element_type=jnp.float32
    ) * HD ** (-0.5)


def shards(
    query_rows,
    key_rows,
    value_rows,
    out_weight,
    out_grad,
    seg_owner,
    seg_parent,
    seg_offset,
    seg_length,
):
    row_count = query_rows.shape[0]
    width = query_rows.shape[1]
    head_count = width // HD
    leaf_count = lax.axis_size("leaf")
    slot_count = row_count * leaf_count
    group = lax.axis_index("head") * head_count // GROUP
    segments = seg_parent.shape[0]
    parent_hot = (seg_parent[:, None] == jnp.arange(segments, dtype=jnp.int32)[None, :]).astype(
        jnp.float32
    )
    lineage = parent_hot + jnp.dot(parent_hot, parent_hot, precision=HIGH)
    own_table = slot_table(
        lax.axis_index("leaf") * row_count, row_count, row_count, seg_owner, seg_offset, seg_length
    )
    live = jnp.sum(own_table[0], axis=1)
    query_heads = query_rows.reshape(row_count, head_count, HD)
    key_mine = lax.dynamic_slice_in_dim(key_rows, group * HD, HD, 1)
    value_mine = lax.dynamic_slice_in_dim(value_rows, group * HD, HD, 1)
    gathered = lax.all_gather(jnp.stack([key_mine, value_mine]), "leaf", axis=1, tiled=True)

    def sweep(step, carry):

        def shard_loop(shard, carry):
            carry = step(carry, shard * row_count + 0)
            return carry

        return lax.fori_loop(0, leaf_count, shard_loop, carry)

    def block_view(first):
        table = slot_table(first, row_count, row_count, seg_owner, seg_offset, seg_length)
        mask = visible(own_table, table, lineage)
        pair = lax.dynamic_slice_in_dim(gathered, first, row_count, 1)
        return (mask, pair)

    def stat_step(carry, first):
        mask, pair = block_view(first)

        def stat_work(carry):
            row_top, row_total = carry
            scores = jnp.where(mask[None], head_scores(query_heads, pair[0]), NEG)
            new_top = jnp.maximum(row_top, jnp.max(scores, axis=2))
            weights = jnp.exp(scores - new_top[:, :, None]) * mask[None]
            return (new_top, row_total * jnp.exp(row_top - new_top) + jnp.sum(weights, axis=2))

        return lax.cond(jnp.any(mask), stat_work, lambda kept: kept, carry)

    start_top = jnp.full((head_count, row_count), NEG, jnp.float32)
    row_top, row_total = sweep(
        stat_step, (start_top, jnp.zeros((head_count, row_count), jnp.float32))
    )
    row_total = row_total + (1.0 - live)[None, :]

    def probabilities(mask, pair):
        scores = jnp.where(mask[None], head_scores(query_heads, pair[0]), NEG)
        return jnp.exp(scores - row_top[:, :, None]) / row_total[:, :, None] * mask[None]

    def value_step(running, first):
        mask, pair = block_view(first)

        def value_work(running):
            probs = probabilities(mask, pair).astype(jnp.bfloat16)
            return running + jnp.einsum(
                "hqk,kd->qhd", probs, pair[1], preferred_element_type=jnp.float32
            )

        return lax.cond(jnp.any(mask), value_work, lambda kept: kept, running)

    attn = (
        sweep(value_step, jnp.zeros((row_count, head_count, HD), jnp.float32))
        .astype(jnp.bfloat16)
        .reshape(row_count, width)
    )
    layer_out = lax.psum_scatter(
        jnp.dot(attn, out_weight, preferred_element_type=jnp.float32).astype(jnp.bfloat16),
        "head",
        scatter_dimension=0,
        tiled=True,
    )
    piece = lax.all_gather(out_grad, "head", axis=0, tiled=True)
    weight_sum = lax.dot_general(
        attn, piece, (((0,), (0,)), ((), ())), preferred_element_type=jnp.float32
    )
    rows_grad = lax.dot_general(
        piece, out_weight, (((1,), (1,)), ((), ())), preferred_element_type=jnp.float32
    )
    attn_sum = rows_grad
    weight_sum, attn_sum = (weight_sum, attn_sum)
    weight_grad = lax.psum_scatter(
        weight_sum.astype(jnp.bfloat16), "leaf", scatter_dimension=1, tiled=True
    )
    attn_grad = attn_sum.astype(jnp.bfloat16)
    grad_heads = attn_grad.reshape(row_count, head_count, HD)
    delta = jnp.transpose(
        jnp.sum(
            grad_heads.astype(jnp.float32)
            * attn.reshape(row_count, head_count, HD).astype(jnp.float32),
            axis=2,
        )
    )

    def score_grads(mask, pair):
        probs_f = probabilities(mask, pair)
        dprobs = jnp.einsum("qhd,kd->hqk", grad_heads, pair[1], preferred_element_type=jnp.float32)
        dscores = (probs_f * (dprobs - delta[:, :, None]) * HD ** (-0.5)).astype(jnp.bfloat16)
        return (probs_f.astype(jnp.bfloat16), dscores)

    def block_terms(mask, pair):
        probs, dscores = score_grads(mask, pair)
        query_part = jnp.einsum("hqk,kd->qhd", dscores, pair[0], preferred_element_type=jnp.float32)
        key_part = jnp.einsum(
            "hqk,qhd->kd", dscores, query_heads, preferred_element_type=jnp.float32
        )
        value_part = jnp.einsum(
            "hqk,qhd->kd", probs, grad_heads, preferred_element_type=jnp.float32
        )
        return (query_part, jnp.stack([key_part, value_part]))

    query_start = jnp.zeros((row_count, head_count, HD), jnp.float32)

    def grad_step(carry, first):
        mask, pair = block_view(first)

        def grad_work(carry):
            query_acc, pair_acc = carry
            query_part, terms = block_terms(mask, pair)
            prior_rows = lax.dynamic_slice_in_dim(pair_acc, first, row_count, 1)
            pair_acc = lax.dynamic_update_slice_in_dim(pair_acc, prior_rows + terms, first, 1)
            return (query_acc + query_part, pair_acc)

        return lax.cond(jnp.any(mask), grad_work, lambda kept: kept, carry)

    query_acc, pair_acc = sweep(
        grad_step, (query_start, jnp.zeros((2, slot_count, HD), jnp.float32))
    )
    pair_local = lax.psum_scatter(
        pair_acc.astype(jnp.bfloat16), "leaf", scatter_dimension=1, tiled=True
    ).astype(jnp.float32)
    term = lax.dynamic_update_slice_in_dim(
        jnp.zeros((2, row_count, KV_HEADS * HD), jnp.float32), pair_local, group * HD, 2
    )
    pair_grads = lax.psum_scatter(
        term.astype(jnp.bfloat16), "head", scatter_dimension=1, tiled=True
    ).astype(jnp.float32)
    query_grads = query_acc.astype(jnp.bfloat16).reshape(row_count, width)
    return (
        layer_out,
        query_grads,
        pair_grads[0].astype(jnp.bfloat16),
        pair_grads[1].astype(jnp.bfloat16),
        weight_grad,
    )


def solution(mesh):
    return jax.shard_map(
        shards,
        mesh=mesh,
        in_specs=(
            P("leaf", "head"),
            P("leaf", None),
            P("leaf", None),
            P("head", None),
            P(("leaf", "head"), None),
            P(),
            P(),
            P(),
            P(),
        ),
        out_specs=(
            P(("leaf", "head"), None),
            P("leaf", "head"),
            P(("leaf", "head"), None),
            P(("leaf", "head"), None),
            P("head", "leaf"),
        ),
        check_vma=False,
    )
```

profile of v0, /device:TPU:0, one launch (start us, length us, event | category | flops | bytes accessed | tf_op | source)
XLA Modules:
  0.0 890.7 jit_solution(17205671807933934811)
XLA Ops:
  18.0 37.2 %all-gather.3.cloned.1.call-done = bf16[2,12288,128]{2,1,0:T(8,128)(2,1)} async-done(((bf16[2,768,128]{2,1,0:T(8,128)(2,1)}), bf16[2,12288,128]{2,1,0:T(8,128)(2,1)}) %all-gather.3.cloned.1.call-update) | async-done | bytes 6291472 | tf_op jit(solution)/shard_map/all_gather | solution.py:71
  55.2 128.0 %while.58 = (s32[]{:T(128)}, f32[4,768]{1,0:T(4,128)S(1)}, f32[4,768]{1,0:T(4,128)S(1)}, s32[42]{0:T(128)S(1)}, s32[42]{0:T(128)}, /*index=5*/s32[1,42]{1,0:T(1,...) while((s32[]{:T(128)}, f32[4,768]{1,0:T(4,128)S(1)}, ...), condition=%wide.region_8.9_spmd.clone.clone, body=%wide.region_1.0_spmd.clone.clone.sunk | while | flops 1222321152 | bytes 31990708 | solution.py:79
  61.5 5.3 conditional.12
  73.2 5.3 conditional.12
  135.5 5.3 conditional.12
  159.8 5.3 conditional.12
  177.8 5.3 conditional.12
  185.0 156.4 %while.59 = (s32[]{:T(128)}, f32[768,4,128]{2,0,1:T(8,128)}, s32[42]{0:T(128)S(1)}, s32[42]{0:T(128)}, s32[1,42]{1,0:T(1,128)}, /*index=5*/f32[768,42]{1,0:T(8,1...) while((s32[]{:T(128)}, f32[768,4,128]{2,0,1:T(8,128)}, ...), condition=%wide.region_15.16_spmd.clone.clone, body=%wide.region_10.15_spmd.clone.clone.sunk | while | flops 1821969408 | bytes 15735213 | solution.py:79
  187.7 3.8 fusion.153
  192.1 8.4 conditional.13
  193.4 7.2 bitcast_add_fusion
  203.2 3.8 fusion.153
  207.6 8.4 conditional.13
  208.9 7.2 bitcast_add_fusion
  218.8 3.8 fusion.153
  225.9 3.8 fusion.153
  233.1 3.8 fusion.153
  240.2 3.8 fusion.153
  247.4 3.8 fusion.153
  261.7 3.8 fusion.153
  280.4 8.4 conditional.13
  281.7 7.2 bitcast_add_fusion
  305.9 3.8 fusion.153
  310.3 8.4 conditional.13
  311.5 7.2 bitcast_add_fusion
  321.4 3.8 fusion.153
  333.0 8.4 conditional.13
  334.2 7.2 bitcast_add_fusion
  343.1 8.3 multiply_reduce_fusion.1
  351.9 5.0 broadcast_in_dim.189
  356.9 192.4 %while.60 = (s32[]{:T(128)}, f32[768,4,128]{2,0,1:T(8,128)S(1)}, f32[2,12288,128]{2,1,0:T(8,128)}, s32[42]{0:T(128)S(1)}, s32[42]{0:T(128)}, /*index=5*/s32[1,42...) while((s32[]{:T(128)}, f32[768,4,128]{2,0,1:T(8,128)S(1)}, ...), condition=%wide.region_23.24_spmd.clone.clone, body=%wide.region_18.23_spmd.clone.clone.sunk | while | flops 3643739136 | bytes 63964200 | solution.py:79
  359.6 3.8 fusion.158
  364.0 15.6 %conditional.14 = ((f32[768,4,128]{2,0,1:T(8,128)S(1)}, f32[2,12288,128]{2,1,0:T(8,128)})) conditional(s32[]{:T(128)} %convert_element_type.188, (f32[768,4,128]{2,0,1:T(8,128)S(1)}, f32[2,12288,128]{2,1,0:T(8,128)}) %tuple.217, (pred[768,768]{0,1:T(8,128)(4,1)}, s32[]{:T(128)}, bf16[2,12288,128]{2,1,0:T(8,128)(2,1)}, ...), branch_computations={%region_21.21_spmd, %region_22.22_spmd} | conditional | flops 3044868096 | bytes 58478708 | solution.py:182
  365.3 4.4 fusion.30
  382.3 3.8 fusion.158
  386.7 15.6 %conditional.14 = ((f32[768,4,128]{2,0,1:T(8,128)S(1)}, f32[2,12288,128]{2,1,0:T(8,128)})) conditional(s32[]{:T(128)} %convert_element_type.188, (f32[768,4,128]{2,0,1:T(8,128)S(1)}, f32[2,12288,128]{2,1,0:T(8,128)}) %tuple.217, (pred[768,768]{0,1:T(8,128)(4,1)}, s32[]{:T(128)}, bf16[2,12288,128]{2,1,0:T(8,128)(2,1)}, ...), branch_computations={%region_21.21_spmd, %region_22.22_spmd} | conditional | flops 3044868096 | bytes 58478708 | solution.py:182
  388.0 4.4 fusion.30
  405.0 3.8 fusion.158
  412.1 3.8 fusion.158
  419.3 3.8 fusion.158
  426.5 3.8 fusion.158
  433.7 3.8 fusion.158
  440.8 3.8 fusion.158
  448.0 3.8 fusion.158
  455.2 3.8 fusion.158
  462.4 3.8 fusion.158
  466.8 15.5 %conditional.14 = ((f32[768,4,128]{2,0,1:T(8,128)S(1)}, f32[2,12288,128]{2,1,0:T(8,128)})) conditional(s32[]{:T(128)} %convert_element_type.188, (f32[768,4,128]{2,0,1:T(8,128)S(1)}, f32[2,12288,128]{2,1,0:T(8,128)}) %tuple.217, (pred[768,768]{0,1:T(8,128)(4,1)}, s32[]{:T(128)}, bf16[2,12288,128]{2,1,0:T(8,128)(2,1)}, ...), branch_computations={%region_21.21_spmd, %region_22.22_spmd} | conditional | flops 3044868096 | bytes 58478708 | solution.py:182
  468.1 4.4 fusion.30
  485.0 3.8 fusion.158
  492.2 3.8 fusion.158
  499.4 3.8 fusion.158
  503.8 15.6 %conditional.14 = ((f32[768,4,128]{2,0,1:T(8,128)S(1)}, f32[2,12288,128]{2,1,0:T(8,128)})) conditional(s32[]{:T(128)} %convert_element_type.188, (f32[768,4,128]{2,0,1:T(8,128)S(1)}, f32[2,12288,128]{2,1,0:T(8,128)}) %tuple.217, (pred[768,768]{0,1:T(8,128)(4,1)}, s32[]{:T(128)}, bf16[2,12288,128]{2,1,0:T(8,128)(2,1)}, ...), branch_computations={%region_21.21_spmd, %region_22.22_spmd} | conditional | flops 3044868096 | bytes 58478708 | solution.py:182
  505.1 4.4 fusion.30
  522.1 3.8 fusion.158
  529.3 3.8 fusion.158
  533.7 15.6 %conditional.14 = ((f32[768,4,128]{2,0,1:T(8,128)S(1)}, f32[2,12288,128]{2,1,0:T(8,128)})) conditional(s32[]{:T(128)} %convert_element_type.188, (f32[768,4,128]{2,0,1:T(8,128)S(1)}, f32[2,12288,128]{2,1,0:T(8,128)}) %tuple.217, (pred[768,768]{0,1:T(8,128)(4,1)}, s32[]{:T(128)}, bf16[2,12288,128]{2,1,0:T(8,128)(2,1)}, ...), branch_computations={%region_21.21_spmd, %region_22.22_spmd} | conditional | flops 3044868096 | bytes 58478708 | solution.py:182
  535.0 4.4 fusion.30
  549.3 8.0 convert_element_type.119
  557.4 78.9 %reduce-scatter.7.cloned.1.call-done = bf16[2,768,128]{2,1,0:T(8,128)(2,1)} async-done(((bf16[2,12288,128]{2,1,0:T(8,128)(2,1)}), bf16[2,768,128]{2,1,0:T(8,128)(2,1)}) %reduce-scatter.7.cloned.1.call-update) | async-done | bytes 393232 | tf_op jit(solution)/shard_map/reduce_scatter | solution.py:187
  638.5 8.1 convolution_convert_fusion.1
  646.6 7.7 convolution_convert_fusion
  655.2 54.6 %reduce-scatter.9.cloned.1.call-done = bf16[2,96,256]{2,1,0:T(8,128)(2,1)} async-done(((bf16[2,768,256]{2,1,0:T(8,128)(2,1)}), bf16[2,96,256]{2,1,0:T(8,128)(2,1)}) %reduce-scatter.9.cloned.1.call-update) | async-done | bytes 98320 | tf_op jit(solution)/shard_map/reduce_scatter | solution.py:193
  711.3 70.9 %reduce-scatter.11.cloned.1.call-done = bf16[512,256]{1,0:T(8,128)(2,1)} async-done(((bf16[512,4096]{1,0:T(8,128)(2,1)}), bf16[512,256]{1,0:T(8,128)(2,1)}) %reduce-scatter.11.cloned.1.call-update) | async-done | bytes 262160 | tf_op jit(solution)/shard_map/reduce_scatter | solution.py:140
  782.2 101.6 %reduce-scatter.5.cloned.1.call-done = bf16[96,4096]{1,0:T(8,128)(2,1)} async-done(((bf16[768,4096]{1,0:T(8,128)(2,1)}), bf16[96,4096]{1,0:T(8,128)(2,1)}) %reduce-scatter.5.cloned.1.call-update) | async-done | bytes 786448 | tf_op jit(solution)/shard_map/reduce_scatter | solution.py:125
  (366 shorter events, 305.8 us)
Async XLA Ops:
  7.2 48.0 %copy-start.3 = (s32[42]{0:T(128)S(1)}, s32[42]{0:T(128)}, u32[]{:S(2)}) copy-start(s32[42]{0:T(128)} %param.26) | copy-start | bytes 508
  7.2 48.0 %all-gather.3.cloned.1.call-start = ((), (), s32[]{:S(2)}) async-start(), calls=%async_computation.4 | async-start | bytes 6684672 | tf_op jit(solution)/shard_map/all_gather | solution.py:71
  9.1 334.0 %all-gather.5.cloned.1.call-start = ((), (), s32[]{:S(2)}) async-start(), calls=%async_computation.6 | async-start | bytes 7077888 | tf_op jit(solution)/shard_map/all_gather | solution.py:131
  9.9 626.5 %reduce-scatter.7.cloned.1.call-start = ((), (), s32[]{:S(2)}) async-start(), calls=%async_computation.7 | async-start | bytes 6684672 | tf_op jit(solution)/shard_map/reduce_scatter | solution.py:187
  343.1 8.4 copy-start.1
  369.7 1.4 copy-start.4
  392.4 1.4 copy-start.4
  472.5 1.4 copy-start.4
  509.5 1.4 copy-start.4
  539.4 1.4 copy-start.4
  557.4 81.1 %copy-start.2 = (bf16[768,4,128]{0,2,1:T(8,128)(2,1)S(1)}, bf16[768,4,128]{0,2,1:T(8,128)(2,1)}, u32[]{:S(2)}) copy-start(bf16[768,4,128]{0,2,1:T(8,128)(2,1)} %copy-done.1) | copy-start | bytes 2359300
  557.4 152.5 %reduce-scatter.9.cloned.1.call-start = ((), (), s32[]{:S(2)}) async-start(), calls=%async_computation.8 | async-start | bytes 884736 | tf_op jit(solution)/shard_map/reduce_scatter | solution.py:193
  637.5 0.9 copy-start
  638.4 143.8 %reduce-scatter.11.cloned.1.call-start = ((), (), s32[]{:S(2)}) async-start(), calls=%async_computation.9 | async-start | bytes 4456448 | tf_op jit(solution)/shard_map/reduce_scatter | solution.py:140
  646.6 237.3 %reduce-scatter.5.cloned.1.call-start = ((), (), s32[]{:S(2)}) async-start(), calls=%async_computation.5 | async-start | bytes 7077888 | tf_op jit(solution)/shard_map/reduce_scatter | solution.py:125
Sparse Core Ops, SparseCore 0:
  10.2 44.8 all-gather.2
  57.5 89.6 all-gather.4
  557.5 78.7 reduce-scatter.6
  639.7 70.0 reduce-scatter.8
  712.8 69.3 reduce-scatter.10
  786.9 96.8 reduce-scatter.4
where the time goes:
time: 896 us; the launch traced here: 891 us
  matrix products  395 us (44%)
  waiting for transfers between devices  344 us (38%)
  other arithmetic  89.6 us (10%)
  loops' own time  34.1 us (4%)
  between operations  14.2 us (2%)
  local copies, waits for them, and re-layouts  13.7 us (2%)
    dot_general x48, matrix products, visible(): same = jnp.dot(query_hot, key_hot.T, precision=HIGH)  169 us
    reduce_scatter x1, waiting for transfers between devices, shards(): lax.psum_scatter(jnp.dot(attn, out_weight, preferred_element_type=jnp.flo...  102 us
    dot_general x48, matrix products, visible(): jnp.dot(jnp.dot(query_hot, lineage, precision=HIGH), key_hot.T, precision...  90.1 us
    reduce_scatter x1, waiting for transfers between devices, shards(): lax.psum_scatter(pair_acc.astype(jnp.bfloat16), 'leaf', scatter_dimension...  78.9 us
    reduce_scatter x1, waiting for transfers between devices, shards(): lax.psum_scatter(weight_sum.astype(jnp.bfloat16), 'leaf', scatter_dimensi...  70.9 us
    reduce_scatter x1, waiting for transfers between devices, shards(): lax.psum_scatter(term.astype(jnp.bfloat16), 'head', scatter_dimension=1,...  54.6 us
    reduce_sum x49, other arithmetic, slot_table(): jnp.sum(jnp.where(inside, seg_offset[None, :], 0), axis=1)  37.6 us
    all_gather x1, waiting for transfers between devices, shards(): lax.all_gather(jnp.stack([key_mine, value_mine]), 'leaf', axis=1, tiled=T...  37.2 us
  transfers between devices with their start and end apart: 6, of which 5 were waited for; matrix products, arithmetic and copies ran while one was open for 33% of the time, Pallas kernels for 0%

commit v1 on v0

v1 whole, which is shorter than its diff:
```python
import functools

import jax
import jax.numpy as jnp
from jax import lax
from jax.experimental import pallas as pl
from jax.experimental.pallas import tpu as pltpu
from jax.sharding import PartitionSpec as P

HD = 128
GROUP = 16
HEADS_DEV = 4
ROWS = 768
WIN = 128
ELDER = 512
TREE = 21
NEG = -1e30
SCALE = HD ** (-0.5)
VMEM = 60 * 1024 * 1024
F32 = jnp.float32
BF16 = jnp.bfloat16

SMEM_SPEC = pl.BlockSpec(memory_space=pltpu.SMEM)
VMEM_SPEC = pl.BlockSpec(memory_space=pltpu.VMEM)


def head_perm(array, dx, dy):
    pairs = [(h, ((h // 4 + dx) % 2) * 4 + (h + dy) % 4) for h in range(8)]
    return lax.ppermute(array, "head", pairs)


def leaf_perm(array, dz, dx, dc):
    pairs = [
        (l, ((l // 4 + dz) % 4) * 4 + ((l // 2 + dx) % 2) * 2 + (l + dc) % 2) for l in range(16)
    ]
    return lax.ppermute(array, "leaf", pairs)


def add(*parts):
    total = parts[0].astype(F32)
    for part in parts[1:]:
        total = total + part.astype(F32)
    return total.astype(BF16)


def pick(rows, side):
    return jnp.where(side == 0, rows[:, :HD], rows[:, HD:])


def elder_start(offset):
    return jnp.minimum(offset, ROWS - ELDER)


def pack_kernel(place, owner, offset, key_ref, value_ref, own_ref, elder_ref):
    leaf, side = place[0], place[1] // 4
    own_ref[:, :HD] = pick(key_ref[...], side)
    own_ref[:, HD:] = pick(value_ref[...], side)

    def find(i, start):
        mine = (owner[i] == leaf) & (i % TREE < 5)
        return jnp.where(mine, elder_start(offset[i]), start)

    start = lax.fori_loop(0, owner.shape[0], find, jnp.int32(0))
    elder_ref[...] = own_ref[pl.ds(pl.multiple_of(start, WIN), ELDER), :]


def pack(place, owner, offset, key_rows, value_rows):
    return pl.pallas_call(
        pack_kernel,
        out_shape=(
            jax.ShapeDtypeStruct((ROWS, 2 * HD), BF16),
            jax.ShapeDtypeStruct((ELDER, 2 * HD), BF16),
        ),
        in_specs=[SMEM_SPEC] * 3 + [VMEM_SPEC] * 2,
        out_specs=(VMEM_SPEC, VMEM_SPEC),
        compiler_params=pltpu.CompilerParams(vmem_limit_bytes=VMEM),
        cost_estimate=pl.CostEstimate(flops=0, bytes_accessed=2_000_000, transcendentals=0),
        name="pack_keys",
    )(place, owner, offset, key_rows, value_rows)


def relative_leaf(leaf, other):
    core = (leaf + other) % 2
    cross = (leaf // 2 + other // 2) % 2
    depth = (other // 4 - leaf // 4 + 4) % 4
    return core * 8 + depth * 2 + cross


def fill_table(table, place, owner, parent, offset, length):
    leaf = place[0]
    for w in range(ROWS // WIN):
        table[w, 0] = -1

    def first_rows(segment):
        shift = offset[segment] - elder_start(offset[segment])
        base = owner[segment] * ELDER + shift
        target = relative_leaf(leaf, owner[segment]) * ELDER + shift
        return base, target

    def visit(i, unused):
        @pl.when(owner[i] == leaf)
        def _():
            level = i % TREE
            prompt = i - level
            branch = jnp.where(level >= 5, parent[i], i)
            prompt_base, prompt_target = first_rows(prompt)
            branch_base, branch_target = first_rows(branch)
            tiles = jnp.where(level == 0, 4, jnp.where(level < 5, 2, 1))
            first = jnp.where(level == 0, 0, jnp.where(level < 5, 4, 6))
            window = offset[i] // WIN
            for j in range(4):

                @pl.when(j < tiles)
                def _():
                    table[window + j, 0] = first + j
                    table[window + j, 1] = length[i] - j * WIN
                    table[window + j, 2] = prompt_base
                    table[window + j, 3] = branch_base
                    table[window + j, 4] = prompt_target
                    table[window + j, 5] = branch_target

        return unused

    lax.fori_loop(0, owner.shape[0], visit, 0)


def heads_down(block):
    return jnp.concatenate([block[:, h * HD : (h + 1) * HD] for h in range(HEADS_DEV)], axis=0)


def tile_base(table, w, column, t):
    base = table[w, column] + t * WIN if t < 4 else table[w, column + 1] + (t - 4) * WIN
    return pl.multiple_of(base, WIN)


def for_windows(table, empty, full):
    def window(w, unused):
        count = table[w, 0]
        rows = pl.ds(pl.multiple_of(w * WIN, WIN), WIN)
        for low, high in ((-1, -1), (0, 3), (4, 5), (6, 6)):

            @pl.when((count >= low) & (count <= high))
            def _(high=high):
                if high < 0:
                    empty(w, rows)
                else:
                    full(w, rows, high, count)

        return unused

    lax.fori_loop(0, ROWS // WIN, window, 0)


def load_tiles(table, w, rows, tiles, gathered_ref, own_ref, pair_buf):
    for t in range(tiles):
        pair_buf[t * WIN : (t + 1) * WIN, :] = gathered_ref[
            pl.ds(tile_base(table, w, 2, t), WIN), :
        ]
    pair_buf[tiles * WIN : (tiles + 1) * WIN, :] = own_ref[rows, :]


def masked(scores, tiles, count):
    shape = scores.shape
    col = lax.broadcasted_iota(jnp.int32, shape, 1)
    row = lax.broadcasted_iota(jnp.int32, shape, 0) % WIN
    seen = (col < count * WIN) | ((col >= tiles * WIN) & (col - tiles * WIN <= row))
    return jnp.where(seen, scores, NEG)


def live_rows(table, w):
    row = lax.broadcasted_iota(jnp.int32, (HEADS_DEV * WIN, 1), 0) % WIN
    return (row < table[w, 1]).astype(F32)


def scores_of(query, keys):
    return lax.dot_general(query, keys, (((1,), (1,)), ((), ())), preferred_element_type=F32)


def forward_kernel(
    place, owner, parent, offset, length, query_ref, own_ref, gathered_ref, attn_ref, stat_ref,
    table, pair_buf,
):
    fill_table(table, place, owner, parent, offset, length)

    def empty(w, rows):
        attn_ref[rows, :] = jnp.zeros((WIN, HEADS_DEV * HD), BF16)
        stat_ref[rows, :] = jnp.zeros((WIN, HD), F32)

    def full(w, rows, tiles, count):
        load_tiles(table, w, rows, tiles, gathered_ref, own_ref, pair_buf)
        span = (tiles + 1) * WIN
        query = heads_down(query_ref[rows, :])
        scores = masked(scores_of(query, pair_buf[:span, :HD]) * SCALE, tiles, count)
        top = jnp.max(scores, axis=1, keepdims=True)
        weights = jnp.exp(scores - top)
        total = jnp.sum(weights, axis=1, keepdims=True)
        probs = (weights * (live_rows(table, w) / total)).astype(BF16)
        attn = jnp.dot(probs, pair_buf[:span, HD:], preferred_element_type=F32).astype(BF16)
        stat = top + jnp.log(total)
        lane = lax.broadcasted_iota(jnp.int32, (WIN, HD), 1)
        packed = jnp.zeros((WIN, HD), F32)
        for h in range(HEADS_DEV):
            part = slice(h * WIN, (h + 1) * WIN)
            attn_ref[rows, h * HD : (h + 1) * HD] = attn[part]
            packed = jnp.where(lane == h, stat[part], packed)
        stat_ref[rows, :] = packed

    for_windows(table, empty, full)


def forward(place, segs, query_rows, own, gathered):
    return pl.pallas_call(
        forward_kernel,
        out_shape=(
            jax.ShapeDtypeStruct((ROWS, HEADS_DEV * HD), BF16),
            jax.ShapeDtypeStruct((ROWS, HD), F32),
        ),
        in_specs=[SMEM_SPEC] * 5 + [VMEM_SPEC] * 3,
        out_specs=(VMEM_SPEC, VMEM_SPEC),
        scratch_shapes=[pltpu.SMEM((6, 8), jnp.int32), pltpu.VMEM((7 * WIN, 2 * HD), BF16)],
        compiler_params=pltpu.CompilerParams(vmem_limit_bytes=VMEM),
        cost_estimate=pl.CostEstimate(
            flops=2_000_000_000, bytes_accessed=8_000_000, transcendentals=2_000_000
        ),
        name="attention",
    )(place, *segs, query_rows, own, gathered)


def relative_head(head, k):
    return ((head // 4 + k // 4) % 2) * 4 + (head + k) % 4


def project_kernel(place, attn_ref, weight_ref, *rest):
    outs, ordered = rest[:8], rest[8]

    @pl.when(pl.program_id(0) == 0)
    def _():
        for k in range(8):
            first = pl.multiple_of(relative_head(place[1], k) * 96, 32)
            ordered[k * 96 : (k + 1) * 96, :] = attn_ref[pl.ds(first, 96), :]

    product = jnp.dot(ordered[...], weight_ref[...], preferred_element_type=F32).astype(BF16)
    for k in range(8):
        outs[k][...] = product[k * 96 : (k + 1) * 96, :]


def project(place, attn, out_weight):
    width = out_weight.shape[1]
    step = 512
    return pl.pallas_call(
        project_kernel,
        grid=(width // step,),
        out_shape=[jax.ShapeDtypeStruct((96, width), BF16)] * 8,
        in_specs=[
            SMEM_SPEC,
            pl.BlockSpec((ROWS, HEADS_DEV * HD), lambda n: (0, 0)),
            pl.BlockSpec((HEADS_DEV * HD, step), lambda n: (0, n)),
        ],
        out_specs=[pl.BlockSpec((96, step), lambda n: (0, n))] * 8,
        scratch_shapes=[pltpu.VMEM((ROWS, HEADS_DEV * HD), BF16)],
        compiler_params=pltpu.CompilerParams(vmem_limit_bytes=VMEM),
        cost_estimate=pl.CostEstimate(
            flops=3_200_000_000, bytes_accessed=11_000_000, transcendentals=0
        ),
        name="project",
    )(place, attn, out_weight)


def absolute_leaf(leaf, n):
    core = (leaf + 1 - n // 8) % 2
    depth = (leaf // 4 + (n % 8) // 2) % 4
    cross = (leaf // 2 + n % 2) % 2
    return depth * 4 + cross * 2 + core


def dense_back_kernel(place, attn_ref, weight_ref, *rest):
    pieces, outs, scratch = rest[:8], rest[8:11], rest[11:]
    grad_ref, other_ref, mine_ref = outs
    turned, rows, total = scratch
    n = pl.program_id(0)

    @pl.when(n == 0)
    def _():
        turned[...] = attn_ref[...].T
        total[...] = jnp.zeros_like(total)

    for k in range(8):
        first = pl.multiple_of(relative_head(place[1], k) * 96, 32)
        rows[pl.ds(first, 96), :] = pieces[k][...]
    block = rows[...]
    part = jnp.dot(turned[...], block, preferred_element_type=F32).astype(BF16)

    @pl.when(n < 8)
    def _():
        other_ref[0] = part

    @pl.when(n >= 8)
    def _():
        mine_ref[0] = part

    total[...] += scores_of(block, weight_ref[...])

    @pl.when(n == 15)
    def _():
        grad_ref[...] = total[...].astype(BF16)


def dense_back(place, attn, out_weight, pieces):
    feats = HEADS_DEV * HD
    step = 256
    column = lambda n, place: (0, absolute_leaf(place[0], n))
    return pl.pallas_call(
        dense_back_kernel,
        grid_spec=pltpu.PrefetchScalarGridSpec(
            num_scalar_prefetch=1,
            grid=(16,),
            in_specs=[
                pl.BlockSpec((ROWS, feats), lambda n, place: (0, 0)),
                pl.BlockSpec((feats, step), column),
            ]
            + [pl.BlockSpec((96, step), column)] * 8,
            out_specs=[
                pl.BlockSpec((ROWS, feats), lambda n, place: (0, 0)),
                pl.BlockSpec((1, feats, step), lambda n, place: (jnp.minimum(n, 7), 0, 0)),
                pl.BlockSpec((1, feats, step), lambda n, place: (jnp.maximum(n - 8, 0), 0, 0)),
            ],
            scratch_shapes=[
                pltpu.VMEM((feats, ROWS), BF16),
                pltpu.VMEM((ROWS, step), BF16),
                pltpu.VMEM((ROWS, feats), F32),
            ],
        ),
        out_shape=[
            jax.ShapeDtypeStruct((ROWS, feats), BF16),
            jax.ShapeDtypeStruct((8, feats, step), BF16),
            jax.ShapeDtypeStruct((8, feats, step), BF16),
        ],
        compiler_params=pltpu.CompilerParams(vmem_limit_bytes=VMEM),
        cost_estimate=pl.CostEstimate(
            flops=6_400_000_000, bytes_accessed=16_000_000, transcendentals=0
        ),
        name="dense_back",
    )(place, attn, out_weight, *pieces)


def backward_kernel(
    place, owner, parent, offset, length, query_ref, grad_ref, attn_ref, stat_ref, own_ref,
    gathered_ref, query_grad_ref, own_grad_ref, mine_ref, other_ref, table, pair_buf, elder_sum,
):
    fill_table(table, place, owner, parent, offset, length)
    elder_sum[...] = jnp.zeros_like(elder_sum)

    def empty(w, rows):
        query_grad_ref[rows, :] = jnp.zeros((WIN, HEADS_DEV * HD), BF16)
        own_grad_ref[rows, :] = jnp.zeros((WIN, 2 * HD), F32)

    def full(w, rows, tiles, count):
        load_tiles(table, w, rows, tiles, gathered_ref, own_ref, pair_buf)
        span = (tiles + 1) * WIN
        query = heads_down(query_ref[rows, :])
        grad = heads_down(grad_ref[rows, :])
        attn = heads_down(attn_ref[rows, :])
        packed = stat_ref[rows, :]
        stat = jnp.concatenate([packed[:, h : h + 1] for h in range(HEADS_DEV)], axis=0)
        delta = jnp.sum(grad.astype(F32) * attn.astype(F32), axis=1, keepdims=True)
        keys, values = pair_buf[:span, :HD], pair_buf[:span, HD:]
        scores = masked(scores_of(query, keys) * SCALE, tiles, count)
        probs = jnp.exp(scores - stat) * live_rows(table, w)
        dprobs = scores_of(grad, values)
        dscores = (probs * ((dprobs - delta) * SCALE)).astype(BF16)
        probs = probs.astype(BF16)
        query_grad = jnp.dot(dscores, keys, preferred_element_type=F32).astype(BF16)
        for h in range(HEADS_DEV):
            query_grad_ref[rows, h * HD : (h + 1) * HD] = query_grad[h * WIN : (h + 1) * WIN]
        turn = (((0,), (0,)), ((), ()))
        key_grad = lax.dot_general(dscores, query, turn, preferred_element_type=F32)
        value_grad = lax.dot_general(probs, grad, turn, preferred_element_type=F32)
        for t in range(tiles):
            spot = pl.ds(tile_base(table, w, 4, t), WIN)
            part = slice(t * WIN, (t + 1) * WIN)
            elder_sum[spot, :HD] += key_grad[part]
            elder_sum[spot, HD:] += value_grad[part]
        own_grad_ref[rows, :HD] = key_grad[tiles * WIN :]
        own_grad_ref[rows, HD:] = value_grad[tiles * WIN :]

    for_windows(table, empty, full)
    mine_ref[...] = elder_sum[: 8 * ELDER, :].astype(BF16)
    other_ref[...] = elder_sum[8 * ELDER :, :].astype(BF16)


def backward(place, segs, query_rows, grad, attn, stat, own, gathered):
    return pl.pallas_call(
        backward_kernel,
        out_shape=(
            jax.ShapeDtypeStruct((ROWS, HEADS_DEV * HD), BF16),
            jax.ShapeDtypeStruct((ROWS, 2 * HD), F32),
            jax.ShapeDtypeStruct((8 * ELDER, 2 * HD), BF16),
            jax.ShapeDtypeStruct((8 * ELDER, 2 * HD), BF16),
        ),
        in_specs=[SMEM_SPEC] * 5 + [VMEM_SPEC] * 6,
        out_specs=(VMEM_SPEC,) * 4,
        scratch_shapes=[
            pltpu.SMEM((6, 8), jnp.int32),
            pltpu.VMEM((7 * WIN, 2 * HD), BF16),
            pltpu.VMEM((16 * ELDER, 2 * HD), F32),
        ],
        compiler_params=pltpu.CompilerParams(vmem_limit_bytes=VMEM),
        cost_estimate=pl.CostEstimate(
            flops=5_000_000_000, bytes_accessed=14_000_000, transcendentals=2_000_000
        ),
        name="attention_back",
    )(place, *segs, query_rows, grad, attn, stat, own, gathered)


def settle_kernel(place, owner, offset, own_ref, *rest):
    parts, outs, total = rest[:2], rest[2:6], rest[6]
    leaf, head = place[0], place[1]
    total[...] = own_ref[...]

    def find(i, start):
        mine = (owner[i] == leaf) & (i % TREE < 5)
        return jnp.where(mine, elder_start(offset[i]), start)

    start = lax.fori_loop(0, owner.shape[0], find, jnp.int32(0))
    spot = pl.ds(pl.multiple_of(start, WIN), ELDER)
    total[spot, :] += sum(part[...].astype(F32) for part in parts)
    for k in range(4):
        for side in range(2):
            first = pl.multiple_of(relative_head(head, side * 4 + k) * 96, 32)
            outs[k][side] = total[pl.ds(first, 96), :].astype(BF16)


def settle(place, owner, offset, own, parts):
    return pl.pallas_call(
        settle_kernel,
        out_shape=[jax.ShapeDtypeStruct((2, 96, 2 * HD), BF16)] * 4,
        in_specs=[SMEM_SPEC] * 3 + [VMEM_SPEC] * 3,
        out_specs=[VMEM_SPEC] * 4,
        scratch_shapes=[pltpu.VMEM((ROWS, 2 * HD), F32)],
        compiler_params=pltpu.CompilerParams(vmem_limit_bytes=VMEM),
        cost_estimate=pl.CostEstimate(flops=0, bytes_accessed=2_000_000, transcendentals=0),
        name="settle",
    )(place, owner, offset, own, *parts)


def gather_grad(rows):
    before = head_perm(rows, 0, 1)
    after = head_perm(rows, 0, -1)
    cross = head_perm(rows, 1, 0)
    half = rows.shape[0] // 2
    far = jnp.concatenate(
        [head_perm(before[:half], 0, 1), head_perm(after[half:], 0, -1)], axis=0
    )
    cross_before = head_perm(cross, 0, 1)
    cross_after = head_perm(cross, 0, -1)
    cross_far = head_perm(far, 1, 0)
    return [rows, after, far, before, cross, cross_after, cross_far, cross_before]


def scatter_rows(parts):
    near, up, far, down, cross, cross_up, cross_far, cross_down = parts
    half = near.shape[0] // 2
    from_down = head_perm(cross_up, 0, 1)
    from_up = head_perm(cross_down, 0, -1)
    from_cross = head_perm(cross_far, 1, 0)
    far = add(far, from_cross)
    cross = add(cross, from_down, from_up)
    first = head_perm(far[:half], 0, 1)
    second = head_perm(far[half:], 0, -1)
    last = head_perm(cross, 1, 0)
    up = jnp.concatenate([add(up[:half], first), up[half:]], axis=0)
    down = jnp.concatenate([down[:half], add(down[half:], second)], axis=0)
    return add(near, last, head_perm(up, 0, 1), head_perm(down, 0, -1))


def scatter_leaf(other, mine):
    rows = mine.shape[0] // 8
    joined = add(mine, leaf_perm(other, 0, 0, 1))
    received = [
        leaf_perm(joined[2 * rows * d : 2 * rows * (d + 1)], d, 0, 0) for d in range(1, 4)
    ]
    summed = add(joined[: 2 * rows], *received)
    return summed[:rows], leaf_perm(summed[rows:], 0, 1, 0)


def shards(
    query_rows, key_rows, value_rows, out_weight, out_grad, seg_owner, seg_parent, seg_offset,
    seg_length,
):
    place = jnp.stack([lax.axis_index("leaf"), lax.axis_index("head")]).astype(jnp.int32)
    side = lax.axis_index("head") // 4
    segs = (seg_owner, seg_parent, seg_offset, seg_length)
    own, elder = pack(place, seg_owner, seg_offset, key_rows, value_rows)
    gathered = lax.all_gather(elder, "leaf", axis=0, tiled=True)
    pieces = gather_grad(out_grad)
    attn, stat = forward(place, segs, query_rows, own, gathered)
    parts = project(place, attn, out_weight)
    layer_out = scatter_rows(parts)
    attn_grad, other_weight, mine_weight = dense_back(place, attn, out_weight, pieces)
    feats = attn.shape[1]
    weight_mine, weight_recv = scatter_leaf(
        other_weight.reshape(8 * feats, -1), mine_weight.reshape(8 * feats, -1)
    )
    weight_grad = add(weight_mine, weight_recv)
    query_grads, own_grad, mine_pair, other_pair = backward(
        place, segs, query_rows, attn_grad, attn, stat, own, gathered
    )
    pair_mine, pair_recv = scatter_leaf(other_pair, mine_pair)
    blocks = settle(
        place, seg_owner, seg_offset, own_grad, [pair_mine, pair_recv]
    )
    total = blocks[0].astype(F32)
    for k in range(1, 4):
        total = total + head_perm(blocks[k], 0, k).astype(F32)
    total = total.astype(BF16)
    near = total[0]
    far = head_perm(total[1], 1, 0)
    first = jnp.where(side == 0, near, far)
    second = jnp.where(side == 0, far, near)
    key_grads = jnp.concatenate([first[:, :HD], second[:, :HD]], axis=1)
    value_grads = jnp.concatenate([first[:, HD:], second[:, HD:]], axis=1)
    return layer_out, query_grads, key_grads, value_grads, weight_grad


def solution(mesh):
    return jax.shard_map(
        shards,
        mesh=mesh,
        in_specs=(
            P("leaf", "head"),
            P("leaf", None),
            P("leaf", None),
            P("head", None),
            P(("leaf", "head"), None),
            P(),
            P(),
            P(),
            P(),
        ),
        out_specs=(
            P(("leaf", "head"), None),
            P("leaf", "head"),
            P(("leaf", "head"), None),
            P(("leaf", "head"), None),
            P("head", "leaf"),
        ),
        check_vma=False,
    )
```

time: 896 us -> 231 us (0.26)
  matrix products: 395 us -> 0 us
  waiting for transfers between devices: 344 us -> 95.1 us
  other arithmetic: 89.6 us -> 9.09 us
  Pallas kernels: 0 us -> 66.9 us
  starting transfers between devices: 0.24 us -> 42.4 us
  loops' own time: 34.1 us -> 0 us
  local copies, waits for them, and re-layouts: 13.7 us -> 3.05 us
    dot_general x136 -> x0, matrix products: 395 us -> none  [the longest x48 169 us: visible(): same = jnp.dot(query_hot, key_hot.T, precision=HIGH)]
    reduce_scatter x4 -> x0, waiting for transfers between devices: 306 us -> none  [the longest x1 102 us: shards(): lax.psum_scatter(jnp.dot(attn, out_weight, preferred_element_type=jnp.flo...]
    ppermute x0 -> x30, waiting for transfers between devices: none -> 87.1 us  [the longest x20 63.4 us: head_perm(): return lax.ppermute(array, 'head', pairs)]
    pallas_call x0 -> x6, Pallas kernels: none -> 66.9 us  [the longest x1 28 us: dense_back(): pl.pallas_call(dense_back_kernel, grid_spec=pltpu.PrefetchScalarGridSpec(...]
    reduce_sum x55 -> x0, other arithmetic: 50.3 us -> none  [the longest x49 37.6 us: slot_table(): jnp.sum(jnp.where(inside, seg_offset[None, :], 0), axis=1)]
    ppermute x0 -> x30, starting transfers between devices: none -> 42.4 us  [the longest x20 31.3 us: head_perm(): return lax.ppermute(array, 'head', pairs)]
    another operation x51 -> x0, loops' own time: 34.1 us -> none  [the longest x3 32.8 us: sweep(): return lax.fori_loop(0, leaf_count, shard_loop, carry)]
    all_gather x2 -> x1, waiting for transfers between devices: 37.2 us -> 7.96 us  [shards(): gathered = lax.all_gather(elder, 'leaf', axis=0, tiled=True)]
  transfers between devices with their start and end apart: 6 -> 31, of which waited for: 5 -> 13; matrix products, arithmetic and copies ran while one was open for 33% -> 4% of each run, Pallas kernels for 0% -> 28%
where the time goes in v1:
time: 231 us
  waiting for transfers between devices  95.1 us (41%)
  Pallas kernels  66.9 us (29%)
  starting transfers between devices  42.4 us (18%)
  between operations  14.3 us (6%)
  other arithmetic  9.09 us (4%)
  local copies, waits for them, and re-layouts  3.05 us (1%)
    ppermute x20, waiting for transfers between devices, head_perm(): return lax.ppermute(array, 'head', pairs)  63.4 us
    ppermute x20, starting transfers between devices, head_perm(): return lax.ppermute(array, 'head', pairs)  31.3 us
    pallas_call x1, Pallas kernels, dense_back(): pl.pallas_call(dense_back_kernel, grid_spec=pltpu.PrefetchScalarGridSpec(...  28 us
    ppermute x10, waiting for transfers between devices, leaf_perm(): return lax.ppermute(array, 'leaf', pairs)  23.7 us
    pallas_call x1, Pallas kernels, backward(): pl.pallas_call(backward_kernel, out_shape=(jax.ShapeDtypeStruct((ROWS, HE...  14.6 us
    ppermute x10, starting transfers between devices, leaf_perm(): return lax.ppermute(array, 'leaf', pairs)  11.1 us
    pallas_call x1, Pallas kernels, forward(): pl.pallas_call(forward_kernel, out_shape=(jax.ShapeDtypeStruct((ROWS, HEA...  10.1 us
    pallas_call x1, Pallas kernels, project(): pl.pallas_call(project_kernel, grid=(width // step,), out_shape=[jax.Shap...  8.85 us
  transfers between devices with their start and end apart: 31, of which 13 were waited for; matrix products, arithmetic and copies ran while one was open for 4% of the time, Pallas kernels for 28%

profile of v1, /device:TPU:0, one launch (start us, length us, event | category | flops | bytes accessed | tf_op | source)
XLA Modules:
  0.0 230.9 jit_solution(9883058120824127887)
XLA Ops:
  7.2 0.6 pad_add_fusion.place
  7.8 2.6 %pack_keys.1 = (bf16[768,256]{1,0:T(8,128)(2,1)}, bf16[512,256]{1,0:T(8,128)(2,1)}) custom-call(s32[2]{0:T(128)} %pad_add_fusion.place, s32[42]{0:T(128)} %owner.7, s32[42]{0:T(128)} %offset.7, bf16[768,256]{1,0:T(8,128)(2,1)} %key_ref.1, bf16[768,256]{1,0:T(8,128)(2,1)} %value_ref.1), custom_call_target="tpu_custom_call" | custom-call | bytes 2000000 | tf_op jit(solution)/shard_map/pack_keys/pallas_call | solution.py:68
  10.4 1.7 collective-permute-start.9
  12.1 1.6 collective-permute-start.8
  13.7 3.1 %collective-permute-start.12 = (bf16[96,4096]{1,0:T(8,128)(2,1)}, bf16[96,4096]{1,0:T(8,128)(2,1)S(1)}, u32[]{:S(2)}, u32[]{:S(2)}) collective-permute-start(bf16[96,4096]{1,0:T(8,128)(2,1)} %rest_0_.1), channel_id=1, source_target_pairs={{0,4},{1,5},{2,6},{3,7},{4,0},{5,1},{6,2},{7,3},{8,12},{9,13},{10,... | collective-permute-start | bytes 2359304 | tf_op jit(solution)/shard_map/ppermute | solution.py:29
  16.8 14.5 %collective-permute-done.9.rest_3_ = bf16[96,4096]{1,0:T(8,128)(2,1)S(1)} collective-permute-done((bf16[96,4096]{1,0:T(8,128)(2,1)}, bf16[96,4096]{1,0:T(8,128)(2,1)S(1)}, u32[]{:S(2)}, u32[]{:S(2)}) %collective-permute-start.9) | collective-permute-done | bytes 786464 | tf_op jit(solution)/shard_map/ppermute | solution.py:29
  31.3 0.4 collective-permute-start.10
  31.7 3.0 %collective-permute-start.11 = (bf16[48,4096]{1,0:T(8,128)(2,1)S(1)}, bf16[48,4096]{1,0:T(8,128)(2,1)S(1)}, u32[]{:S(2)}, u32[]{:S(2)}) collective-permute-start(bf16[48,4096]{1,0:T(8,128)(2,1)S(1)} %slice.107), channel_id=1, source_target_pairs={{0,3},{1,0},{2,1},{3,2},{4,7},{5,4},{6,5},{7,6},{8,11},{9,8},{10,9... | collective-permute-start | bytes 1179656 | tf_op jit(solution)/shard_map/ppermute | solution.py:29
  34.7 11.8 %collective-permute-done.12.rest_4_ = bf16[96,4096]{1,0:T(8,128)(2,1)S(1)} collective-permute-done((bf16[96,4096]{1,0:T(8,128)(2,1)}, bf16[96,4096]{1,0:T(8,128)(2,1)S(1)}, u32[]{:S(2)}, u32[]{:S(2)}) %collective-permute-start.12) | collective-permute-done | bytes 786464 | tf_op jit(solution)/shard_map/ppermute | solution.py:29
  46.5 0.5 collective-permute-start.13
  47.0 1.5 collective-permute-start.15
  48.6 4.0 %collective-permute-start.14 = (bf16[96,4096]{1,0:T(8,128)(2,1)S(1)}, bf16[96,4096]{1,0:T(8,128)(2,1)}, u32[]{:S(2)}, u32[]{:S(2)}) collective-permute-start(bf16[96,4096]{1,0:T(8,128)(2,1)S(1)} %constant_dynamic-update-slice_fusion.rest_2_), channel_id=1, source_target_pairs={{0,4},{1,5},{2,6},{3,7},{4,0},{5,1},{6,2},{7,3},{8,12},{9,13},{10,... | collective-permute-start | bytes 2359304 | tf_op jit(solution)/shard_map/ppermute | solution.py:29
  52.6 8.0 %all-gather.2.cloned.1.call-done.gathered_ref = bf16[8192,256]{1,0:T(8,128)(2,1)} async-done(((bf16[512,256]{1,0:T(8,128)(2,1)}), bf16[8192,256]{1,0:T(8,128)(2,1)}) %all-gather.2.cloned.1.call-update) | async-done | bytes 4194320 | tf_op jit(solution)/shard_map/all_gather | solution.py:494
  60.5 10.1 %attention.1 = (bf16[768,512]{1,0:T(8,128)(2,1)}, f32[768,128]{1,0:T(8,128)}) custom-call(s32[2]{0:T(128)} %pad_add_fusion.place, s32[42]{0:T(128)} %owner.7, s32[42]{0:T(128)} %parent.3, s32[42]{0:T(128)} %offset.7, s32[42]{0:T(128)} %length.3, bf16[768,512]{1,0:T(8,128)(2,1)} %query_ref.3, bf16[768,256]{1,0:T(8,128)(2,1)} %get-tuple-element.28.own_ref, ...), custom_call_target="tpu_custom_call" | custom-call | flops 2000000000 | bytes 8000000 | tf_op jit(solution)/shard_map/attention/pallas_call | solution.py:212
  70.6 8.8 %project.1 = (bf16[96,4096]{1,0:T(8,128)(2,1)}, bf16[96,4096]{1,0:T(8,128)(2,1)}, bf16[96,4096]{1,0:T(8,128)(2,1)}, bf16[96,4096]{1,0:T(8,128)(2,1)}, bf16[96,40...) custom-call(s32[2]{0:T(128)} %pad_add_fusion.place, ...), custom_call_target="tpu_custom_call" | custom-call | flops 3200000000 | bytes 11000000 | tf_op jit(solution)/shard_map/project/pallas_call | solution.py:250
  79.5 2.6 %collective-permute-start.3 = (bf16[96,4096]{1,0:T(8,128)(2,1)}, bf16[96,4096]{1,0:T(8,128)(2,1)}, u32[]{:S(2)}, u32[]{:S(2)}) collective-permute-start(bf16[96,4096]{1,0:T(8,128)(2,1)} %get-tuple-element.37), channel_id=1, source_target_pairs={{0,4},{1,5},{2,6},{3,7},{4,0},{5,1},{6,2},{7,3},{8,12},{9,13},{10,... | collective-permute-start | bytes 2359304 | tf_op jit(solution)/shard_map/ppermute | solution.py:29
  82.1 28.0 %dense_back.1 = (bf16[768,512]{1,0:T(8,128)(2,1)}, bf16[8,512,256]{2,1,0:T(8,128)(2,1)}, bf16[8,512,256]{2,1,0:T(8,128)(2,1)}) custom-call(s32[2]{0:T(128)} %pad_add_fusion.place, bf16[768,512]{1,0:T(8,128)(2,1)} %get-tuple-element.30.attn_ref, bf16[512,4096]{1,0:T(8,128)(2,1)} %weight_ref.3, bf16[96,4096]{1,0:T(8,128)(2,1)} %rest_0_.1, ...), custom_call_target="tpu_custom_call" | custom-call | flops 6400000000 | bytes 16000000 | tf_op jit(solution)/shard_map/dense_back/pallas_call | solution.py:312
  110.1 1.5 collective-permute-start.25
  111.6 14.6 %attention_back.1 = (bf16[768,512]{1,0:T(8,128)(2,1)}, f32[768,256]{1,0:T(8,128)}, bf16[4096,256]{1,0:T(8,128)(2,1)}, bf16[4096,256]{1,0:T(8,128)(2,1)}) custom-call(s32[2]{0:T(128)} %pad_add_fusion.place, s32[42]{0:T(128)} %owner.7, s32[42]{0:T(128)} %parent.3, s32[42]{0:T(128)} %offset.7, s32[42]{0:T(128)} %length.3, bf16[768,512]{1,0:T(8,128)(2,1)} %query_ref.3, ...), custom_call_target="tpu_custom_call" | custom-call | flops 5000000000 | bytes 14000000 | tf_op jit(solution)/shard_map/attention_back/pallas_call | solution.py:392
  126.2 3.0 %collective-permute-start.16 = (bf16[4096,256]{1,0:T(8,128)(2,1)}, bf16[4096,256]{1,0:T(8,128)(2,1)S(1)}, u32[]{:S(2)}, u32[]{:S(2)}) collective-permute-start(bf16[4096,256]{1,0:T(8,128)(2,1)} %get-tuple-element.44), channel_id=1, source_target_pairs={{0,8},{8,0},{16,24},{24,16},{32,40},{40,32},{48,56},{56,48},{64,72... | collective-permute-start | bytes 6291464 | tf_op jit(solution)/shard_map/ppermute | solution.py:36
  129.2 0.3 collective-permute-start
  129.6 3.0 %collective-permute-start.1 = (bf16[96,4096]{1,0:T(8,128)(2,1)}, bf16[96,4096]{1,0:T(8,128)(2,1)S(1)}, u32[]{:S(2)}, u32[]{:S(2)}) collective-permute-start(bf16[96,4096]{1,0:T(8,128)(2,1)} %get-tuple-element.34), channel_id=1, source_target_pairs={{0,3},{1,0},{2,1},{3,2},{4,7},{5,4},{6,5},{7,6},{8,11},{9,8},{10,9... | collective-permute-start | bytes 2359304 | tf_op jit(solution)/shard_map/ppermute | solution.py:29
  132.6 1.3 add_convert_fusion.2
  134.0 0.1 collective-permute-start.4
  134.0 17.1 %collective-permute-done = bf16[96,4096]{1,0:T(8,128)(2,1)S(1)} collective-permute-done((bf16[96,4096]{1,0:T(8,128)(2,1)}, bf16[96,4096]{1,0:T(8,128)(2,1)S(1)}, u32[]{:S(2)}, u32[]{:S(2)}) %collective-permute-start) | collective-permute-done | bytes 786464 | tf_op jit(solution)/shard_map/ppermute | solution.py:29
  151.1 0.5 collective-permute-start.6
  151.6 0.3 add_convert_fusion.3
  151.9 1.1 collective-permute-start.2
  153.0 5.7 %collective-permute-done.4 = bf16[48,4096]{1,0:T(8,128)(2,1)S(1)} collective-permute-done((bf16[48,4096]{1,0:T(8,128)(2,1)S(1)}, bf16[48,4096]{1,0:T(8,128)(2,1)S(1)}, u32[]{:S(2)}, u32[]{:S(2)}) %collective-permute-start.4) | collective-permute-done | bytes 393248 | tf_op jit(solution)/shard_map/ppermute | solution.py:29
  158.6 0.1 add_convert_fusion.7
  158.8 0.1 collective-permute-start.5
  158.9 1.5 collective-permute-done.6
  160.4 0.1 add_convert_fusion.6
  160.6 0.5 add_convert_fusion
  161.1 0.1 fusion.2
  161.2 0.1 collective-permute-start.17
  161.3 0.8 collective-permute-start.18
  162.1 2.5 %collective-permute-start.19 = (bf16[1024,256]{1,0:T(8,128)(2,1)S(1)}, bf16[1024,256]{1,0:T(8,128)(2,1)S(1)}, u32[]{:S(2)}, u32[]{:S(2)}) collective-permute-start(bf16[1024,256]{1,0:T(8,128)(2,1)S(1)} %get-tuple-element.55), channel_id=1, source_target_pairs={{0,96},{8,104},{16,112},{24,120},{32,0},{40,8},{48,16},{56,24},{64... | collective-permute-start | bytes 1572872 | tf_op jit(solution)/shard_map/ppermute | solution.py:36
  164.6 2.1 fusion
  166.8 19.7 %collective-permute-done.17 = bf16[1024,256]{1,0:T(8,128)(2,1)S(1)} collective-permute-done((bf16[1024,256]{1,0:T(8,128)(2,1)S(1)}, bf16[1024,256]{1,0:T(8,128)(2,1)S(1)}, u32[]{:S(2)}, u32[]{:S(2)}) %collective-permute-start.17) | collective-permute-done | bytes 524320 | tf_op jit(solution)/shard_map/ppermute | solution.py:36
  186.5 1.7 collective-permute-start.7
  188.2 1.2 fusion.1
  189.4 1.0 collective-permute-start.27
  190.4 0.3 add_convert_fusion.5
  190.7 0.7 fusion.4
  191.4 2.2 collective-permute-start.28
  193.7 10.3 %collective-permute-done.7 = bf16[96,4096]{1,0:T(8,128)(2,1)S(1)} collective-permute-done((bf16[96,4096]{1,0:T(8,128)(2,1)S(1)}, bf16[96,4096]{1,0:T(8,128)(2,1)S(1)}, u32[]{:S(2)}, u32[]{:S(2)}) %collective-permute-start.7) | collective-permute-done | bytes 786464 | tf_op jit(solution)/shard_map/ppermute | solution.py:29
  203.9 1.3 add_convert_fusion.1
  205.3 0.7 copy-done.8
  206.0 2.8 %settle.1 = (bf16[2,96,256]{2,1,0:T(8,128)(2,1)}, bf16[2,96,256]{2,1,0:T(8,128)(2,1)}, bf16[2,96,256]{2,1,0:T(8,128)(2,1)}, bf16[2,96,256]{2,1,0:T(8,128)(2,1)}) custom-call(s32[2]{0:T(128)} %pad_add_fusion.place, s32[42]{0:T(128)} %owner.7, s32[42]{0:T(128)} %offset.7, f32[768,256]{1,0:T(8,128)} %get-tuple-element.42.own_ref, ...), custom_call_target="tpu_custom_call" | custom-call | bytes 2000000 | tf_op jit(solution)/shard_map/settle/pallas_call | solution.py:434
  208.8 0.4 collective-permute-start.21
  209.1 2.6 %collective-permute-start.22 = (bf16[2,96,256]{2,1,0:T(8,128)(2,1)}, bf16[2,96,256]{2,1,0:T(8,128)(2,1)S(1)}, u32[]{:S(2)}, u32[]{:S(2)}) collective-permute-start(bf16[2,96,256]{2,1,0:T(8,128)(2,1)} %get-tuple-element.47), channel_id=1, source_target_pairs={{0,2},{1,3},{2,0},{3,1},{4,6},{5,7},{6,4},{7,5},{8,10},{9,11},{10,... | collective-permute-start | bytes 294920 | tf_op jit(solution)/shard_map/ppermute | solution.py:29
  211.7 0.5 collective-permute-done.26
  212.2 2.2 collective-permute-start.23
  214.4 0.3 add_convert_fusion.4
  214.7 0.1 collective-permute-start.29
  214.8 1.1 collective-permute-done.21
  215.9 1.1 collective-permute-done.23
  217.1 1.0 collective-permute-start.24
  218.1 3.5 %collective-permute-done.29 = bf16[512,256]{1,0:T(8,128)(2,1)S(1)} collective-permute-done((bf16[512,256]{1,0:T(8,128)(2,1)S(1)}, bf16[512,256]{1,0:T(8,128)(2,1)S(1)}, u32[]{:S(2)}, u32[]{:S(2)}) %collective-permute-start.29) | collective-permute-done | bytes 262176 | tf_op jit(solution)/shard_map/ppermute | solution.py:36
  221.6 0.8 add_convert_fusion.8
  222.4 0.3 collective-permute-done.24
  222.8 0.6 pad_maximum_fusion.3
  223.4 0.6 pad_maximum_fusion.2
  (63 shorter events, 0.6 us)
Async XLA Ops:
  7.2 53.3 %all-gather.2.cloned.1.call-start = ((), (), s32[]{:S(2)}) async-start(), calls=%async_computation | async-start | bytes 4456448 | tf_op jit(solution)/shard_map/all_gather | solution.py:494
  10.4 20.9 %collective-permute-start.9 = (bf16[96,4096]{1,0:T(8,128)(2,1)}, bf16[96,4096]{1,0:T(8,128)(2,1)S(1)}, u32[]{:S(2)}, u32[]{:S(2)}) collective-permute-start(bf16[96,4096]{1,0:T(8,128)(2,1)} %rest_0_.1), channel_id=1, source_target_pairs={{0,1},{1,2},{2,3},{3,0},{4,5},{5,6},{6,7},{7,4},{8,9},{9,10},{10,1... | collective-permute-start | bytes 2359304 | tf_op jit(solution)/shard_map/ppermute | solution.py:29
  12.1 19.6 %collective-permute-start.8 = (bf16[96,4096]{1,0:T(8,128)(2,1)}, bf16[96,4096]{1,0:T(8,128)(2,1)S(1)}, u32[]{:S(2)}, u32[]{:S(2)}) collective-permute-start(bf16[96,4096]{1,0:T(8,128)(2,1)} %rest_0_.1), channel_id=1, source_target_pairs={{0,3},{1,0},{2,1},{3,2},{4,7},{5,4},{6,5},{7,6},{8,11},{9,8},{10,9... | collective-permute-start | bytes 2359304 | tf_op jit(solution)/shard_map/ppermute | solution.py:29
  13.7 32.8 %collective-permute-start.12 = (bf16[96,4096]{1,0:T(8,128)(2,1)}, bf16[96,4096]{1,0:T(8,128)(2,1)S(1)}, u32[]{:S(2)}, u32[]{:S(2)}) collective-permute-start(bf16[96,4096]{1,0:T(8,128)(2,1)} %rest_0_.1), channel_id=1, source_target_pairs={{0,4},{1,5},{2,6},{3,7},{4,0},{5,1},{6,2},{7,3},{8,12},{9,13},{10,... | collective-permute-start | bytes 2359304 | tf_op jit(solution)/shard_map/ppermute | solution.py:29
  31.3 39.3 %copy-start.9 = (bf16[96,4096]{1,0:T(8,128)(2,1)}, bf16[96,4096]{1,0:T(8,128)(2,1)S(1)}, u32[]{:S(2)}) copy-start(bf16[96,4096]{1,0:T(8,128)(2,1)S(1)} %collective-permute-done.9.rest_3_) | copy-start | bytes 2359300
  31.3 17.2 %collective-permute-start.10 = (bf16[48,4096]{1,0:T(8,128)(2,1)S(1)}, bf16[48,4096]{1,0:T(8,128)(2,1)S(1)}, u32[]{:S(2)}, u32[]{:S(2)}) collective-permute-start(bf16[48,4096]{1,0:T(8,128)(2,1)S(1)} %slice.106), channel_id=1, source_target_pairs={{0,1},{1,2},{2,3},{3,0},{4,5},{5,6},{6,7},{7,4},{8,9},{9,10},{10,1... | collective-permute-start | bytes 1179656 | tf_op jit(solution)/shard_map/ppermute | solution.py:29
  31.7 38.9 %copy-start.10 = (bf16[96,4096]{1,0:T(8,128)(2,1)}, bf16[96,4096]{1,0:T(8,128)(2,1)S(1)}, u32[]{:S(2)}) copy-start(bf16[96,4096]{1,0:T(8,128)(2,1)S(1)} %collective-permute-done.8.rest_1_) | copy-start | bytes 2359300
  31.7 16.8 %collective-permute-start.11 = (bf16[48,4096]{1,0:T(8,128)(2,1)S(1)}, bf16[48,4096]{1,0:T(8,128)(2,1)S(1)}, u32[]{:S(2)}, u32[]{:S(2)}) collective-permute-start(bf16[48,4096]{1,0:T(8,128)(2,1)S(1)} %slice.107), channel_id=1, source_target_pairs={{0,3},{1,0},{2,1},{3,2},{4,7},{5,4},{6,5},{7,6},{8,11},{9,8},{10,9... | collective-permute-start | bytes 1179656 | tf_op jit(solution)/shard_map/ppermute | solution.py:29
  46.5 24.1 %copy-start.13 = (bf16[96,4096]{1,0:T(8,128)(2,1)}, bf16[96,4096]{1,0:T(8,128)(2,1)S(1)}, u32[]{:S(2)}) copy-start(bf16[96,4096]{1,0:T(8,128)(2,1)S(1)} %collective-permute-done.12.rest_4_) | copy-start | bytes 2359300
  46.5 35.6 %collective-permute-start.13 = (bf16[96,4096]{1,0:T(8,128)(2,1)S(1)}, bf16[96,4096]{1,0:T(8,128)(2,1)}, u32[]{:S(2)}, u32[]{:S(2)}) collective-permute-start(bf16[96,4096]{1,0:T(8,128)(2,1)S(1)} %collective-permute-done.12.rest_4_), channel_id=1, source_target_pairs={{0,3},{1,0},{2,1},{3,2},{4,7},{5,4},{6,5},{7,6},{8,11},{9,8},{10,9... | collective-permute-start | bytes 2359304 | tf_op jit(solution)/shard_map/ppermute | solution.py:29
  47.0 35.1 %collective-permute-start.15 = (bf16[96,4096]{1,0:T(8,128)(2,1)S(1)}, bf16[96,4096]{1,0:T(8,128)(2,1)}, u32[]{:S(2)}, u32[]{:S(2)}) collective-permute-start(bf16[96,4096]{1,0:T(8,128)(2,1)S(1)} %collective-permute-done.12.rest_4_), channel_id=1, source_target_pairs={{0,1},{1,2},{2,3},{3,0},{4,5},{5,6},{6,7},{7,4},{8,9},{9,10},{10,1... | collective-permute-start | bytes 2359304 | tf_op jit(solution)/shard_map/ppermute | solution.py:29
  48.6 22.0 %copy-start.11 = (bf16[96,4096]{1,0:T(8,128)(2,1)}, bf16[96,4096]{1,0:T(8,128)(2,1)S(1)}, u32[]{:S(2)}) copy-start(bf16[96,4096]{1,0:T(8,128)(2,1)S(1)} %constant_dynamic-update-slice_fusion.rest_2_) | copy-start | bytes 2359300
  48.6 33.5 %collective-permute-start.14 = (bf16[96,4096]{1,0:T(8,128)(2,1)S(1)}, bf16[96,4096]{1,0:T(8,128)(2,1)}, u32[]{:S(2)}, u32[]{:S(2)}) collective-permute-start(bf16[96,4096]{1,0:T(8,128)(2,1)S(1)} %constant_dynamic-update-slice_fusion.rest_2_), channel_id=1, source_target_pairs={{0,4},{1,5},{2,6},{3,7},{4,0},{5,1},{6,2},{7,3},{8,12},{9,13},{10,... | collective-permute-start | bytes 2359304 | tf_op jit(solution)/shard_map/ppermute | solution.py:29
  79.5 53.1 %collective-permute-start.3 = (bf16[96,4096]{1,0:T(8,128)(2,1)}, bf16[96,4096]{1,0:T(8,128)(2,1)}, u32[]{:S(2)}, u32[]{:S(2)}) collective-permute-start(bf16[96,4096]{1,0:T(8,128)(2,1)} %get-tuple-element.37), channel_id=1, source_target_pairs={{0,4},{1,5},{2,6},{3,7},{4,0},{5,1},{6,2},{7,3},{8,12},{9,13},{10,... | collective-permute-start | bytes 2359304 | tf_op jit(solution)/shard_map/ppermute | solution.py:29
  110.1 52.0 %collective-permute-start.25 = (bf16[4096,256]{1,0:T(8,128)(2,1)}, bf16[4096,256]{1,0:T(8,128)(2,1)S(1)}, u32[]{:S(2)}, u32[]{:S(2)}) collective-permute-start(bf16[4096,256]{1,0:T(8,128)(2,1)} %bitcast.14), channel_id=1, source_target_pairs={{0,8},{8,0},{16,24},{24,16},{32,40},{40,32},{48,56},{56,48},{64,72... | collective-permute-start | bytes 6291464 | tf_op jit(solution)/shard_map/ppermute | solution.py:36
  111.6 17.6 %copy-start.4 = (bf16[96,4096]{1,0:T(8,128)(2,1)S(1)}, bf16[96,4096]{1,0:T(8,128)(2,1)}, u32[]{:S(2)}) copy-start(bf16[96,4096]{1,0:T(8,128)(2,1)} %get-tuple-element.35) | copy-start | bytes 2359300
  111.6 17.6 %copy-start.3 = (bf16[96,4096]{1,0:T(8,128)(2,1)S(1)}, bf16[96,4096]{1,0:T(8,128)(2,1)}, u32[]{:S(2)}) copy-start(bf16[96,4096]{1,0:T(8,128)(2,1)} %get-tuple-element.38) | copy-start | bytes 2359300
  126.2 6.4 %copy-start.6 = (bf16[96,4096]{1,0:T(8,128)(2,1)S(1)}, bf16[96,4096]{1,0:T(8,128)(2,1)}, u32[]{:S(2)}) copy-start(bf16[96,4096]{1,0:T(8,128)(2,1)} %get-tuple-element.36) | copy-start | bytes 2359300
  126.2 34.4 %collective-permute-start.16 = (bf16[4096,256]{1,0:T(8,128)(2,1)}, bf16[4096,256]{1,0:T(8,128)(2,1)S(1)}, u32[]{:S(2)}, u32[]{:S(2)}) collective-permute-start(bf16[4096,256]{1,0:T(8,128)(2,1)} %get-tuple-element.44), channel_id=1, source_target_pairs={{0,8},{8,0},{16,24},{24,16},{32,40},{40,32},{48,56},{56,48},{64,72... | collective-permute-start | bytes 6291464 | tf_op jit(solution)/shard_map/ppermute | solution.py:36
  129.2 22.4 %copy-start.5 = (bf16[96,4096]{1,0:T(8,128)(2,1)S(1)}, bf16[96,4096]{1,0:T(8,128)(2,1)}, u32[]{:S(2)}) copy-start(bf16[96,4096]{1,0:T(8,128)(2,1)} %get-tuple-element.32) | copy-start | bytes 2359300
  129.2 21.9 %collective-permute-start = (bf16[96,4096]{1,0:T(8,128)(2,1)}, bf16[96,4096]{1,0:T(8,128)(2,1)S(1)}, u32[]{:S(2)}, u32[]{:S(2)}) collective-permute-start(bf16[96,4096]{1,0:T(8,128)(2,1)} %get-tuple-element.33), channel_id=1, source_target_pairs={{0,1},{1,2},{2,3},{3,0},{4,5},{5,6},{6,7},{7,4},{8,9},{9,10},{10,1... | collective-permute-start | bytes 2359304 | tf_op jit(solution)/shard_map/ppermute | solution.py:29
  129.6 22.0 %collective-permute-start.1 = (bf16[96,4096]{1,0:T(8,128)(2,1)}, bf16[96,4096]{1,0:T(8,128)(2,1)S(1)}, u32[]{:S(2)}, u32[]{:S(2)}) collective-permute-start(bf16[96,4096]{1,0:T(8,128)(2,1)} %get-tuple-element.34), channel_id=1, source_target_pairs={{0,3},{1,0},{2,1},{3,2},{4,7},{5,4},{6,5},{7,6},{8,11},{9,8},{10,9... | collective-permute-start | bytes 2359304 | tf_op jit(solution)/shard_map/ppermute | solution.py:29
  134.0 24.7 %collective-permute-start.4 = (bf16[48,4096]{1,0:T(8,128)(2,1)S(1)}, bf16[48,4096]{1,0:T(8,128)(2,1)S(1)}, u32[]{:S(2)}, u32[]{:S(2)}) collective-permute-start(bf16[48,4096]{1,0:T(8,128)(2,1)S(1)} %get-tuple-element.57), channel_id=1, source_target_pairs={{0,1},{1,2},{2,3},{3,0},{4,5},{5,6},{6,7},{7,4},{8,9},{9,10},{10,1... | collective-permute-start | bytes 1179656 | tf_op jit(solution)/shard_map/ppermute | solution.py:29
  151.1 9.3 %collective-permute-start.6 = (bf16[48,4096]{1,0:T(8,128)(2,1)S(1)}, bf16[48,4096]{1,0:T(8,128)(2,1)S(1)}, u32[]{:S(2)}, u32[]{:S(2)}) collective-permute-start(bf16[48,4096]{1,0:T(8,128)(2,1)S(1)} %get-tuple-element.58), channel_id=1, source_target_pairs={{0,3},{1,0},{2,1},{3,2},{4,7},{5,4},{6,5},{7,6},{8,11},{9,8},{10,9... | collective-permute-start | bytes 1179656 | tf_op jit(solution)/shard_map/ppermute | solution.py:29
  151.9 39.5 %collective-permute-start.2 = (bf16[96,4096]{1,0:T(8,128)(2,1)S(1)}, bf16[96,4096]{1,0:T(8,128)(2,1)S(1)}, u32[]{:S(2)}, u32[]{:S(2)}) collective-permute-start(bf16[96,4096]{1,0:T(8,128)(2,1)S(1)} %add_convert_fusion.3), channel_id=1, source_target_pairs={{0,4},{1,5},{2,6},{3,7},{4,0},{5,1},{6,2},{7,3},{8,12},{9,13},{10,... | collective-permute-start | bytes 2359304 | tf_op jit(solution)/shard_map/ppermute | solution.py:29
  158.7 1.8 copy-start.2
  158.8 34.8 %collective-permute-start.5 = (bf16[96,4096]{1,0:T(8,128)(2,1)S(1)}, bf16[96,4096]{1,0:T(8,128)(2,1)S(1)}, u32[]{:S(2)}, u32[]{:S(2)}) collective-permute-start(bf16[96,4096]{1,0:T(8,128)(2,1)S(1)} %pad_maximum_fusion), channel_id=1, source_target_pairs={{0,1},{1,2},{2,3},{3,0},{4,5},{5,6},{6,7},{7,4},{8,9},{9,10},{10,1... | collective-permute-start | bytes 2359304 | tf_op jit(solution)/shard_map/ppermute | solution.py:29
  161.1 3.5 %copy-start = (bf16[8,512,256]{2,1,0:T(8,128)(2,1)S(1)}, bf16[8,512,256]{2,1,0:T(8,128)(2,1)}, u32[]{:S(2)}) copy-start(bf16[8,512,256]{2,1,0:T(8,128)(2,1)} %get-tuple-element.49) | copy-start | bytes 6291460
  161.2 25.3 %collective-permute-start.17 = (bf16[1024,256]{1,0:T(8,128)(2,1)S(1)}, bf16[1024,256]{1,0:T(8,128)(2,1)S(1)}, u32[]{:S(2)}, u32[]{:S(2)}) collective-permute-start(bf16[1024,256]{1,0:T(8,128)(2,1)S(1)} %get-tuple-element.54), channel_id=1, source_target_pairs={{0,32},{8,40},{16,48},{24,56},{32,64},{40,72},{48,80},{56,88},{64,... | collective-permute-start | bytes 1572872 | tf_op jit(solution)/shard_map/ppermute | solution.py:36
  161.3 28.1 %collective-permute-start.18 = (bf16[1024,256]{1,0:T(8,128)(2,1)S(1)}, bf16[1024,256]{1,0:T(8,128)(2,1)S(1)}, u32[]{:S(2)}, u32[]{:S(2)}) collective-permute-start(bf16[1024,256]{1,0:T(8,128)(2,1)S(1)} %get-tuple-element.56), channel_id=1, source_target_pairs={{0,64},{8,72},{16,80},{24,88},{32,96},{40,104},{48,112},{56,120},{... | collective-permute-start | bytes 1572872 | tf_op jit(solution)/shard_map/ppermute | solution.py:36
  162.1 2.5 %copy-start.1 = (bf16[4096,256]{1,0:T(8,128)(2,1)}, bf16[4096,256]{1,0:T(8,128)(2,1)S(1)}, u32[]{:S(2)}) copy-start(bf16[4096,256]{1,0:T(8,128)(2,1)S(1)} %collective-permute-done.25) | copy-start | bytes 6291460
  162.1 27.3 %collective-permute-start.19 = (bf16[1024,256]{1,0:T(8,128)(2,1)S(1)}, bf16[1024,256]{1,0:T(8,128)(2,1)S(1)}, u32[]{:S(2)}, u32[]{:S(2)}) collective-permute-start(bf16[1024,256]{1,0:T(8,128)(2,1)S(1)} %get-tuple-element.55), channel_id=1, source_target_pairs={{0,96},{8,104},{16,112},{24,120},{32,0},{40,8},{48,16},{56,24},{64... | collective-permute-start | bytes 1572872 | tf_op jit(solution)/shard_map/ppermute | solution.py:36
  186.5 17.4 %collective-permute-start.7 = (bf16[96,4096]{1,0:T(8,128)(2,1)S(1)}, bf16[96,4096]{1,0:T(8,128)(2,1)S(1)}, u32[]{:S(2)}, u32[]{:S(2)}) collective-permute-start(bf16[96,4096]{1,0:T(8,128)(2,1)S(1)} %pad_maximum_fusion.1), channel_id=1, source_target_pairs={{0,3},{1,0},{2,1},{3,2},{4,7},{5,4},{6,5},{7,6},{8,11},{9,8},{10,9... | collective-permute-start | bytes 2359304 | tf_op jit(solution)/shard_map/ppermute | solution.py:29
  189.4 14.5 %copy-start.7 = (bf16[96,4096]{1,0:T(8,128)(2,1)S(1)}, bf16[96,4096]{1,0:T(8,128)(2,1)}, u32[]{:S(2)}) copy-start(bf16[96,4096]{1,0:T(8,128)(2,1)} %get-tuple-element.31) | copy-start | bytes 2359300
  189.4 22.8 %collective-permute-start.26 = (bf16[1024,256]{1,0:T(8,128)(2,1)}, bf16[1024,256]{1,0:T(8,128)(2,1)S(1)}, u32[]{:S(2)}, u32[]{:S(2)}) collective-permute-start(bf16[1024,256]{1,0:T(8,128)(2,1)} %get-tuple-element.51), channel_id=1, source_target_pairs={{0,32},{8,40},{16,48},{24,56},{32,64},{40,72},{48,80},{56,88},{64,... | collective-permute-start | bytes 1572872 | tf_op jit(solution)/shard_map/ppermute | solution.py:36
  189.4 25.0 %collective-permute-start.27 = (bf16[1024,256]{1,0:T(8,128)(2,1)}, bf16[1024,256]{1,0:T(8,128)(2,1)S(1)}, u32[]{:S(2)}, u32[]{:S(2)}) collective-permute-start(bf16[1024,256]{1,0:T(8,128)(2,1)} %get-tuple-element.53), channel_id=1, source_target_pairs={{0,64},{8,72},{16,80},{24,88},{32,96},{40,104},{48,112},{56,120},{... | collective-permute-start | bytes 1572872 | tf_op jit(solution)/shard_map/ppermute | solution.py:36
  191.4 23.0 %collective-permute-start.28 = (bf16[1024,256]{1,0:T(8,128)(2,1)}, bf16[1024,256]{1,0:T(8,128)(2,1)S(1)}, u32[]{:S(2)}, u32[]{:S(2)}) collective-permute-start(bf16[1024,256]{1,0:T(8,128)(2,1)} %get-tuple-element.52), channel_id=1, source_target_pairs={{0,96},{8,104},{16,112},{24,120},{32,0},{40,8},{48,16},{56,24},{64... | collective-permute-start | bytes 1572872 | tf_op jit(solution)/shard_map/ppermute | solution.py:36
  193.7 11.6 %collective-permute-start.20 = (bf16[512,256]{1,0:T(8,128)(2,1)S(1)}, bf16[512,256]{1,0:T(8,128)(2,1)S(1)}, u32[]{:S(2)}, u32[]{:S(2)}) collective-permute-start(bf16[512,256]{1,0:T(8,128)(2,1)S(1)} %get-tuple-element.59), channel_id=1, source_target_pairs={{0,16},{8,24},{16,0},{24,8},{32,48},{40,56},{48,32},{56,40},{64,80... | collective-permute-start | bytes 786440 | tf_op jit(solution)/shard_map/ppermute | solution.py:36
  205.3 0.7 copy-start.8
  208.8 8.2 %copy-start.12 = (bf16[2,96,256]{2,1,0:T(8,128)(2,1)S(1)}, bf16[2,96,256]{2,1,0:T(8,128)(2,1)}, u32[]{:S(2)}) copy-start(bf16[2,96,256]{2,1,0:T(8,128)(2,1)} %get-tuple-element.45) | copy-start | bytes 294916
  208.8 7.1 %collective-permute-start.21 = (bf16[2,96,256]{2,1,0:T(8,128)(2,1)}, bf16[2,96,256]{2,1,0:T(8,128)(2,1)S(1)}, u32[]{:S(2)}, u32[]{:S(2)}) collective-permute-start(bf16[2,96,256]{2,1,0:T(8,128)(2,1)} %get-tuple-element.46), channel_id=1, source_target_pairs={{0,1},{1,2},{2,3},{3,0},{4,5},{5,6},{6,7},{7,4},{8,9},{9,10},{10,1... | collective-permute-start | bytes 294920 | tf_op jit(solution)/shard_map/ppermute | solution.py:29
  209.1 6.7 %collective-permute-start.22 = (bf16[2,96,256]{2,1,0:T(8,128)(2,1)}, bf16[2,96,256]{2,1,0:T(8,128)(2,1)S(1)}, u32[]{:S(2)}, u32[]{:S(2)}) collective-permute-start(bf16[2,96,256]{2,1,0:T(8,128)(2,1)} %get-tuple-element.47), channel_id=1, source_target_pairs={{0,2},{1,3},{2,0},{3,1},{4,6},{5,7},{6,4},{7,5},{8,10},{9,11},{10,... | collective-permute-start | bytes 294920 | tf_op jit(solution)/shard_map/ppermute | solution.py:29
  212.2 4.8 %collective-permute-start.23 = (bf16[2,96,256]{2,1,0:T(8,128)(2,1)}, bf16[2,96,256]{2,1,0:T(8,128)(2,1)S(1)}, u32[]{:S(2)}, u32[]{:S(2)}) collective-permute-start(bf16[2,96,256]{2,1,0:T(8,128)(2,1)} %get-tuple-element.48), channel_id=1, source_target_pairs={{0,3},{1,0},{2,1},{3,2},{4,7},{5,4},{6,5},{7,6},{8,11},{9,8},{10,9... | collective-permute-start | bytes 294920 | tf_op jit(solution)/shard_map/ppermute | solution.py:29
  214.7 6.9 %collective-permute-start.29 = (bf16[512,256]{1,0:T(8,128)(2,1)S(1)}, bf16[512,256]{1,0:T(8,128)(2,1)S(1)}, u32[]{:S(2)}, u32[]{:S(2)}) collective-permute-start(bf16[512,256]{1,0:T(8,128)(2,1)S(1)} %slice.125), channel_id=1, source_target_pairs={{0,16},{8,24},{16,0},{24,8},{32,48},{40,56},{48,32},{56,40},{64,80... | collective-permute-start | bytes 786440 | tf_op jit(solution)/shard_map/ppermute | solution.py:36
  217.1 5.7 %collective-permute-start.24 = (bf16[96,256]{1,0:T(8,128)(2,1)S(1)}, bf16[96,256]{1,0:T(8,128)(2,1)S(1)}, u32[]{:S(2)}, u32[]{:S(2)}) collective-permute-start(bf16[96,256]{1,0:T(8,128)(2,1)S(1)} %slice_bitcast_fusion), channel_id=1, source_target_pairs={{0,4},{1,5},{2,6},{3,7},{4,0},{5,1},{6,2},{7,3},{8,12},{9,13},{10,... | collective-permute-start | bytes 147464 | tf_op jit(solution)/shard_map/ppermute | solution.py:29
Sparse Core Ops, SparseCore 0:
  10.5 49.9 all-gather.1

commit v2 on v1

v2 whole, which is shorter than its diff:
```python
import functools
import math

import jax
import jax.numpy as jnp
from jax import lax
from jax.experimental import pallas as pl
from jax.experimental.pallas import tpu as pltpu
from jax.sharding import PartitionSpec as P

HD = 128
GROUP = 16
HEADS_DEV = 4
ROWS = 768
WIN = 128
ELDER = 512
TREE = 21
NEG = -1e30
SCALE = HD ** (-0.5)
SCALE2 = SCALE * math.log2(math.e)
VMEM = 60 * 1024 * 1024
F32 = jnp.float32
BF16 = jnp.bfloat16

Y_GROUPS = [[0, 1, 2, 3], [4, 5, 6, 7]]
Z_GROUPS = [[0, 4, 8, 12], [1, 5, 9, 13], [2, 6, 10, 14], [3, 7, 11, 15]]
SMEM_SPEC = pl.BlockSpec(memory_space=pltpu.SMEM)
VMEM_SPEC = pl.BlockSpec(memory_space=pltpu.VMEM)


def head_perm(array, dx, dy):
    pairs = [(h, ((h // 4 + dx) % 2) * 4 + (h + dy) % 4) for h in range(8)]
    return lax.ppermute(array, "head", pairs)


def leaf_perm(array, dz, dx, dc):
    pairs = [
        (l, ((l // 4 + dz) % 4) * 4 + ((l // 2 + dx) % 2) * 2 + (l + dc) % 2) for l in range(16)
    ]
    return lax.ppermute(array, "leaf", pairs)


def after(array, *others):
    return lax.optimization_barrier((array, *others))[0]


def add(*parts):
    total = parts[0].astype(F32)
    for part in parts[1:]:
        total = total + part.astype(F32)
    return total.astype(BF16)


def pick(rows, side):
    return jnp.where(side == 0, rows[:, :HD], rows[:, HD:])


def elder_start(offset):
    return jnp.minimum(offset, ROWS - ELDER)


def pack_kernel(place, owner, offset, key_ref, value_ref, own_ref, elder_ref):
    leaf, side = place[0], place[1] // 4
    own_ref[:, :HD] = pick(key_ref[...], side)
    own_ref[:, HD:] = pick(value_ref[...], side)

    def find(i, start):
        mine = (owner[i] == leaf) & (i % TREE < 5)
        return jnp.where(mine, elder_start(offset[i]), start)

    start = lax.fori_loop(0, owner.shape[0], find, jnp.int32(0))
    elder_ref[...] = own_ref[pl.ds(pl.multiple_of(start, WIN), ELDER), :]


def pack(place, owner, offset, key_rows, value_rows):
    return pl.pallas_call(
        pack_kernel,
        out_shape=(
            jax.ShapeDtypeStruct((ROWS, 2 * HD), BF16),
            jax.ShapeDtypeStruct((ELDER, 2 * HD), BF16),
        ),
        in_specs=[SMEM_SPEC] * 3 + [VMEM_SPEC] * 2,
        out_specs=(VMEM_SPEC, VMEM_SPEC),
        compiler_params=pltpu.CompilerParams(vmem_limit_bytes=VMEM),
        cost_estimate=pl.CostEstimate(flops=0, bytes_accessed=100_000, transcendentals=0),
        name="pack_keys",
    )(place, owner, offset, key_rows, value_rows)


def relative_leaf(leaf, other):
    core = (leaf + other) % 2
    cross = (leaf // 2 + other // 2) % 2
    return core * 8 + other // 4 * 2 + cross


def fill_table(table, place, owner, parent, offset, length):
    leaf = place[0]
    for w in range(ROWS // WIN):
        table[w, 0] = -1

    def first_row(segment):
        shift = offset[segment] - elder_start(offset[segment])
        return relative_leaf(leaf, owner[segment]) * ELDER + shift

    def visit(i, unused):
        @pl.when(owner[i] == leaf)
        def _():
            level = i % TREE
            prompt = i - level
            branch = jnp.where(level >= 5, parent[i], i)
            prompt_base = first_row(prompt)
            branch_base = first_row(branch)
            tiles = jnp.where(level == 0, 4, jnp.where(level < 5, 2, 1))
            first = jnp.where(level == 0, 0, jnp.where(level < 5, 4, 6))
            window = offset[i] // WIN
            for j in range(4):

                @pl.when(j < tiles)
                def _():
                    table[window + j, 0] = first + j
                    table[window + j, 1] = length[i] - j * WIN
                    table[window + j, 2] = prompt_base
                    table[window + j, 3] = branch_base

        return unused

    lax.fori_loop(0, owner.shape[0], visit, 0)


def heads_down(block):
    return jnp.concatenate([block[:, h * HD : (h + 1) * HD] for h in range(HEADS_DEV)], axis=0)


def tile_base(table, w, t):
    base = table[w, 2] + t * WIN if t < 4 else table[w, 3] + (t - 4) * WIN
    return pl.multiple_of(base, WIN)


def for_windows(table, empty, full):
    def window(w, unused):
        count = table[w, 0]
        rows = pl.ds(pl.multiple_of(w * WIN, WIN), WIN)
        for tiles in range(-1, 7):

            @pl.when(count == tiles)
            def _(tiles=tiles):
                if tiles < 0:
                    empty(w, rows)
                else:
                    full(w, rows, tiles)

        return unused

    lax.fori_loop(0, ROWS // WIN, window, 0)


def load_tiles(table, w, rows, tiles, mine_ref, other_ref, own_ref, pair_buf):
    half = 8 * ELDER
    for t in range(tiles):
        base = tile_base(table, w, t)
        spot = pl.ds(pl.multiple_of(base % half, WIN), WIN)
        pair_buf[t * WIN : (t + 1) * WIN, :] = jnp.where(
            base < half, mine_ref[spot, :], other_ref[spot, :]
        )
    pair_buf[tiles * WIN : (tiles + 1) * WIN, :] = own_ref[rows, :]


def masked(scores, tiles, fill):
    own = scores[:, tiles * WIN :]
    col = lax.broadcasted_iota(jnp.int32, own.shape, 1)
    row = lax.broadcasted_iota(jnp.int32, own.shape, 0) % WIN
    own = jnp.where(col <= row, own, fill)
    return jnp.concatenate([scores[:, : tiles * WIN], own], axis=1) if tiles else own


def live_rows(table, w):
    row = lax.broadcasted_iota(jnp.int32, (HEADS_DEV * WIN, 1), 0) % WIN
    return row < table[w, 1]


def scores_of(query, keys):
    return lax.dot_general(query, keys, (((1,), (1,)), ((), ())), preferred_element_type=F32)


def forward_kernel(
    place, owner, parent, offset, length, query_ref, own_ref, elder_mine_ref,
    elder_other_ref, attn_ref, stat_ref, table, pair_buf,
):
    fill_table(table, place, owner, parent, offset, length)

    def empty(w, rows):
        attn_ref[rows, :] = jnp.zeros((WIN, HEADS_DEV * HD), BF16)
        stat_ref[rows, :] = jnp.zeros((WIN, HD), F32)

    def full(w, rows, tiles):
        load_tiles(table, w, rows, tiles, elder_mine_ref, elder_other_ref, own_ref, pair_buf)
        span = (tiles + 1) * WIN
        query = heads_down(query_ref[rows, :])
        scores = masked(scores_of(query, pair_buf[:span, :HD]), tiles, NEG)
        top = jnp.max(scores, axis=1, keepdims=True)
        weights = jnp.exp2((scores - top) * SCALE2)
        total = jnp.sum(weights, axis=1, keepdims=True)
        live = live_rows(table, w)
        attn = jnp.dot(weights.astype(BF16), pair_buf[:span, HD:], preferred_element_type=F32)
        attn = (attn * jnp.where(live, 1.0 / total, 0.0)).astype(BF16)
        stat = jnp.where(live, top * SCALE2 + jnp.log2(total), -NEG)
        lane = lax.broadcasted_iota(jnp.int32, (WIN, HD), 1)
        packed = jnp.zeros((WIN, HD), F32)
        for h in range(HEADS_DEV):
            part = slice(h * WIN, (h + 1) * WIN)
            attn_ref[rows, h * HD : (h + 1) * HD] = attn[part]
            packed = jnp.where(lane == h, stat[part], packed)
        stat_ref[rows, :] = packed

    for_windows(table, empty, full)


def forward(place, segs, query_rows, own, elders):
    return pl.pallas_call(
        forward_kernel,
        out_shape=(
            jax.ShapeDtypeStruct((ROWS, HEADS_DEV * HD), BF16),
            jax.ShapeDtypeStruct((ROWS, HD), F32),
        ),
        in_specs=[SMEM_SPEC] * 5 + [VMEM_SPEC] * 4,
        out_specs=(VMEM_SPEC, VMEM_SPEC),
        scratch_shapes=[pltpu.SMEM((6, 8), jnp.int32), pltpu.VMEM((7 * WIN, 2 * HD), BF16)],
        compiler_params=pltpu.CompilerParams(vmem_limit_bytes=VMEM),
        cost_estimate=pl.CostEstimate(flops=0, bytes_accessed=100_000, transcendentals=0),
        name="attention",
    )(place, *segs, query_rows, own, *elders)


def relative_head(head, k):
    return ((head // 4 + k // 4) % 2) * 4 + (head + k) % 4


def project_kernel(attn_ref, weight_ref, out_ref):
    out_ref[...] = jnp.dot(attn_ref[...], weight_ref[...], preferred_element_type=F32).astype(BF16)


def project(attn, out_weight):
    width = out_weight.shape[1]
    step = 1024
    return pl.pallas_call(
        project_kernel,
        grid=(width // step,),
        out_shape=jax.ShapeDtypeStruct((ROWS, width), BF16),
        in_specs=[
            pl.BlockSpec((ROWS, HEADS_DEV * HD), lambda n: (0, 0)),
            pl.BlockSpec((HEADS_DEV * HD, step), lambda n: (0, n)),
        ],
        out_specs=pl.BlockSpec((ROWS, step), lambda n: (0, n)),
        compiler_params=pltpu.CompilerParams(vmem_limit_bytes=VMEM),
        cost_estimate=pl.CostEstimate(flops=0, bytes_accessed=100_000, transcendentals=0),
        name="project",
    )(attn, out_weight)


def attn_grad_kernel(place, weight_ref, *refs):
    pieces, grad_ref, rows, total = refs[:8], *refs[8:]
    n = pl.program_id(0)
    for k in range(8):
        first = pl.multiple_of(relative_head(place[1], k) * 96, 32)
        rows[pl.ds(first, 96), :] = pieces[k][...]
    part = scores_of(rows[...], weight_ref[...])

    @pl.when(n == 0)
    def _():
        total[...] = part

    @pl.when(n > 0)
    def _():
        total[...] += part

    @pl.when(n == pl.num_programs(0) - 1)
    def _():
        grad_ref[...] = total[...].astype(BF16)


def attn_grad_of(place, out_weight, pieces):
    feats, width = out_weight.shape
    step = 1024
    return pl.pallas_call(
        attn_grad_kernel,
        grid=(width // step,),
        out_shape=jax.ShapeDtypeStruct((ROWS, feats), BF16),
        in_specs=[SMEM_SPEC, pl.BlockSpec((feats, step), lambda n: (0, n))]
        + [pl.BlockSpec((96, step), lambda n: (0, n))] * 8,
        out_specs=pl.BlockSpec((ROWS, feats), lambda n: (0, 0)),
        scratch_shapes=[pltpu.VMEM((ROWS, step), BF16), pltpu.VMEM((ROWS, feats), F32)],
        compiler_params=pltpu.CompilerParams(vmem_limit_bytes=VMEM),
        cost_estimate=pl.CostEstimate(flops=0, bytes_accessed=100_000, transcendentals=0),
        name="attn_grad",
    )(place, out_weight, *pieces)


def weight_grad_kernel(place, attn_ref, *rest):
    pieces, mine_ref, other_ref, turned, rows = rest[:8], *rest[8:]
    leaf = place[0]

    @pl.when(pl.program_id(0) == 0)
    def _():
        turned[...] = attn_ref[...].T

    for k in range(8):
        first = pl.multiple_of(relative_head(place[1], k) * 96, 32)
        rows[pl.ds(first, 96), :] = pieces[k][...]
    product = jnp.dot(turned[...], rows[...], preferred_element_type=F32).astype(BF16)
    for j in range(4):
        part = product[:, j * 256 : (j + 1) * 256]
        cross = (leaf // 2 + j // 2) % 2

        @pl.when(leaf % 2 == j % 2)
        def _():
            mine_ref[cross] = part

        @pl.when(leaf % 2 != j % 2)
        def _():
            other_ref[cross] = part


def weight_grad_of(place, attn, pieces):
    feats, width = HEADS_DEV * HD, pieces[0].shape[1]
    step = width // 4
    return pl.pallas_call(
        weight_grad_kernel,
        grid=(4,),
        in_specs=[SMEM_SPEC, pl.BlockSpec((ROWS, feats), lambda n: (0, 0))]
        + [pl.BlockSpec((96, step), lambda n: (0, n))] * 8,
        out_specs=[pl.BlockSpec((2, feats, step // 4), lambda n: (n, 0, 0))] * 2,
        scratch_shapes=[pltpu.VMEM((feats, ROWS), BF16), pltpu.VMEM((ROWS, step), BF16)],
        out_shape=[jax.ShapeDtypeStruct((8, feats, step // 4), BF16)] * 2,
        compiler_params=pltpu.CompilerParams(vmem_limit_bytes=VMEM),
        cost_estimate=pl.CostEstimate(flops=0, bytes_accessed=100_000, transcendentals=0),
        name="weight_grad",
    )(place, attn, *pieces)


def backward_kernel(
    place, owner, parent, offset, length, query_ref, grad_ref, attn_ref, stat_ref, own_ref,
    elder_mine_ref, elder_other_ref, query_grad_ref, own_grad_ref, mine_ref, other_ref, table,
    pair_buf, elder_sum,
):
    fill_table(table, place, owner, parent, offset, length)
    elder_sum[...] = jnp.zeros_like(elder_sum)

    def empty(w, rows):
        query_grad_ref[rows, :] = jnp.zeros((WIN, HEADS_DEV * HD), BF16)
        own_grad_ref[rows, :] = jnp.zeros((WIN, 2 * HD), F32)

    def full(w, rows, tiles):
        load_tiles(table, w, rows, tiles, elder_mine_ref, elder_other_ref, own_ref, pair_buf)
        span = (tiles + 1) * WIN
        query = heads_down(query_ref[rows, :])
        grad = heads_down(grad_ref[rows, :])
        attn = heads_down(attn_ref[rows, :])
        packed = stat_ref[rows, :]
        stat = jnp.concatenate([packed[:, h : h + 1] for h in range(HEADS_DEV)], axis=0)
        delta = jnp.sum(grad.astype(F32) * attn.astype(F32), axis=1, keepdims=True)
        keys, values = pair_buf[:span, :HD], pair_buf[:span, HD:]
        probs = jnp.exp2(masked(scores_of(query, keys) * SCALE2 - stat, tiles, NEG))
        dprobs = scores_of(grad, values)
        dscores = (probs * (dprobs - delta)).astype(BF16)
        probs = probs.astype(BF16)
        query_grad = jnp.dot(dscores, keys, preferred_element_type=F32)
        query_grad = (query_grad * SCALE).astype(BF16)
        for h in range(HEADS_DEV):
            query_grad_ref[rows, h * HD : (h + 1) * HD] = query_grad[h * WIN : (h + 1) * WIN]
        turn = (((0,), (0,)), ((), ()))
        key_grad = SCALE * lax.dot_general(dscores, query, turn, preferred_element_type=F32)
        value_grad = lax.dot_general(probs, grad, turn, preferred_element_type=F32)
        for t in range(tiles):
            spot = pl.ds(tile_base(table, w, t), WIN)
            part = slice(t * WIN, (t + 1) * WIN)
            elder_sum[spot, :HD] += key_grad[part]
            elder_sum[spot, HD:] += value_grad[part]
        own_grad_ref[rows, :HD] = key_grad[tiles * WIN :]
        own_grad_ref[rows, HD:] = value_grad[tiles * WIN :]

    for_windows(table, empty, full)
    mine_ref[...] = elder_sum[: 8 * ELDER, :].astype(BF16)
    other_ref[...] = elder_sum[8 * ELDER :, :].astype(BF16)


def backward(place, segs, query_rows, grad, attn, stat, own, elders):
    return pl.pallas_call(
        backward_kernel,
        out_shape=(
            jax.ShapeDtypeStruct((ROWS, HEADS_DEV * HD), BF16),
            jax.ShapeDtypeStruct((ROWS, 2 * HD), F32),
            jax.ShapeDtypeStruct((8 * ELDER, 2 * HD), BF16),
            jax.ShapeDtypeStruct((8 * ELDER, 2 * HD), BF16),
        ),
        in_specs=[SMEM_SPEC] * 5 + [VMEM_SPEC] * 7,
        out_specs=(VMEM_SPEC,) * 4,
        scratch_shapes=[
            pltpu.SMEM((6, 8), jnp.int32),
            pltpu.VMEM((7 * WIN, 2 * HD), BF16),
            pltpu.VMEM((16 * ELDER, 2 * HD), F32),
        ],
        compiler_params=pltpu.CompilerParams(vmem_limit_bytes=VMEM),
        cost_estimate=pl.CostEstimate(flops=0, bytes_accessed=100_000, transcendentals=0),
        name="attention_back",
    )(place, *segs, query_rows, grad, attn, stat, own, *elders)


def settle_kernel(place, owner, offset, own_ref, *rest):
    parts, out_ref, total = rest[:2], rest[2], rest[3]
    leaf, head = place[0], place[1]
    total[...] = own_ref[...]

    def find(i, start):
        mine = (owner[i] == leaf) & (i % TREE < 5)
        return jnp.where(mine, elder_start(offset[i]), start)

    start = lax.fori_loop(0, owner.shape[0], find, jnp.int32(0))
    spot = pl.ds(pl.multiple_of(start, WIN), ELDER)
    total[spot, :] += sum(part[...].astype(F32) for part in parts)
    for y in range(4):
        for side in range(2):
            first = pl.multiple_of(((head // 4 + side) % 2 * 4 + y) * 96, 32)
            out_ref[y, side] = total[pl.ds(first, 96), :].astype(BF16)


def settle(place, owner, offset, own, parts):
    return pl.pallas_call(
        settle_kernel,
        out_shape=jax.ShapeDtypeStruct((4, 2, 96, 2 * HD), BF16),
        in_specs=[SMEM_SPEC] * 3 + [VMEM_SPEC] * 3,
        out_specs=VMEM_SPEC,
        scratch_shapes=[pltpu.VMEM((ROWS, 2 * HD), F32)],
        compiler_params=pltpu.CompilerParams(vmem_limit_bytes=VMEM),
        cost_estimate=pl.CostEstimate(flops=0, bytes_accessed=100_000, transcendentals=0),
        name="settle",
    )(place, owner, offset, own, *parts)


def exchange(blocks, axis, groups=None):
    return lax.all_to_all(blocks, axis, 0, 0, axis_index_groups=groups)


def spread_depth(blocks):
    depth = lax.axis_index("leaf") // 4
    ahead = [
        lax.dynamic_index_in_dim(blocks, (depth + d) % 4, 0, keepdims=False) for d in range(4)
    ]
    return [ahead[0], *[leaf_perm(ahead[d], d, 0, 0) for d in range(1, 4)]]


def sum_blocks(blocks):
    return add(*[blocks[i] for i in range(blocks.shape[0])])


def shards(
    query_rows, key_rows, value_rows, out_weight, out_grad, seg_owner, seg_parent, seg_offset,
    seg_length,
):
    place = jnp.stack([lax.axis_index("leaf"), lax.axis_index("head")]).astype(jnp.int32)
    side = lax.axis_index("head") // 4
    segs = (seg_owner, seg_parent, seg_offset, seg_length)
    own, elder = pack(place, seg_owner, seg_offset, key_rows, value_rows)
    pair = jnp.concatenate([elder, leaf_perm(elder, 0, 1, 0)], axis=0)

    rows = after(out_grad, pair)
    elder_mine = exchange(jnp.broadcast_to(pair, (4, *pair.shape)), "leaf", Z_GROUPS)
    before = head_perm(rows, 0, 1)
    behind = head_perm(rows, 0, -1)
    cross = head_perm(rows, 1, 0)
    elder_mine, before, behind, cross = lax.optimization_barrier(
        (elder_mine, before, behind, cross)
    )

    half = rows.shape[0] // 2
    far = jnp.concatenate(
        [head_perm(before[:half], 0, 1), head_perm(behind[half:], 0, -1)], axis=0
    )
    elder_mine = elder_mine.reshape(8 * ELDER, 2 * HD)
    elder_other = leaf_perm(elder_mine, 0, 0, 1)
    far, elder_other, cross = lax.optimization_barrier((far, elder_other, cross))

    cross_before = head_perm(cross, 0, 1)
    cross_behind = head_perm(cross, 0, -1)
    cross_far = head_perm(far, 1, 0)
    elders = (elder_mine, elder_other)
    attn, stat = forward(place, segs, query_rows, own, elders)
    partial = project(attn, out_weight)
    partial, cross_before, cross_behind, cross_far = lax.optimization_barrier(
        (partial, cross_before, cross_behind, cross_far)
    )

    pieces = [rows, behind, far, before, cross, cross_behind, cross_far, cross_before]
    layer_parts = exchange(partial.reshape(8, 96, -1), "head")
    attn_grad = attn_grad_of(place, after(out_weight, partial), pieces)
    query_grads, own_grad, mine_pair, other_pair = backward(
        place, segs, query_rows, attn_grad, attn, stat, own, elders
    )
    pair_recv = leaf_perm(other_pair, 0, 0, 1)
    mine_weight, other_weight = weight_grad_of(place, after(attn, other_pair), pieces)
    weight_recv = leaf_perm(other_weight, 0, 0, 1)
    pair_joined = add(after(mine_pair, other_weight), pair_recv)
    pair_parts = spread_depth(pair_joined.reshape(4, 2 * ELDER, 2 * HD))
    weight_joined = add(mine_weight, weight_recv)
    weight_joined = after(weight_joined, *pair_parts)
    weight_parts = spread_depth(weight_joined.reshape(4, 2, *weight_joined.shape[1:]))
    pair_sum = add(*pair_parts)
    pair_sum, layer_parts = lax.optimization_barrier((pair_sum, layer_parts))
    pair_last = leaf_perm(pair_sum[ELDER:], 0, 1, 0)
    layer_out = sum_blocks(layer_parts)
    blocks = settle(place, seg_owner, seg_offset, own_grad, [pair_sum[:ELDER], pair_last])
    weight_parts = [after(part, blocks) for part in weight_parts]
    weight_sum = add(*weight_parts)
    weight_grad = add(weight_sum[0], leaf_perm(weight_sum[1], 0, 1, 0))
    total = sum_blocks(exchange(blocks, "head", Y_GROUPS))
    near = total[0]
    far = head_perm(total[1], 1, 0)
    first = jnp.where(side == 0, near, far)
    second = jnp.where(side == 0, far, near)
    key_grads = jnp.concatenate([first[:, :HD], second[:, :HD]], axis=1)
    value_grads = jnp.concatenate([first[:, HD:], second[:, HD:]], axis=1)
    return layer_out, query_grads, key_grads, value_grads, weight_grad


def solution(mesh):
    return jax.shard_map(
        shards,
        mesh=mesh,
        in_specs=(
            P("leaf", "head"),
            P("leaf", None),
            P("leaf", None),
            P("head", None),
            P(("leaf", "head"), None),
            P(),
            P(),
            P(),
            P(),
        ),
        out_specs=(
            P(("leaf", "head"), None),
            P("leaf", "head"),
            P(("leaf", "head"), None),
            P(("leaf", "head"), None),
            P("head", "leaf"),
        ),
        check_vma=False,
    )
```

time: 231 us -> 196 us (0.85)
  waiting for transfers between devices: 95.1 us -> 66.9 us
  Pallas kernels: 66.9 us -> 47.9 us
  between operations: 14.3 us -> 0.86 us
  starting transfers between devices: 42.4 us -> 53.6 us
  other arithmetic: 9.09 us -> 15.8 us
  local copies, waits for them, and re-layouts: 3.05 us -> 9.33 us
    ppermute x20 -> x9, waiting for transfers between devices: 63.4 us -> 30.4 us  [head_perm(): return lax.ppermute(array, 'head', pairs)]
    all_to_all x0 -> x3, starting transfers between devices: none -> 15.4 us  [exchange(): return lax.all_to_all(blocks, axis, 0, 0, axis_index_groups=groups)]
    pallas_call x3 -> x4, Pallas kernels: 39.7 us -> 27.5 us  [the longest x1 8.97 us: weight_grad_of(): pl.pallas_call(weight_grad_kernel, grid=(4,), in_specs=[SMEM_SPEC, pl.Blo...]
    ppermute x20 -> x9, starting transfers between devices: 31.3 us -> 20.1 us  [head_perm(): return lax.ppermute(array, 'head', pairs)]
    ppermute x10 -> x12, waiting for transfers between devices: 23.7 us -> 33.8 us  [leaf_perm(): return lax.ppermute(array, 'leaf', pairs)]
    all_gather x1 -> x0, waiting for transfers between devices: 7.96 us -> none  [shards(): gathered = lax.all_gather(elder, 'leaf', axis=0, tiled=True)]
    ppermute x10 -> x12, starting transfers between devices: 11.1 us -> 18.1 us  [leaf_perm(): return lax.ppermute(array, 'leaf', pairs)]
    convert_element_type x10 -> x6, other arithmetic: 7.1 us -> 13.8 us  [add(): return total.astype(BF16)]
  transfers between devices with their start and end apart: 31 -> 24, of which waited for: 13 -> 13; matrix products, arithmetic and copies ran while one was open for 4% -> 10% of each run, Pallas kernels for 28% -> 23%
where the time goes in v2:
time: 196 us; the launch traced here: 194 us
  waiting for transfers between devices  66.9 us (34%)
  starting transfers between devices  53.6 us (27%)
  Pallas kernels  47.9 us (24%)
  other arithmetic  15.8 us (8%)
  local copies, waits for them, and re-layouts  9.33 us (5%)
    ppermute x12, waiting for transfers between devices, leaf_perm(): return lax.ppermute(array, 'leaf', pairs)  33.8 us
    ppermute x9, waiting for transfers between devices, head_perm(): return lax.ppermute(array, 'head', pairs)  30.4 us
    ppermute x9, starting transfers between devices, head_perm(): return lax.ppermute(array, 'head', pairs)  20.1 us
    ppermute x12, starting transfers between devices, leaf_perm(): return lax.ppermute(array, 'leaf', pairs)  18.1 us
    all_to_all x3, starting transfers between devices, exchange(): return lax.all_to_all(blocks, axis, 0, 0, axis_index_groups=groups)  15.4 us
    convert_element_type x6, other arithmetic, add(): return total.astype(BF16)  13.8 us
    pallas_call x1, Pallas kernels, backward(): pl.pallas_call(backward_kernel, out_shape=(jax.ShapeDtypeStruct((ROWS, HE...  10.8 us
    pallas_call x1, Pallas kernels, weight_grad_of(): pl.pallas_call(weight_grad_kernel, grid=(4,), in_specs=[SMEM_SPEC, pl.Blo...  8.97 us
  transfers between devices with their start and end apart: 24, of which 13 were waited for; matrix products, arithmetic and copies ran while one was open for 10% of the time, Pallas kernels for 23%

profile of v2, /device:TPU:0, one launch (start us, length us, event | category | flops | bytes accessed | tf_op | source)
XLA Modules:
  0.0 194.4 jit_solution(8400547894921822440)
XLA Ops:
  0.6 0.6 pad_add_fusion.place
  1.2 2.6 %pack_keys.1 = (bf16[768,256]{1,0:T(8,128)(2,1)}, bf16[512,256]{1,0:T(8,128)(2,1)}) custom-call(s32[2]{0:T(128)} %pad_add_fusion.place, s32[42]{0:T(128)} %owner.7, s32[42]{0:T(128)} %offset.7, bf16[768,256]{1,0:T(8,128)(2,1)} %key_ref.1, bf16[768,256]{1,0:T(8,128)(2,1)} %value_ref.1), custom_call_target="tpu_custom_call" | custom-call | bytes 100000 | tf_op jit(solution)/shard_map/pack_keys/pallas_call | solution.py:76
  3.8 1.6 collective-permute-start
  5.4 1.0 constant_dynamic-update-slice_fusion.1
  6.4 5.5 %collective-permute-done = bf16[512,256]{1,0:T(8,128)(2,1)S(1)} collective-permute-done((bf16[512,256]{1,0:T(8,128)(2,1)}, bf16[512,256]{1,0:T(8,128)(2,1)S(1)}, u32[]{:S(2)}, u32[]{:S(2)}) %collective-permute-start) | collective-permute-done | bytes 262176 | tf_op jit(solution)/shard_map/ppermute | solution.py:40
  11.9 1.5 broadcast_in_dim.3
  13.4 5.6 %all-to-all-start = ((bf16[4,1024,256]{2,1,0:T(8,128)(2,1)}), bf16[4,1024,256]{2,1,0:T(8,128)(2,1)S(1)}, u32[]{:S(2)}, u32[]{:S(2)}) async-start(bf16[4,1024,256]{2,1,0:T(8,128)(2,1)} %broadcast_in_dim.3), calls=%async_computation | async-start | bytes 4194304 | tf_op jit(solution)/shard_map/all_to_all | solution.py:440
  18.9 1.6 collective-permute-start.1
  20.5 1.7 collective-permute-start.2
  22.2 3.0 %collective-permute-start.3 = (bf16[96,4096]{1,0:T(8,128)(2,1)}, bf16[96,4096]{1,0:T(8,128)(2,1)}, u32[]{:S(2)}, u32[]{:S(2)}) collective-permute-start(bf16[96,4096]{1,0:T(8,128)(2,1)} %rest_0_), channel_id=1, source_target_pairs={{0,4},{1,5},{2,6},{3,7},{4,0},{5,1},{6,2},{7,3},{8,12},{9,13},{10,... | collective-permute-start | bytes 2359304 | tf_op jit(solution)/shard_map/ppermute | solution.py:33
  25.2 13.3 %collective-permute-done.1.refs_3_.rest_3_ = bf16[96,4096]{1,0:T(8,128)(2,1)S(1)} collective-permute-done((bf16[96,4096]{1,0:T(8,128)(2,1)}, bf16[96,4096]{1,0:T(8,128)(2,1)S(1)}, u32[]{:S(2)}, u32[]{:S(2)}) %collective-permute-start.1) | collective-permute-done | bytes 786464 | tf_op jit(solution)/shard_map/ppermute | solution.py:33
  38.6 0.0 collective-permute-done.2.refs_1_.rest_1_
  38.6 0.9 copy-done.4
  39.5 2.1 %collective-permute-done.3.refs_4_.rest_4_ = bf16[96,4096]{1,0:T(8,128)(2,1)} collective-permute-done((bf16[96,4096]{1,0:T(8,128)(2,1)}, bf16[96,4096]{1,0:T(8,128)(2,1)}, u32[]{:S(2)}, u32[]{:S(2)}) %collective-permute-start.3) | collective-permute-done | bytes 786464 | tf_op jit(solution)/shard_map/ppermute | solution.py:33
  41.6 2.8 %all-to-all-done = bf16[4,1024,256]{2,1,0:T(8,128)(2,1)S(1)} async-done(((bf16[4,1024,256]{2,1,0:T(8,128)(2,1)}), bf16[4,1024,256]{2,1,0:T(8,128)(2,1)S(1)}, u32[]{:S(2)}, u32[]{:S(2)}) %all-to-all-start) | async-done | bytes 2097184 | tf_op jit(solution)/shard_map/all_to_all | solution.py:440
  44.4 1.6 collective-permute-start.4
  46.1 1.0 slice.75
  47.1 2.0 %collective-permute-start.5 = (bf16[48,4096]{1,0:T(8,128)(2,1)S(1)}, bf16[48,4096]{1,0:T(8,128)(2,1)S(1)}, u32[]{:S(2)}, u32[]{:S(2)}) collective-permute-start(bf16[48,4096]{1,0:T(8,128)(2,1)S(1)} %slice.75), channel_id=1, source_target_pairs={{0,3},{1,0},{2,1},{3,2},{4,7},{5,4},{6,5},{7,6},{8,11},{9,8},{10,9... | collective-permute-start | bytes 1179656 | tf_op jit(solution)/shard_map/ppermute | solution.py:33
  49.1 8.2 %collective-permute-done.4 = bf16[48,4096]{1,0:T(8,128)(2,1)S(1)} collective-permute-done((bf16[48,4096]{1,0:T(8,128)(2,1)S(1)}, bf16[48,4096]{1,0:T(8,128)(2,1)S(1)}, u32[]{:S(2)}, u32[]{:S(2)}) %collective-permute-start.4) | collective-permute-done | bytes 393248 | tf_op jit(solution)/shard_map/ppermute | solution.py:33
  57.3 1.1 collective-permute-done.5
  58.4 0.1 pad_maximum_fusion.refs_2_.rest_2_
  58.5 1.3 copy-done.1
  59.9 1.6 collective-permute-start.7
  61.4 1.7 collective-permute-start.8
  63.1 3.0 %collective-permute-start.9 = (bf16[96,4096]{1,0:T(8,128)(2,1)S(1)}, bf16[96,4096]{1,0:T(8,128)(2,1)}, u32[]{:S(2)}, u32[]{:S(2)}) collective-permute-start(bf16[96,4096]{1,0:T(8,128)(2,1)S(1)} %pad_maximum_fusion.refs_2_.rest_2_), channel_id=1, source_target_pairs={{0,4},{1,5},{2,6},{3,7},{4,0},{5,1},{6,2},{7,3},{8,12},{9,13},{10,... | collective-permute-start | bytes 2359304 | tf_op jit(solution)/shard_map/ppermute | solution.py:33
  66.1 7.1 %attention.1 = (bf16[768,512]{1,0:T(8,128)(2,1)}, f32[768,128]{1,0:T(8,128)}) custom-call(s32[2]{0:T(128)} %pad_add_fusion.place, s32[42]{0:T(128)} %owner.7, s32[42]{0:T(128)} %parent.3, s32[42]{0:T(128)} %offset.7, s32[42]{0:T(128)} %length.3, bf16[768,512]{1,0:T(8,128)(2,1)} %query_ref.3, bf16[768,256]{1,0:T(8,128)(2,1)} %get-tuple-element.37.own_ref, ...), custom_call_target="tpu_custom_call" | custom-call | bytes 100000 | tf_op jit(solution)/shard_map/attention/pallas_call | solution.py:219
  73.2 7.5 %project.1 = bf16[768,4096]{1,0:T(8,128)(2,1)} custom-call(bf16[768,512]{1,0:T(8,128)(2,1)} %get-tuple-element.56.attn_ref, bf16[512,4096]{1,0:T(8,128)(2,1)} %weight_ref.2), custom_call_target="tpu_custom_call" | custom-call | bytes 100000 | tf_op jit(solution)/shard_map/project/pallas_call | solution.py:245
  80.7 2.3 %collective-permute-done.9.refs_6_.rest_6_ = bf16[96,4096]{1,0:T(8,128)(2,1)} collective-permute-done((bf16[96,4096]{1,0:T(8,128)(2,1)S(1)}, bf16[96,4096]{1,0:T(8,128)(2,1)}, u32[]{:S(2)}, u32[]{:S(2)}) %collective-permute-start.9) | collective-permute-done | bytes 786464 | tf_op jit(solution)/shard_map/ppermute | solution.py:33
  83.0 5.4 %all-to-all-start.1 = ((bf16[8,96,4096]{2,1,0:T(8,128)(2,1)}), bf16[8,96,4096]{2,1,0:T(8,128)(2,1)}, u32[]{:S(2)}, u32[]{:S(2)}) async-start(bf16[8,96,4096]{2,1,0:T(8,128)(2,1)} %bitcast.40), calls=%async_computation.1 | async-start | bytes 12582912 | tf_op jit(solution)/shard_map/all_to_all | solution.py:440
  88.4 8.2 %attn_grad.1.grad_ref = bf16[768,512]{1,0:T(8,128)(2,1)} custom-call(s32[2]{0:T(128)} %pad_add_fusion.place, bf16[512,4096]{1,0:T(8,128)(2,1)} %weight_ref.2, bf16[96,4096]{1,0:T(8,128)(2,1)} %rest_0_, bf16[96,4096]{1,0:T(8,128)(2,1)} %copy-done.4, bf16[96,4096]{1,0:T(8,128)(2,1)} %copy-done.2, bf16[96,4096]{1,0:T(8,128)(2,1)} %copy-done.3, ...), custom_call_target="tpu_custom_call" | custom-call | bytes 100000 | tf_op jit(solution)/shard_map/attn_grad/pallas_call | solution.py:284
  96.7 10.8 %attention_back.1 = (bf16[768,512]{1,0:T(8,128)(2,1)}, f32[768,256]{1,0:T(8,128)}, bf16[4096,256]{1,0:T(8,128)(2,1)}, bf16[4096,256]{1,0:T(8,128)(2,1)}) custom-call(s32[2]{0:T(128)} %pad_add_fusion.place, s32[42]{0:T(128)} %owner.7, s32[42]{0:T(128)} %parent.3, s32[42]{0:T(128)} %offset.7, s32[42]{0:T(128)} %length.3, bf16[768,512]{1,0:T(8,128)(2,1)} %query_ref.3, ...), custom_call_target="tpu_custom_call" | custom-call | bytes 100000 | tf_op jit(solution)/shard_map/attention_back/pallas_call | solution.py:387
  107.4 1.3 collective-permute-start.10
  108.8 9.0 %weight_grad.1 = (bf16[8,512,256]{2,1,0:T(8,128)(2,1)}, bf16[8,512,256]{2,1,0:T(8,128)(2,1)}) custom-call(s32[2]{0:T(128)} %pad_add_fusion.place, bf16[768,512]{1,0:T(8,128)(2,1)} %get-tuple-element.56.attn_ref, bf16[96,4096]{1,0:T(8,128)(2,1)} %rest_0_, bf16[96,4096]{1,0:T(8,128)(2,1)} %copy-done.4, bf16[96,4096]{1,0:T(8,128)(2,1)} %copy-done.2, ...), custom_call_target="tpu_custom_call" | custom-call | bytes 100000 | tf_op jit(solution)/shard_map/weight_grad/pallas_call | solution.py:326
  117.7 0.3 collective-permute-start.16
  118.1 2.8 %add_convert_fusion.1 = bf16[4096,256]{1,0:T(8,128)(2,1)S(1)} fusion(bf16[4096,256]{1,0:T(8,128)(2,1)} %collective-permute-done.10, bf16[4096,256]{1,0:T(8,128)(2,1)} %get-tuple-element.58), kind=kLoop, calls=%fused_computation.1 | loop fusion | flops 4194304 | bytes 6291456 | tf_op jit(solution)/shard_map/convert_element_type | solution.py:51
  120.9 0.9 dynamic-slice_bitcast_fusion.6
  121.8 3.9 %collective-permute-start.11 = (bf16[1024,256]{1,0:T(8,128)(2,1)}, bf16[1024,256]{1,0:T(8,128)(2,1)}, u32[]{:S(2)}, u32[]{:S(2)}) collective-permute-start(bf16[1024,256]{1,0:T(8,128)(2,1)} %get-tuple-element.75), channel_id=1, source_target_pairs={{0,32},{8,40},{16,48},{24,56},{32,64},{40,72},{48,80},{56,88},{64,... | collective-permute-start | bytes 1572872 | tf_op jit(solution)/shard_map/ppermute | solution.py:40
  125.7 1.1 collective-permute-start.12
  126.8 1.6 collective-permute-start.13
  128.4 2.7 %add_convert_fusion = bf16[8,512,256]{2,1,0:T(8,128)(2,1)S(1)} fusion(bf16[8,512,256]{2,1,0:T(8,128)(2,1)} %collective-permute-done.16, bf16[8,512,256]{2,1,0:T(8,128)(2,1)} %get-tuple-element.63), kind=kLoop, calls=%fused_computation | loop fusion | flops 4194304 | bytes 6291456 | tf_op jit(solution)/shard_map/convert_element_type | solution.py:51
  131.1 7.2 %collective-permute-done.11 = bf16[1024,256]{1,0:T(8,128)(2,1)} collective-permute-done((bf16[1024,256]{1,0:T(8,128)(2,1)}, bf16[1024,256]{1,0:T(8,128)(2,1)}, u32[]{:S(2)}, u32[]{:S(2)}) %collective-permute-start.11) | collective-permute-done | bytes 524320 | tf_op jit(solution)/shard_map/ppermute | solution.py:40
  138.3 11.9 %collective-permute-done.12 = bf16[1024,256]{1,0:T(8,128)(2,1)} collective-permute-done((bf16[1024,256]{1,0:T(8,128)(2,1)S(1)}, bf16[1024,256]{1,0:T(8,128)(2,1)}, u32[]{:S(2)}, u32[]{:S(2)}) %collective-permute-start.12) | collective-permute-done | bytes 524320 | tf_op jit(solution)/shard_map/ppermute | solution.py:40
  150.3 1.6 add_convert_fusion.4
  151.9 1.1 dynamic-slice_bitcast_fusion.3
  153.0 1.9 collective-permute-start.17
  154.9 1.4 collective-permute-start.18
  156.3 2.2 %collective-permute-start.19 = (bf16[2,512,256]{2,1,0:T(8,128)(2,1)S(1)}, bf16[2,512,256]{2,1,0:T(8,128)(2,1)}, u32[]{:S(2)}, u32[]{:S(2)}) collective-permute-start(bf16[2,512,256]{2,1,0:T(8,128)(2,1)S(1)} %get-tuple-element.72), channel_id=1, source_target_pairs={{0,96},{8,104},{16,112},{24,120},{32,0},{40,8},{48,16},{56,24},{64... | collective-permute-start | bytes 1572872 | tf_op jit(solution)/shard_map/ppermute | solution.py:40
  158.5 0.7 fusion.2
  159.3 0.5 collective-permute-start.14
  159.7 4.7 %fusion = bf16[96,4096]{1,0:T(8,128)(2,1)} fusion(bf16[8,96,4096]{2,1,0:T(8,128)(2,1)} %all-to-all-done.1), kind=kLoop, calls=%fused_computation.5 | loop fusion | flops 6291456 | bytes 7077888 | tf_op jit(solution)/shard_map/convert_element_type | solution.py:51
  164.4 1.9 collective-permute-done.14.rest_1_
  166.3 0.7 copy-done.5
  167.0 2.8 %settle.1 = bf16[4,2,96,256]{3,2,1,0:T(8,128)(2,1)} custom-call(s32[2]{0:T(128)} %pad_add_fusion.place, s32[42]{0:T(128)} %owner.7, s32[42]{0:T(128)} %offset.7, f32[768,256]{1,0:T(8,128)} %get-tuple-element.61.own_ref, bf16[512,256]{1,0:T(8,128)(2,1)} %get-tuple-element.79.rest_0_, bf16[512,256]{1,0:T(8,128)(2,1)} %copy-done.5), custom_call_target="tpu_custom_call" | custom-call | bytes 100000 | tf_op jit(solution)/shard_map/settle/pallas_call | solution.py:427
  169.8 4.4 %all-to-all-start.2 = ((bf16[4,2,96,256]{3,2,1,0:T(8,128)(2,1)}), bf16[4,2,96,256]{3,2,1,0:T(8,128)(2,1)S(1)}, u32[]{:S(2)}, u32[]{:S(2)}) async-start(bf16[4,2,96,256]{3,2,1,0:T(8,128)(2,1)} %settle.1), calls=%async_computation.2 | async-start | bytes 786432 | tf_op jit(solution)/shard_map/all_to_all | solution.py:440
  174.2 5.4 %collective-permute-done.18 = bf16[2,512,256]{2,1,0:T(8,128)(2,1)S(1)} collective-permute-done((bf16[2,512,256]{2,1,0:T(8,128)(2,1)}, bf16[2,512,256]{2,1,0:T(8,128)(2,1)S(1)}, u32[]{:S(2)}, u32[]{:S(2)}) %collective-permute-start.18) | collective-permute-done | bytes 524320 | tf_op jit(solution)/shard_map/ppermute | solution.py:40
  179.6 1.3 add_convert_fusion.3
  180.9 2.3 %collective-permute-start.20 = (bf16[512,256]{1,0:T(8,128)(2,1)S(1)}, bf16[512,256]{1,0:T(8,128)(2,1)S(1)}, u32[]{:S(2)}, u32[]{:S(2)}) collective-permute-start(bf16[512,256]{1,0:T(8,128)(2,1)S(1)} %slice_bitcast_fusion), channel_id=1, source_target_pairs={{0,16},{8,24},{16,0},{24,8},{32,48},{40,56},{48,32},{56,40},{64,80... | collective-permute-start | bytes 786440 | tf_op jit(solution)/shard_map/ppermute | solution.py:40
  183.2 0.1 add_convert_fusion.5
  183.3 3.9 %collective-permute-start.15 = (bf16[96,256]{1,0:T(8,128)(2,1)S(1)}, bf16[96,256]{1,0:T(8,128)(2,1)S(1)}, u32[]{:S(2)}, u32[]{:S(2)}) collective-permute-start(bf16[96,256]{1,0:T(8,128)(2,1)S(1)} %slice_bitcast_fusion.2), channel_id=1, source_target_pairs={{0,4},{1,5},{2,6},{3,7},{4,0},{5,1},{6,2},{7,3},{8,12},{9,13},{10,... | collective-permute-start | bytes 147464 | tf_op jit(solution)/shard_map/ppermute | solution.py:33
  187.2 1.8 collective-permute-done.20
  189.0 0.8 fusion.1
  189.8 3.3 %collective-permute-done.15 = bf16[96,256]{1,0:T(8,128)(2,1)S(1)} collective-permute-done((bf16[96,256]{1,0:T(8,128)(2,1)S(1)}, bf16[96,256]{1,0:T(8,128)(2,1)S(1)}, u32[]{:S(2)}, u32[]{:S(2)}) %collective-permute-start.15) | collective-permute-done | bytes 49184 | tf_op jit(solution)/shard_map/ppermute | solution.py:33
  193.2 0.6 pad_maximum_fusion.2
  193.8 0.6 pad_maximum_fusion.1
  (26 shorter events, 0.1 us)
Async XLA Ops:
  3.8 8.1 %collective-permute-start = (bf16[512,256]{1,0:T(8,128)(2,1)}, bf16[512,256]{1,0:T(8,128)(2,1)S(1)}, u32[]{:S(2)}, u32[]{:S(2)}) collective-permute-start(bf16[512,256]{1,0:T(8,128)(2,1)} %get-tuple-element.38), channel_id=1, source_target_pairs={{0,16},{8,24},{16,0},{24,8},{32,48},{40,56},{48,32},{56,40},{64,80... | collective-permute-start | bytes 786440 | tf_op jit(solution)/shard_map/ppermute | solution.py:40
  13.4 31.0 %all-to-all-start = ((bf16[4,1024,256]{2,1,0:T(8,128)(2,1)}), bf16[4,1024,256]{2,1,0:T(8,128)(2,1)S(1)}, u32[]{:S(2)}, u32[]{:S(2)}) async-start(bf16[4,1024,256]{2,1,0:T(8,128)(2,1)} %broadcast_in_dim.3), calls=%async_computation | async-start | bytes 4194304 | tf_op jit(solution)/shard_map/all_to_all | solution.py:440
  18.9 19.6 %collective-permute-start.1 = (bf16[96,4096]{1,0:T(8,128)(2,1)}, bf16[96,4096]{1,0:T(8,128)(2,1)S(1)}, u32[]{:S(2)}, u32[]{:S(2)}) collective-permute-start(bf16[96,4096]{1,0:T(8,128)(2,1)} %rest_0_), channel_id=1, source_target_pairs={{0,1},{1,2},{2,3},{3,0},{4,5},{5,6},{6,7},{7,4},{8,9},{9,10},{10,1... | collective-permute-start | bytes 2359304 | tf_op jit(solution)/shard_map/ppermute | solution.py:33
  20.5 18.1 %collective-permute-start.2 = (bf16[96,4096]{1,0:T(8,128)(2,1)}, bf16[96,4096]{1,0:T(8,128)(2,1)S(1)}, u32[]{:S(2)}, u32[]{:S(2)}) collective-permute-start(bf16[96,4096]{1,0:T(8,128)(2,1)} %rest_0_), channel_id=1, source_target_pairs={{0,3},{1,0},{2,1},{3,2},{4,7},{5,4},{6,5},{7,6},{8,11},{9,8},{10,9... | collective-permute-start | bytes 2359304 | tf_op jit(solution)/shard_map/ppermute | solution.py:33
  22.2 19.4 %collective-permute-start.3 = (bf16[96,4096]{1,0:T(8,128)(2,1)}, bf16[96,4096]{1,0:T(8,128)(2,1)}, u32[]{:S(2)}, u32[]{:S(2)}) collective-permute-start(bf16[96,4096]{1,0:T(8,128)(2,1)} %rest_0_), channel_id=1, source_target_pairs={{0,4},{1,5},{2,6},{3,7},{4,0},{5,1},{6,2},{7,3},{8,12},{9,13},{10,... | collective-permute-start | bytes 2359304 | tf_op jit(solution)/shard_map/ppermute | solution.py:33
  38.6 18.8 %copy-start.3 = (bf16[96,4096]{1,0:T(8,128)(2,1)}, bf16[96,4096]{1,0:T(8,128)(2,1)S(1)}, u32[]{:S(2)}) copy-start(bf16[96,4096]{1,0:T(8,128)(2,1)S(1)} %collective-permute-done.1.refs_3_.rest_3_) | copy-start | bytes 2359300
  38.6 0.9 copy-start.4
  44.4 21.7 %copy-start = (bf16[4,1024,256]{2,1,0:T(8,128)(2,1)}, bf16[4,1024,256]{2,1,0:T(8,128)(2,1)S(1)}, u32[]{:S(2)}) copy-start(bf16[4,1024,256]{2,1,0:T(8,128)(2,1)S(1)} %all-to-all-done) | copy-start | bytes 6291460
  44.4 14.1 %collective-permute-start.6 = (bf16[4096,256]{1,0:T(8,128)(2,1)S(1)}, bf16[4096,256]{1,0:T(8,128)(2,1)S(1)}, u32[]{:S(2)}, u32[]{:S(2)}) collective-permute-start(bf16[4096,256]{1,0:T(8,128)(2,1)S(1)} %bitcast.41), channel_id=1, source_target_pairs={{0,8},{8,0},{16,24},{24,16},{32,40},{40,32},{48,56},{56,48},{64,72... | collective-permute-start | bytes 6291464 | tf_op jit(solution)/shard_map/ppermute | solution.py:40
  44.4 12.9 %collective-permute-start.4 = (bf16[48,4096]{1,0:T(8,128)(2,1)S(1)}, bf16[48,4096]{1,0:T(8,128)(2,1)S(1)}, u32[]{:S(2)}, u32[]{:S(2)}) collective-permute-start(bf16[48,4096]{1,0:T(8,128)(2,1)S(1)} %slice.74), channel_id=1, source_target_pairs={{0,1},{1,2},{2,3},{3,0},{4,5},{5,6},{6,7},{7,4},{8,9},{9,10},{10,1... | collective-permute-start | bytes 1179656 | tf_op jit(solution)/shard_map/ppermute | solution.py:33
  47.1 11.3 %collective-permute-start.5 = (bf16[48,4096]{1,0:T(8,128)(2,1)S(1)}, bf16[48,4096]{1,0:T(8,128)(2,1)S(1)}, u32[]{:S(2)}, u32[]{:S(2)}) collective-permute-start(bf16[48,4096]{1,0:T(8,128)(2,1)S(1)} %slice.75), channel_id=1, source_target_pairs={{0,3},{1,0},{2,1},{3,2},{4,7},{5,4},{6,5},{7,6},{8,11},{9,8},{10,9... | collective-permute-start | bytes 1179656 | tf_op jit(solution)/shard_map/ppermute | solution.py:33
  58.5 22.2 %copy-start.2 = (bf16[96,4096]{1,0:T(8,128)(2,1)}, bf16[96,4096]{1,0:T(8,128)(2,1)S(1)}, u32[]{:S(2)}) copy-start(bf16[96,4096]{1,0:T(8,128)(2,1)S(1)} %pad_maximum_fusion.refs_2_.rest_2_) | copy-start | bytes 2359300
  58.5 1.4 copy-start.1
  59.9 20.9 %collective-permute-start.7 = (bf16[96,4096]{1,0:T(8,128)(2,1)}, bf16[96,4096]{1,0:T(8,128)(2,1)}, u32[]{:S(2)}, u32[]{:S(2)}) collective-permute-start(bf16[96,4096]{1,0:T(8,128)(2,1)} %collective-permute-done.3.refs_4_.rest_4_), channel_id=1, source_target_pairs={{0,1},{1,2},{2,3},{3,0},{4,5},{5,6},{6,7},{7,4},{8,9},{9,10},{10,1... | collective-permute-start | bytes 2359304 | tf_op jit(solution)/shard_map/ppermute | solution.py:33
  61.4 19.3 %collective-permute-start.8 = (bf16[96,4096]{1,0:T(8,128)(2,1)}, bf16[96,4096]{1,0:T(8,128)(2,1)}, u32[]{:S(2)}, u32[]{:S(2)}) collective-permute-start(bf16[96,4096]{1,0:T(8,128)(2,1)} %collective-permute-done.3.refs_4_.rest_4_), channel_id=1, source_target_pairs={{0,3},{1,0},{2,1},{3,2},{4,7},{5,4},{6,5},{7,6},{8,11},{9,8},{10,9... | collective-permute-start | bytes 2359304 | tf_op jit(solution)/shard_map/ppermute | solution.py:33
  63.1 19.9 %collective-permute-start.9 = (bf16[96,4096]{1,0:T(8,128)(2,1)S(1)}, bf16[96,4096]{1,0:T(8,128)(2,1)}, u32[]{:S(2)}, u32[]{:S(2)}) collective-permute-start(bf16[96,4096]{1,0:T(8,128)(2,1)S(1)} %pad_maximum_fusion.refs_2_.rest_2_), channel_id=1, source_target_pairs={{0,4},{1,5},{2,6},{3,7},{4,0},{5,1},{6,2},{7,3},{8,12},{9,13},{10,... | collective-permute-start | bytes 2359304 | tf_op jit(solution)/shard_map/ppermute | solution.py:33
  83.0 75.5 %all-to-all-start.1 = ((bf16[8,96,4096]{2,1,0:T(8,128)(2,1)}), bf16[8,96,4096]{2,1,0:T(8,128)(2,1)}, u32[]{:S(2)}, u32[]{:S(2)}) async-start(bf16[8,96,4096]{2,1,0:T(8,128)(2,1)} %bitcast.40), calls=%async_computation.1 | async-start | bytes 12582912 | tf_op jit(solution)/shard_map/all_to_all | solution.py:440
  107.4 10.7 %collective-permute-start.10 = (bf16[4096,256]{1,0:T(8,128)(2,1)}, bf16[4096,256]{1,0:T(8,128)(2,1)}, u32[]{:S(2)}, u32[]{:S(2)}) collective-permute-start(bf16[4096,256]{1,0:T(8,128)(2,1)} %get-tuple-element.55), channel_id=1, source_target_pairs={{0,8},{8,0},{16,24},{24,16},{32,40},{40,32},{48,56},{56,48},{64,72... | collective-permute-start | bytes 6291464 | tf_op jit(solution)/shard_map/ppermute | solution.py:40
  117.7 10.7 %collective-permute-start.16 = (bf16[8,512,256]{2,1,0:T(8,128)(2,1)}, bf16[8,512,256]{2,1,0:T(8,128)(2,1)}, u32[]{:S(2)}, u32[]{:S(2)}) collective-permute-start(bf16[8,512,256]{2,1,0:T(8,128)(2,1)} %get-tuple-element.57), channel_id=1, source_target_pairs={{0,8},{8,0},{16,24},{24,16},{32,40},{40,32},{48,56},{56,48},{64,72... | collective-permute-start | bytes 6291464 | tf_op jit(solution)/shard_map/ppermute | solution.py:40
  121.8 16.5 %collective-permute-start.11 = (bf16[1024,256]{1,0:T(8,128)(2,1)}, bf16[1024,256]{1,0:T(8,128)(2,1)}, u32[]{:S(2)}, u32[]{:S(2)}) collective-permute-start(bf16[1024,256]{1,0:T(8,128)(2,1)} %get-tuple-element.75), channel_id=1, source_target_pairs={{0,32},{8,40},{16,48},{24,56},{32,64},{40,72},{48,80},{56,88},{64,... | collective-permute-start | bytes 1572872 | tf_op jit(solution)/shard_map/ppermute | solution.py:40
  125.7 24.5 %collective-permute-start.12 = (bf16[1024,256]{1,0:T(8,128)(2,1)S(1)}, bf16[1024,256]{1,0:T(8,128)(2,1)}, u32[]{:S(2)}, u32[]{:S(2)}) collective-permute-start(bf16[1024,256]{1,0:T(8,128)(2,1)S(1)} %get-tuple-element.77), channel_id=1, source_target_pairs={{0,64},{8,72},{16,80},{24,88},{32,96},{40,104},{48,112},{56,120},{... | collective-permute-start | bytes 1572872 | tf_op jit(solution)/shard_map/ppermute | solution.py:40
  126.8 23.5 %collective-permute-start.13 = (bf16[1024,256]{1,0:T(8,128)(2,1)S(1)}, bf16[1024,256]{1,0:T(8,128)(2,1)}, u32[]{:S(2)}, u32[]{:S(2)}) collective-permute-start(bf16[1024,256]{1,0:T(8,128)(2,1)S(1)} %get-tuple-element.76), channel_id=1, source_target_pairs={{0,96},{8,104},{16,112},{24,120},{32,0},{40,8},{48,16},{56,24},{64... | collective-permute-start | bytes 1572872 | tf_op jit(solution)/shard_map/ppermute | solution.py:40
  153.0 21.2 %collective-permute-start.17 = (bf16[2,512,256]{2,1,0:T(8,128)(2,1)}, bf16[2,512,256]{2,1,0:T(8,128)(2,1)S(1)}, u32[]{:S(2)}, u32[]{:S(2)}) collective-permute-start(bf16[2,512,256]{2,1,0:T(8,128)(2,1)} %get-tuple-element.74), channel_id=1, source_target_pairs={{0,32},{8,40},{16,48},{24,56},{32,64},{40,72},{48,80},{56,88},{64,... | collective-permute-start | bytes 1572872 | tf_op jit(solution)/shard_map/ppermute | solution.py:40
  154.9 24.7 %collective-permute-start.18 = (bf16[2,512,256]{2,1,0:T(8,128)(2,1)}, bf16[2,512,256]{2,1,0:T(8,128)(2,1)S(1)}, u32[]{:S(2)}, u32[]{:S(2)}) collective-permute-start(bf16[2,512,256]{2,1,0:T(8,128)(2,1)} %get-tuple-element.73), channel_id=1, source_target_pairs={{0,64},{8,72},{16,80},{24,88},{32,96},{40,104},{48,112},{56,120},{... | collective-permute-start | bytes 1572872 | tf_op jit(solution)/shard_map/ppermute | solution.py:40
  156.3 23.3 %collective-permute-start.19 = (bf16[2,512,256]{2,1,0:T(8,128)(2,1)S(1)}, bf16[2,512,256]{2,1,0:T(8,128)(2,1)}, u32[]{:S(2)}, u32[]{:S(2)}) collective-permute-start(bf16[2,512,256]{2,1,0:T(8,128)(2,1)S(1)} %get-tuple-element.72), channel_id=1, source_target_pairs={{0,96},{8,104},{16,112},{24,120},{32,0},{40,8},{48,16},{56,24},{64... | collective-permute-start | bytes 1572872 | tf_op jit(solution)/shard_map/ppermute | solution.py:40
  159.3 7.0 %collective-permute-start.14 = (bf16[512,256]{1,0:T(8,128)(2,1)S(1)}, bf16[512,256]{1,0:T(8,128)(2,1)S(1)}, u32[]{:S(2)}, u32[]{:S(2)}) collective-permute-start(bf16[512,256]{1,0:T(8,128)(2,1)S(1)} %get-tuple-element.78), channel_id=1, source_target_pairs={{0,16},{8,24},{16,0},{24,8},{32,48},{40,56},{48,32},{56,40},{64,80... | collective-permute-start | bytes 786440 | tf_op jit(solution)/shard_map/ppermute | solution.py:40
  166.3 0.7 copy-start.5
  169.8 13.5 %all-to-all-start.2 = ((bf16[4,2,96,256]{3,2,1,0:T(8,128)(2,1)}), bf16[4,2,96,256]{3,2,1,0:T(8,128)(2,1)S(1)}, u32[]{:S(2)}, u32[]{:S(2)}) async-start(bf16[4,2,96,256]{3,2,1,0:T(8,128)(2,1)} %settle.1), calls=%async_computation.2 | async-start | bytes 786432 | tf_op jit(solution)/shard_map/all_to_all | solution.py:440
  180.9 8.1 %collective-permute-start.20 = (bf16[512,256]{1,0:T(8,128)(2,1)S(1)}, bf16[512,256]{1,0:T(8,128)(2,1)S(1)}, u32[]{:S(2)}, u32[]{:S(2)}) collective-permute-start(bf16[512,256]{1,0:T(8,128)(2,1)S(1)} %slice_bitcast_fusion), channel_id=1, source_target_pairs={{0,16},{8,24},{16,0},{24,8},{32,48},{40,56},{48,32},{56,40},{64,80... | collective-permute-start | bytes 786440 | tf_op jit(solution)/shard_map/ppermute | solution.py:40
  183.3 9.8 %collective-permute-start.15 = (bf16[96,256]{1,0:T(8,128)(2,1)S(1)}, bf16[96,256]{1,0:T(8,128)(2,1)S(1)}, u32[]{:S(2)}, u32[]{:S(2)}) collective-permute-start(bf16[96,256]{1,0:T(8,128)(2,1)S(1)} %slice_bitcast_fusion.2), channel_id=1, source_target_pairs={{0,4},{1,5},{2,6},{3,7},{4,0},{5,1},{6,2},{7,3},{8,12},{9,13},{10,... | collective-permute-start | bytes 147464 | tf_op jit(solution)/shard_map/ppermute | solution.py:33

commit v3 on v2

--- a/solution.py
+++ b/solution.py
@@ -15,6 +15,7 @@
 WIN = 128
 ELDER = 512
 TREE = 21
+SEEN = 2 * ELDER + 8 * 2 * WIN
 NEG = -1e30
 SCALE = HD ** (-0.5)
 SCALE2 = SCALE * math.log2(math.e)
@@ -24,6 +25,8 @@
 
 Y_GROUPS = [[0, 1, 2, 3], [4, 5, 6, 7]]
 Z_GROUPS = [[0, 4, 8, 12], [1, 5, 9, 13], [2, 6, 10, 14], [3, 7, 11, 15]]
+DOWN = (((0,), (0,)), ((), ()))
+ANY_SPEC = pl.BlockSpec(memory_space=pl.ANY)
 SMEM_SPEC = pl.BlockSpec(memory_space=pltpu.SMEM)
 VMEM_SPEC = pl.BlockSpec(memory_space=pltpu.VMEM)
 
@@ -87,10 +90,29 @@
     )(place, owner, offset, key_rows, value_rows)
 
 
+def empty_kernel(place, mine_ref, other_ref):
+    del place
+    mine_ref[...] = jnp.zeros_like(mine_ref)
+    other_ref[...] = jnp.zeros_like(other_ref)
+
+
+def empty_elders(place):
+    return pl.pallas_call(
+        empty_kernel,
+        out_shape=[jax.ShapeDtypeStruct((8 * ELDER, 2 * HD), BF16)] * 2,
+        in_specs=[SMEM_SPEC],
+        out_specs=[VMEM_SPEC] * 2,
+        compiler_params=pltpu.CompilerParams(vmem_limit_bytes=VMEM),
+        cost_estimate=pl.CostEstimate(flops=0, bytes_accessed=100_000, transcendentals=0),
+        name="empty_elders",
+    )(place)
+
+
 def relative_leaf(leaf, other):
     core = (leaf + other) % 2
     cross = (leaf // 2 + other // 2) % 2
-    return core * 8 + other // 4 * 2 + cross
+    depth = (other // 4 - leaf // 4 + 4) % 4
+    return core * 8 + depth * 2 + cross
 
 
 def fill_table(table, place, owner, parent, offset, length):
@@ -110,6 +132,7 @@
             branch = jnp.where(level >= 5, parent[i], i)
             prompt_base = first_row(prompt)
             branch_base = first_row(branch)
+            number = branch // TREE * 4 + branch % TREE - 1
             tiles = jnp.where(level == 0, 4, jnp.where(level < 5, 2, 1))
             first = jnp.where(level == 0, 0, jnp.where(level < 5, 4, 6))
             window = offset[i] // WIN
@@ -121,6 +144,8 @@
                     table[window + j, 1] = length[i] - j * WIN
                     table[window + j, 2] = prompt_base
                     table[window + j, 3] = branch_base
+                    table[window + j, 4] = prompt // TREE * ELDER
+                    table[window + j, 5] = 2 * ELDER + number * 2 * WIN
 
         return unused
 
@@ -131,8 +156,8 @@
     return jnp.concatenate([block[:, h * HD : (h + 1) * HD] for h in range(HEADS_DEV)], axis=0)
 
 
-def tile_base(table, w, t):
-    base = table[w, 2] + t * WIN if t < 4 else table[w, 3] + (t - 4) * WIN
+def tile_base(table, w, column, t):
+    base = table[w, column] + t * WIN if t < 4 else table[w, column + 1] + (t - 4) * WIN
     return pl.multiple_of(base, WIN)
 
 
@@ -154,28 +179,49 @@
     lax.fori_loop(0, ROWS // WIN, window, 0)
 
 
-def load_tiles(table, w, rows, tiles, mine_ref, other_ref, own_ref, pair_buf):
+def start_tiles(table, mine_ref, other_ref, pair_buf, sems):
     half = 8 * ELDER
-    for t in range(tiles):
-        base = tile_base(table, w, t)
-        spot = pl.ds(pl.multiple_of(base % half, WIN), WIN)
-        pair_buf[t * WIN : (t + 1) * WIN, :] = jnp.where(
-            base < half, mine_ref[spot, :], other_ref[spot, :]
-        )
-    pair_buf[tiles * WIN : (tiles + 1) * WIN, :] = own_ref[rows, :]
-
-
-def masked(scores, tiles, fill):
-    own = scores[:, tiles * WIN :]
-    col = lax.broadcasted_iota(jnp.int32, own.shape, 1)
-    row = lax.broadcasted_iota(jnp.int32, own.shape, 0) % WIN
-    own = jnp.where(col <= row, own, fill)
-    return jnp.concatenate([scores[:, : tiles * WIN], own], axis=1) if tiles else own
-
-
-def live_rows(table, w):
-    row = lax.broadcasted_iota(jnp.int32, (HEADS_DEV * WIN, 1), 0) % WIN
-    return row < table[w, 1]
+
+    def window(w, unused):
+        for t in range(6):
+            base = tile_base(table, w, 2, t)
+            there = pair_buf.at[w, pl.ds(t * WIN, WIN), :]
+
+            @pl.when((t < table[w, 0]) & (base < half))
+            def _():
+                source = mine_ref.at[pl.ds(base, WIN), :]
+                pltpu.make_async_copy(source, there, sems.at[w]).start()
+
+            @pl.when((t < table[w, 0]) & (base >= half))
+            def _():
+                source = other_ref.at[pl.ds(pl.multiple_of(base - half, WIN), WIN), :]
+                pltpu.make_async_copy(source, there, sems.at[w]).start()
+
+        return unused
+
+    lax.fori_loop(0, ROWS // WIN, window, 0)
+
+
+def wait_tiles(w, rows, tiles, mine_ref, own_ref, pair_buf, sems):
+    span = tiles * WIN
+    if tiles:
+        spot = pair_buf.at[w, pl.ds(0, span), :]
+        pltpu.make_async_copy(mine_ref.at[pl.ds(0, span), :], spot, sems.at[w]).wait()
+    pair_buf[w, span : span + WIN, :] = own_ref[rows, :]
+    return pair_buf[w, : span + WIN, :HD], pair_buf[w, : span + WIN, HD:]
+
+
+def masked(scores, tiles):
+    own = scores[tiles * WIN :, :]
+    key = lax.broadcasted_iota(jnp.int32, own.shape, 0)
+    query = lax.broadcasted_iota(jnp.int32, own.shape, 1) % WIN
+    own = jnp.where(key <= query, own, NEG)
+    return jnp.concatenate([scores[: tiles * WIN, :], own], axis=0) if tiles else own
+
+
+def live_columns(table, w):
+    place = lax.broadcasted_iota(jnp.int32, (1, HEADS_DEV * WIN), 1) % WIN
+    return place < table[w, 1]
 
 
 def scores_of(query, keys):
@@ -184,33 +230,27 @@
 
 def forward_kernel(
     place, owner, parent, offset, length, query_ref, own_ref, elder_mine_ref,
-    elder_other_ref, attn_ref, stat_ref, table, pair_buf,
+    elder_other_ref, attn_ref, stat_ref, table, pair_buf, sems,
 ):
     fill_table(table, place, owner, parent, offset, length)
+    start_tiles(table, elder_mine_ref, elder_other_ref, pair_buf, sems)
 
     def empty(w, rows):
         attn_ref[rows, :] = jnp.zeros((WIN, HEADS_DEV * HD), BF16)
-        stat_ref[rows, :] = jnp.zeros((WIN, HD), F32)
 
     def full(w, rows, tiles):
-        load_tiles(table, w, rows, tiles, elder_mine_ref, elder_other_ref, own_ref, pair_buf)
-        span = (tiles + 1) * WIN
+        keys, values = wait_tiles(w, rows, tiles, elder_mine_ref, own_ref, pair_buf, sems)
         query = heads_down(query_ref[rows, :])
-        scores = masked(scores_of(query, pair_buf[:span, :HD]), tiles, NEG)
-        top = jnp.max(scores, axis=1, keepdims=True)
+        scores = masked(scores_of(keys, query), tiles)
+        top = jnp.max(scores, axis=0, keepdims=True)
         weights = jnp.exp2((scores - top) * SCALE2)
-        total = jnp.sum(weights, axis=1, keepdims=True)
-        live = live_rows(table, w)
-        attn = jnp.dot(weights.astype(BF16), pair_buf[:span, HD:], preferred_element_type=F32)
-        attn = (attn * jnp.where(live, 1.0 / total, 0.0)).astype(BF16)
-        stat = jnp.where(live, top * SCALE2 + jnp.log2(total), -NEG)
-        lane = lax.broadcasted_iota(jnp.int32, (WIN, HD), 1)
-        packed = jnp.zeros((WIN, HD), F32)
+        total = jnp.sum(weights, axis=0, keepdims=True)
+        live = live_columns(table, w)
+        attn = lax.dot_general(values, weights.astype(BF16), DOWN, preferred_element_type=F32)
+        attn = (attn * jnp.where(live, 1.0 / total, 0.0)).astype(BF16).T
+        stat_ref[w, 0:1, :] = jnp.where(live, top * SCALE2 + jnp.log2(total), -NEG)
         for h in range(HEADS_DEV):
-            part = slice(h * WIN, (h + 1) * WIN)
-            attn_ref[rows, h * HD : (h + 1) * HD] = attn[part]
-            packed = jnp.where(lane == h, stat[part], packed)
-        stat_ref[rows, :] = packed
+            attn_ref[rows, h * HD : (h + 1) * HD] = attn[h * WIN : (h + 1) * WIN]
 
     for_windows(table, empty, full)
 
@@ -220,11 +260,15 @@
         forward_kernel,
         out_shape=(
             jax.ShapeDtypeStruct((ROWS, HEADS_DEV * HD), BF16),
-            jax.ShapeDtypeStruct((ROWS, HD), F32),
+            jax.ShapeDtypeStruct((ROWS // WIN, 8, HEADS_DEV * WIN), F32),
         ),
-        in_specs=[SMEM_SPEC] * 5 + [VMEM_SPEC] * 4,
+        in_specs=[SMEM_SPEC] * 5 + [VMEM_SPEC] * 2 + [ANY_SPEC] * 2,
         out_specs=(VMEM_SPEC, VMEM_SPEC),
-        scratch_shapes=[pltpu.SMEM((6, 8), jnp.int32), pltpu.VMEM((7 * WIN, 2 * HD), BF16)],
+        scratch_shapes=[
+            pltpu.SMEM((6, 8), jnp.int32),
+            pltpu.VMEM((6, 7 * WIN, 2 * HD), BF16),
+            pltpu.SemaphoreType.DMA((6,)),
+        ],
         compiler_params=pltpu.CompilerParams(vmem_limit_bytes=VMEM),
         cost_estimate=pl.CostEstimate(flops=0, bytes_accessed=100_000, transcendentals=0),
         name="attention",
@@ -295,42 +339,42 @@
     )(place, out_weight, *pieces)
 
 
-def weight_grad_kernel(place, attn_ref, *rest):
-    pieces, mine_ref, other_ref, turned, rows = rest[:8], *rest[8:]
+def weight_grad_kernel(flip, place, attn_ref, *rest):
+    pieces, out_ref, turned, rows = rest[:8], *rest[8:]
     leaf = place[0]
 
     @pl.when(pl.program_id(0) == 0)
     def _():
         turned[...] = attn_ref[...].T
 
-    for k in range(8):
-        first = pl.multiple_of(relative_head(place[1], k) * 96, 32)
-        rows[pl.ds(first, 96), :] = pieces[k][...]
+    for core in range(2):
+
+        @pl.when((leaf + flip) % 2 == core)
+        def _():
+            for k in range(8):
+                first = pl.multiple_of(relative_head(place[1], k) * 96, 32)
+                for j in range(4):
+                    begin = (j * 2 + core) * 256
+                    rows[pl.ds(first, 96), j * 256 : (j + 1) * 256] = pieces[k][
+                        :, begin : begin + 256
+                    ]
+
     product = jnp.dot(turned[...], rows[...], preferred_element_type=F32).astype(BF16)
     for j in range(4):
-        part = product[:, j * 256 : (j + 1) * 256]
-        cross = (leaf // 2 + j // 2) % 2
-
-        @pl.when(leaf % 2 == j % 2)
-        def _():
-            mine_ref[cross] = part
-
-        @pl.when(leaf % 2 != j % 2)
-        def _():
-            other_ref[cross] = part
-
-
-def weight_grad_of(place, attn, pieces):
+        out_ref[j // 2 * 2 + (leaf // 2 + j) % 2] = product[:, j * 256 : (j + 1) * 256]
+
+
+def weight_grad_of(place, attn, pieces, flip):
     feats, width = HEADS_DEV * HD, pieces[0].shape[1]
-    step = width // 4
-    return pl.pallas_call(
-        weight_grad_kernel,
-        grid=(4,),
+    step = width // 2
+    return pl.pallas_call(
+        functools.partial(weight_grad_kernel, flip),
+        grid=(2,),
         in_specs=[SMEM_SPEC, pl.BlockSpec((ROWS, feats), lambda n: (0, 0))]
         + [pl.BlockSpec((96, step), lambda n: (0, n))] * 8,
-        out_specs=[pl.BlockSpec((2, feats, step // 4), lambda n: (n, 0, 0))] * 2,
-        scratch_shapes=[pltpu.VMEM((feats, ROWS), BF16), pltpu.VMEM((ROWS, step), BF16)],
-        out_shape=[jax.ShapeDtypeStruct((8, feats, step // 4), BF16)] * 2,
+        out_specs=pl.BlockSpec((4, feats, 256), lambda n: (n, 0, 0)),
+        scratch_shapes=[pltpu.VMEM((feats, ROWS), BF16), pltpu.VMEM((ROWS, step // 2), BF16)],
+        out_shape=jax.ShapeDtypeStruct((8, feats, 256), BF16),
         compiler_params=pltpu.CompilerParams(vmem_limit_bytes=VMEM),
         cost_estimate=pl.CostEstimate(flops=0, bytes_accessed=100_000, transcendentals=0),
         name="weight_grad",
@@ -339,10 +383,12 @@
 
 def backward_kernel(
     place, owner, parent, offset, length, query_ref, grad_ref, attn_ref, stat_ref, own_ref,
-    elder_mine_ref, elder_other_ref, query_grad_ref, own_grad_ref, mine_ref, other_ref, table,
-    pair_buf, elder_sum,
+    elder_mine_ref, elder_other_ref, zero_mine_ref, zero_other_ref, query_grad_ref, own_grad_ref,
+    mine_ref, other_ref, table, pair_buf, elder_sum, elder_out, sems, out_sem,
 ):
+    del zero_mine_ref, zero_other_ref
     fill_table(table, place, owner, parent, offset, length)
+    start_tiles(table, elder_mine_ref, elder_other_ref, pair_buf, sems)
     elder_sum[...] = jnp.zeros_like(elder_sum)
 
     def empty(w, rows):
@@ -350,28 +396,22 @@
         own_grad_ref[rows, :] = jnp.zeros((WIN, 2 * HD), F32)
 
     def full(w, rows, tiles):
-        load_tiles(table, w, rows, tiles, elder_mine_ref, elder_other_ref, own_ref, pair_buf)
-        span = (tiles + 1) * WIN
+        keys, values = wait_tiles(w, rows, tiles, elder_mine_ref, own_ref, pair_buf, sems)
         query = heads_down(query_ref[rows, :])
         grad = heads_down(grad_ref[rows, :])
         attn = heads_down(attn_ref[rows, :])
-        packed = stat_ref[rows, :]
-        stat = jnp.concatenate([packed[:, h : h + 1] for h in range(HEADS_DEV)], axis=0)
-        delta = jnp.sum(grad.astype(F32) * attn.astype(F32), axis=1, keepdims=True)
-        keys, values = pair_buf[:span, :HD], pair_buf[:span, HD:]
-        probs = jnp.exp2(masked(scores_of(query, keys) * SCALE2 - stat, tiles, NEG))
-        dprobs = scores_of(grad, values)
+        delta = jnp.sum((grad.astype(F32) * attn.astype(F32)).T, axis=0, keepdims=True)
+        probs = jnp.exp2(masked(scores_of(keys, query) * SCALE2 - stat_ref[w, 0:1, :], tiles))
+        dprobs = scores_of(values, grad)
         dscores = (probs * (dprobs - delta)).astype(BF16)
-        probs = probs.astype(BF16)
-        query_grad = jnp.dot(dscores, keys, preferred_element_type=F32)
-        query_grad = (query_grad * SCALE).astype(BF16)
+        query_grad = lax.dot_general(keys, dscores, DOWN, preferred_element_type=F32)
+        query_grad = (query_grad * SCALE).astype(BF16).T
         for h in range(HEADS_DEV):
             query_grad_ref[rows, h * HD : (h + 1) * HD] = query_grad[h * WIN : (h + 1) * WIN]
-        turn = (((0,), (0,)), ((), ()))
-        key_grad = SCALE * lax.dot_general(dscores, query, turn, preferred_element_type=F32)
-        value_grad = lax.dot_general(probs, grad, turn, preferred_element_type=F32)
+        key_grad = SCALE * jnp.dot(dscores, query, preferred_element_type=F32)
+        value_grad = jnp.dot(probs.astype(BF16), grad, preferred_element_type=F32)
         for t in range(tiles):
-            spot = pl.ds(tile_base(table, w, t), WIN)
+            spot = pl.ds(tile_base(table, w, 4, t), WIN)
             part = slice(t * WIN, (t + 1) * WIN)
             elder_sum[spot, :HD] += key_grad[part]
             elder_sum[spot, HD:] += value_grad[part]
@@ -379,11 +419,31 @@
         own_grad_ref[rows, HD:] = value_grad[tiles * WIN :]
 
     for_windows(table, empty, full)
-    mine_ref[...] = elder_sum[: 8 * ELDER, :].astype(BF16)
-    other_ref[...] = elder_sum[8 * ELDER :, :].astype(BF16)
-
-
-def backward(place, segs, query_rows, grad, attn, stat, own, elders):
+    elder_out[...] = elder_sum[...].astype(BF16)
+    half = 8 * ELDER
+    for tree in range(2):
+        for level in range(5):
+            segment = tree * TREE + level
+            count = ELDER if level == 0 else 2 * WIN
+            first = tree * ELDER if level == 0 else 2 * ELDER + (tree * 4 + level - 1) * 2 * WIN
+            shift = offset[segment] - elder_start(offset[segment])
+            base = relative_leaf(place[0], owner[segment]) * ELDER + shift
+            source = elder_out.at[pl.ds(first, count), :]
+
+            @pl.when(base < half)
+            def _():
+                target = mine_ref.at[pl.ds(pl.multiple_of(base, WIN), count), :]
+                pltpu.make_async_copy(source, target, out_sem).start()
+
+            @pl.when(base >= half)
+            def _():
+                target = other_ref.at[pl.ds(pl.multiple_of(base - half, WIN), count), :]
+                pltpu.make_async_copy(source, target, out_sem).start()
+
+    pltpu.make_async_copy(elder_out, mine_ref.at[pl.ds(0, SEEN), :], out_sem).wait()
+
+
+def backward(place, segs, query_rows, grad, attn, stat, own, elders, zeros):
     return pl.pallas_call(
         backward_kernel,
         out_shape=(
@@ -392,17 +452,21 @@
             jax.ShapeDtypeStruct((8 * ELDER, 2 * HD), BF16),
             jax.ShapeDtypeStruct((8 * ELDER, 2 * HD), BF16),
         ),
-        in_specs=[SMEM_SPEC] * 5 + [VMEM_SPEC] * 7,
-        out_specs=(VMEM_SPEC,) * 4,
+        in_specs=[SMEM_SPEC] * 5 + [VMEM_SPEC] * 5 + [ANY_SPEC] * 4,
+        out_specs=(VMEM_SPEC, VMEM_SPEC, ANY_SPEC, ANY_SPEC),
+        input_output_aliases={12: 2, 13: 3},
         scratch_shapes=[
             pltpu.SMEM((6, 8), jnp.int32),
-            pltpu.VMEM((7 * WIN, 2 * HD), BF16),
-            pltpu.VMEM((16 * ELDER, 2 * HD), F32),
+            pltpu.VMEM((6, 7 * WIN, 2 * HD), BF16),
+            pltpu.VMEM((SEEN, 2 * HD), F32),
+            pltpu.VMEM((SEEN, 2 * HD), BF16),
+            pltpu.SemaphoreType.DMA((6,)),
+            pltpu.SemaphoreType.DMA,
         ],
         compiler_params=pltpu.CompilerParams(vmem_limit_bytes=VMEM),
         cost_estimate=pl.CostEstimate(flops=0, bytes_accessed=100_000, transcendentals=0),
         name="attention_back",
-    )(place, *segs, query_rows, grad, attn, stat, own, *elders)
+    )(place, *segs, query_rows, grad, attn, stat, own, *elders, *zeros)
 
 
 def settle_kernel(place, owner, offset, own_ref, *rest):
@@ -462,44 +526,42 @@
     own, elder = pack(place, seg_owner, seg_offset, key_rows, value_rows)
     pair = jnp.concatenate([elder, leaf_perm(elder, 0, 1, 0)], axis=0)
 
-    rows = after(out_grad, pair)
-    elder_mine = exchange(jnp.broadcast_to(pair, (4, *pair.shape)), "leaf", Z_GROUPS)
-    before = head_perm(rows, 0, 1)
-    behind = head_perm(rows, 0, -1)
-    cross = head_perm(rows, 1, 0)
-    elder_mine, before, behind, cross = lax.optimization_barrier(
-        (elder_mine, before, behind, cross)
-    )
-
-    half = rows.shape[0] // 2
+    before = head_perm(out_grad, 0, 1)
+    behind = head_perm(out_grad, 0, -1)
+    cross = head_perm(out_grad, 1, 0)
+    half = out_grad.shape[0] // 2
     far = jnp.concatenate(
         [head_perm(before[:half], 0, 1), head_perm(behind[half:], 0, -1)], axis=0
     )
-    elder_mine = elder_mine.reshape(8 * ELDER, 2 * HD)
-    elder_other = leaf_perm(elder_mine, 0, 0, 1)
-    far, elder_other, cross = lax.optimization_barrier((far, elder_other, cross))
-
     cross_before = head_perm(cross, 0, 1)
     cross_behind = head_perm(cross, 0, -1)
+    zeros = empty_elders(after(place, pair))
+    elder_mine = jnp.concatenate(
+        [pair, *[leaf_perm(pair, -d, 0, 0) for d in range(1, 4)]], axis=0
+    )
+    elder_mine, far, cross_before, cross_behind, *zeros = lax.optimization_barrier(
+        (elder_mine, far, cross_before, cross_behind, *zeros)
+    )
+    elder_other = leaf_perm(elder_mine, 0, 0, 1)
     cross_far = head_perm(far, 1, 0)
     elders = (elder_mine, elder_other)
     attn, stat = forward(place, segs, query_rows, own, elders)
     partial = project(attn, out_weight)
-    partial, cross_before, cross_behind, cross_far = lax.optimization_barrier(
-        (partial, cross_before, cross_behind, cross_far)
-    )
-
-    pieces = [rows, behind, far, before, cross, cross_behind, cross_far, cross_before]
+    partial, cross_far = lax.optimization_barrier((partial, cross_far))
+
+    pieces = [out_grad, behind, far, before, cross, cross_behind, cross_far, cross_before]
     layer_parts = exchange(partial.reshape(8, 96, -1), "head")
     attn_grad = attn_grad_of(place, after(out_weight, partial), pieces)
     query_grads, own_grad, mine_pair, other_pair = backward(
-        place, segs, query_rows, attn_grad, attn, stat, own, elders
+        place, segs, query_rows, attn_grad, attn, stat, own, elders, zeros
     )
     pair_recv = leaf_perm(other_pair, 0, 0, 1)
-    mine_weight, other_weight = weight_grad_of(place, after(attn, other_pair), pieces)
+    other_weight = weight_grad_of(place, after(attn, other_pair), pieces, 1)
     weight_recv = leaf_perm(other_weight, 0, 0, 1)
     pair_joined = add(after(mine_pair, other_weight), pair_recv)
-    pair_parts = spread_depth(pair_joined.reshape(4, 2 * ELDER, 2 * HD))
+    pair_blocks = pair_joined.reshape(4, 2 * ELDER, 2 * HD)
+    pair_parts = [pair_blocks[0], *[leaf_perm(pair_blocks[d], d, 0, 0) for d in range(1, 4)]]
+    mine_weight = weight_grad_of(place, after(attn, pair_joined), pieces, 0)
     weight_joined = add(mine_weight, weight_recv)
     weight_joined = after(weight_joined, *pair_parts)
     weight_parts = spread_depth(weight_joined.reshape(4, 2, *weight_joined.shape[1:]))

time: 196 us -> 190 us (0.969)
  waiting for transfers between devices: 66.9 us -> 58.5 us
  starting transfers between devices: 53.6 us -> 47.1 us
  local copies, waits for them, and re-layouts: 9.33 us -> 13.9 us
  Pallas kernels: 47.9 us -> 51.8 us
    ppermute x9, waiting for transfers between devices: 30.4 us -> 16.5 us  [head_perm(): return lax.ppermute(array, 'head', pairs)]
    all_to_all x3 -> x2, waiting for transfers between devices: 2.78 us -> 9.99 us  [exchange(): return lax.all_to_all(blocks, axis, 0, 0, axis_index_groups=groups)]
    all_to_all x3 -> x2, starting transfers between devices: 15.4 us -> 9.22 us  [exchange(): return lax.all_to_all(blocks, axis, 0, 0, axis_index_groups=groups)]
    pallas_call x1 -> x3, Pallas kernels: 8.97 us -> 15.1 us  [the longest x2 12.4 us: weight_grad_of(): pl.pallas_call(functools.partial(weight_grad_kernel, flip), grid=(2,), in...]
    ppermute x9, starting transfers between devices: 20.1 us -> 16.8 us  [head_perm(): return lax.ppermute(array, 'head', pairs)]
    unnamed x13 -> x27, local copies, waits for them, and re-layouts: 3.98 us -> 7.25 us
    ppermute x12 -> x15, starting transfers between devices: 18.1 us -> 21.1 us  [leaf_perm(): return lax.ppermute(array, 'leaf', pairs)]
    ppermute x12 -> x15, waiting for transfers between devices: 33.8 us -> 32.1 us  [leaf_perm(): return lax.ppermute(array, 'leaf', pairs)]
  transfers between devices with their start and end apart: 24 -> 26, of which waited for: 13 -> 17; matrix products, arithmetic and copies ran while one was open for 10% -> 14% of each run, Pallas kernels for 23% -> 27%
where the time goes in v3:
time: 190 us; the launch traced here: 189 us
  waiting for transfers between devices  58.5 us (31%)
  Pallas kernels  51.8 us (27%)
  starting transfers between devices  47.1 us (25%)
  other arithmetic  17.1 us (9%)
  local copies, waits for them, and re-layouts  13.9 us (7%)
    ppermute x15, waiting for transfers between devices, leaf_perm(): return lax.ppermute(array, 'leaf', pairs)  32.1 us
    ppermute x15, starting transfers between devices, leaf_perm(): return lax.ppermute(array, 'leaf', pairs)  21.1 us
    ppermute x9, starting transfers between devices, head_perm(): return lax.ppermute(array, 'head', pairs)  16.8 us
    ppermute x9, waiting for transfers between devices, head_perm(): return lax.ppermute(array, 'head', pairs)  16.5 us
    convert_element_type x6, other arithmetic, add(): return total.astype(BF16)  14 us
    pallas_call x2, Pallas kernels, weight_grad_of(): pl.pallas_call(functools.partial(weight_grad_kernel, flip), grid=(2,), in...  12.4 us
    all_to_all x2, waiting for transfers between devices, exchange(): return lax.all_to_all(blocks, axis, 0, 0, axis_index_groups=groups)  9.99 us
    all_to_all x2, starting transfers between devices, exchange(): return lax.all_to_all(blocks, axis, 0, 0, axis_index_groups=groups)  9.22 us
  transfers between devices with their start and end apart: 26, of which 17 were waited for; matrix products, arithmetic and copies ran while one was open for 14% of the time, Pallas kernels for 27%

profile of v3, /device:TPU:0, one launch (start us, length us, event | category | flops | bytes accessed | tf_op | source)
XLA Modules:
  0.0 189.3 jit_solution(16594782986802902371)
XLA Ops:
  0.6 1.7 collective-permute-start.4
  2.4 0.6 pad_add_fusion.place
  3.0 2.6 %pack_keys.1 = (bf16[768,256]{1,0:T(8,128)(2,1)}, bf16[512,256]{1,0:T(8,128)(2,1)}) custom-call(s32[2]{0:T(128)} %pad_add_fusion.place, s32[42]{0:T(128)} %owner.7, s32[42]{0:T(128)} %offset.7, bf16[768,256]{1,0:T(8,128)(2,1)} %key_ref.1, bf16[768,256]{1,0:T(8,128)(2,1)} %value_ref.1), custom_call_target="tpu_custom_call" | custom-call | bytes 100000 | tf_op jit(solution)/shard_map/pack_keys/pallas_call | solution.py:79
  5.6 1.5 collective-permute-start
  7.1 1.7 collective-permute-start.6
  8.7 2.7 %collective-permute-start.8 = (bf16[96,4096]{1,0:T(8,128)(2,1)}, bf16[96,4096]{1,0:T(8,128)(2,1)S(1)}, u32[]{:S(2)}, u32[]{:S(2)}) collective-permute-start(bf16[96,4096]{1,0:T(8,128)(2,1)} %rest_0_.3), channel_id=1, source_target_pairs={{0,4},{1,5},{2,6},{3,7},{4,0},{5,1},{6,2},{7,3},{8,12},{9,13},{10,... | collective-permute-start | bytes 2359304 | tf_op jit(solution)/shard_map/ppermute | solution.py:36
  11.5 1.8 constant_dynamic-update-slice_fusion.1
  13.3 1.8 collective-permute-done
  15.0 0.8 constant_dynamic-update-slice_fusion
  15.8 4.0 %collective-permute-start.1 = (bf16[1024,256]{1,0:T(8,128)(2,1)}, bf16[1024,256]{1,0:T(8,128)(2,1)S(1)}, u32[]{:S(2)}, u32[]{:S(2)}) collective-permute-start(bf16[1024,256]{1,0:T(8,128)(2,1)} %get-tuple-element.74), channel_id=1, source_target_pairs={{0,96},{8,104},{16,112},{24,120},{32,0},{40,8},{48,16},{56,24},{64... | collective-permute-start | bytes 1572872 | tf_op jit(solution)/shard_map/ppermute | solution.py:43
  19.9 1.7 collective-permute-done.4.refs_3_.rest_3_
  21.6 1.9 %collective-permute-start.3 = (bf16[1024,256]{1,0:T(8,128)(2,1)}, bf16[1024,256]{1,0:T(8,128)(2,1)}, u32[]{:S(2)}, u32[]{:S(2)}) collective-permute-start(bf16[1024,256]{1,0:T(8,128)(2,1)} %get-tuple-element.74), channel_id=1, source_target_pairs={{0,32},{8,40},{16,48},{24,56},{32,64},{40,72},{48,80},{56,88},{64,... | collective-permute-start | bytes 1572872 | tf_op jit(solution)/shard_map/ppermute | solution.py:43
  23.5 2.5 %collective-permute-done.6.refs_1_.rest_1_ = bf16[96,4096]{1,0:T(8,128)(2,1)S(1)} collective-permute-done((bf16[96,4096]{1,0:T(8,128)(2,1)}, bf16[96,4096]{1,0:T(8,128)(2,1)S(1)}, u32[]{:S(2)}, u32[]{:S(2)}) %collective-permute-start.6) | collective-permute-done | bytes 786464 | tf_op jit(solution)/shard_map/ppermute | solution.py:36
  26.0 1.6 collective-permute-start.5
  27.6 0.8 slice.119
  28.4 11.6 %collective-permute-done.1 = bf16[1024,256]{1,0:T(8,128)(2,1)S(1)} collective-permute-done((bf16[1024,256]{1,0:T(8,128)(2,1)}, bf16[1024,256]{1,0:T(8,128)(2,1)S(1)}, u32[]{:S(2)}, u32[]{:S(2)}) %collective-permute-start.1) | collective-permute-done | bytes 524320 | tf_op jit(solution)/shard_map/ppermute | solution.py:43
  40.0 1.8 collective-permute-start.7
  41.8 2.7 %empty_elders.1 = (bf16[4096,256]{1,0:T(8,128)(2,1)}, bf16[4096,256]{1,0:T(8,128)(2,1)}) custom-call(s32[2]{0:T(128)} %pad_add_fusion.place), custom_call_target="tpu_custom_call" | custom-call | bytes 100000 | tf_op jit(solution)/shard_map/empty_elders/pallas_call | solution.py:100
  44.5 1.6 collective-permute-start.10
  46.5 0.8 constant_dynamic-update-slice_fusion.4
  47.4 0.8 constant_dynamic-update-slice_fusion.3
  48.2 1.9 constant_dynamic-update-slice_fusion.2.elder_mine_ref
  50.1 1.2 pad_maximum_fusion.refs_2_.rest_2_
  51.3 5.2 %collective-permute-done.10.refs_5_.rest_5_ = bf16[96,4096]{1,0:T(8,128)(2,1)S(1)} collective-permute-done((bf16[96,4096]{1,0:T(8,128)(2,1)S(1)}, bf16[96,4096]{1,0:T(8,128)(2,1)S(1)}, u32[]{:S(2)}, u32[]{:S(2)}) %collective-permute-start.10) | collective-permute-done | bytes 786464 | tf_op jit(solution)/shard_map/ppermute | solution.py:36
  56.5 2.8 %collective-permute-done.9.refs_7_.rest_7_ = bf16[96,4096]{1,0:T(8,128)(2,1)S(1)} collective-permute-done((bf16[96,4096]{1,0:T(8,128)(2,1)S(1)}, bf16[96,4096]{1,0:T(8,128)(2,1)S(1)}, u32[]{:S(2)}, u32[]{:S(2)}) %collective-permute-start.9) | collective-permute-done | bytes 786464 | tf_op jit(solution)/shard_map/ppermute | solution.py:36
  59.4 3.0 %collective-permute-start.12 = (bf16[96,4096]{1,0:T(8,128)(2,1)S(1)}, bf16[96,4096]{1,0:T(8,128)(2,1)S(1)}, u32[]{:S(2)}, u32[]{:S(2)}) collective-permute-start(bf16[96,4096]{1,0:T(8,128)(2,1)S(1)} %pad_maximum_fusion.refs_2_.rest_2_), channel_id=1, source_target_pairs={{0,4},{1,5},{2,6},{3,7},{4,0},{5,1},{6,2},{7,3},{8,12},{9,13},{10,... | collective-permute-start | bytes 2359304 | tf_op jit(solution)/shard_map/ppermute | solution.py:36
  62.4 1.3 collective-permute-done.11.elder_other_ref
  63.7 1.3 copy-done.3
  65.1 6.5 %attention.1 = (bf16[768,512]{1,0:T(8,128)(2,1)}, f32[6,8,512]{2,1,0:T(8,128)}) custom-call(s32[2]{0:T(128)} %pad_add_fusion.place, s32[42]{0:T(128)} %owner.7, s32[42]{0:T(128)} %parent.3, s32[42]{0:T(128)} %offset.7, s32[42]{0:T(128)} %length.3, bf16[768,512]{1,0:T(8,128)(2,1)} %query_ref.3, bf16[768,256]{1,0:T(8,128)(2,1)} %get-tuple-element.35.own_ref, ...), custom_call_target="tpu_custom_call" | custom-call | bytes 100000 | tf_op jit(solution)/shard_map/attention/pallas_call | solution.py:259
  71.6 7.5 %project.1 = bf16[768,4096]{1,0:T(8,128)(2,1)} custom-call(bf16[768,512]{1,0:T(8,128)(2,1)} %get-tuple-element.59.attn_ref, bf16[512,4096]{1,0:T(8,128)(2,1)} %weight_ref.2), custom_call_target="tpu_custom_call" | custom-call | bytes 100000 | tf_op jit(solution)/shard_map/project/pallas_call | solution.py:289
  79.1 1.7 collective-permute-done.12.refs_6_.rest_6_
  80.8 0.9 copy-done.7
  81.8 4.9 %all-to-all-start = ((bf16[8,96,4096]{2,1,0:T(8,128)(2,1)}), bf16[8,96,4096]{2,1,0:T(8,128)(2,1)}, u32[]{:S(2)}, u32[]{:S(2)}) async-start(bf16[8,96,4096]{2,1,0:T(8,128)(2,1)} %bitcast.29), calls=%async_computation | async-start | bytes 12582912 | tf_op jit(solution)/shard_map/all_to_all | solution.py:504
  86.7 8.3 %attn_grad.1.grad_ref = bf16[768,512]{1,0:T(8,128)(2,1)} custom-call(s32[2]{0:T(128)} %pad_add_fusion.place, bf16[512,4096]{1,0:T(8,128)(2,1)} %weight_ref.2, bf16[96,4096]{1,0:T(8,128)(2,1)} %rest_0_.3, bf16[96,4096]{1,0:T(8,128)(2,1)} %copy-done.2, bf16[96,4096]{1,0:T(8,128)(2,1)} %copy-done, bf16[96,4096]{1,0:T(8,128)(2,1)} %copy-done.1, ...), custom_call_target="tpu_custom_call" | custom-call | bytes 100000 | tf_op jit(solution)/shard_map/attn_grad/pallas_call | solution.py:328
  95.0 9.1 %attention_back.1 = (bf16[768,512]{1,0:T(8,128)(2,1)}, f32[768,256]{1,0:T(8,128)}, bf16[4096,256]{1,0:T(8,128)(2,1)}, bf16[4096,256]{1,0:T(8,128)(2,1)}) custom-call(s32[2]{0:T(128)} %pad_add_fusion.place, s32[42]{0:T(128)} %owner.7, s32[42]{0:T(128)} %parent.3, s32[42]{0:T(128)} %offset.7, ...), custom_call_target="tpu_custom_call", output_to_operand_aliasing={{2}: (12, {}), {3}: (13, {})} | custom-call | bytes 100000 | tf_op jit(solution)/shard_map/attention_back/pallas_call | solution.py:447
  104.0 2.8 %collective-permute-start.13 = (bf16[4096,256]{1,0:T(8,128)(2,1)}, bf16[4096,256]{1,0:T(8,128)(2,1)}, u32[]{:S(2)}, u32[]{:S(2)}) collective-permute-start(bf16[4096,256]{1,0:T(8,128)(2,1)} %get-tuple-element.52), channel_id=1, source_target_pairs={{0,8},{8,0},{16,24},{24,16},{32,40},{40,32},{48,56},{56,48},{64,72... | collective-permute-start | bytes 6291464 | tf_op jit(solution)/shard_map/ppermute | solution.py:43
  106.8 6.2 %weight_grad.2 = bf16[8,512,256]{2,1,0:T(8,128)(2,1)} custom-call(s32[2]{0:T(128)} %pad_add_fusion.place, bf16[768,512]{1,0:T(8,128)(2,1)} %get-tuple-element.59.attn_ref, bf16[96,4096]{1,0:T(8,128)(2,1)} %rest_0_.3, bf16[96,4096]{1,0:T(8,128)(2,1)} %copy-done.2, bf16[96,4096]{1,0:T(8,128)(2,1)} %copy-done, bf16[96,4096]{1,0:T(8,128)(2,1)} %copy-done.1, ...), custom_call_target="tpu_custom_call" | custom-call | bytes 100000 | tf_op jit(solution)/shard_map/weight_grad/pallas_call | solution.py:370
  113.0 2.8 %add_convert_fusion.1 = bf16[4096,256]{1,0:T(8,128)(2,1)S(1)} fusion(bf16[4096,256]{1,0:T(8,128)(2,1)} %collective-permute-done.13, bf16[4096,256]{1,0:T(8,128)(2,1)} %get-tuple-element.54), kind=kLoop, calls=%fused_computation.1 | loop fusion | flops 4194304 | bytes 6291456 | tf_op jit(solution)/shard_map/convert_element_type | solution.py:54
  115.8 1.2 fusion.2
  117.0 6.5 %collective-permute-start.15 = (bf16[1024,256]{1,0:T(8,128)(2,1)}, bf16[1024,256]{1,0:T(8,128)(2,1)S(1)}, u32[]{:S(2)}, u32[]{:S(2)}) collective-permute-start(bf16[1024,256]{1,0:T(8,128)(2,1)} %get-tuple-element.71), channel_id=1, source_target_pairs={{0,64},{8,72},{16,80},{24,88},{32,96},{40,104},{48,112},{56,120},{... | collective-permute-start | bytes 1572872 | tf_op jit(solution)/shard_map/ppermute | solution.py:43
  123.5 6.2 %weight_grad.3 = bf16[8,512,256]{2,1,0:T(8,128)(2,1)} custom-call(s32[2]{0:T(128)} %pad_add_fusion.place, bf16[768,512]{1,0:T(8,128)(2,1)} %get-tuple-element.59.attn_ref, bf16[96,4096]{1,0:T(8,128)(2,1)} %rest_0_.3, bf16[96,4096]{1,0:T(8,128)(2,1)} %copy-done.2, bf16[96,4096]{1,0:T(8,128)(2,1)} %copy-done, bf16[96,4096]{1,0:T(8,128)(2,1)} %copy-done.1, ...), custom_call_target="tpu_custom_call" | custom-call | bytes 100000 | tf_op jit(solution)/shard_map/weight_grad/pallas_call | solution.py:370
  129.7 2.7 %add_convert_fusion = bf16[8,512,256]{2,1,0:T(8,128)(2,1)S(1)} fusion(bf16[8,512,256]{2,1,0:T(8,128)(2,1)} %collective-permute-done.19, bf16[8,512,256]{2,1,0:T(8,128)(2,1)} %weight_grad.3), kind=kLoop, calls=%fused_computation | loop fusion | flops 4194304 | bytes 6291456 | tf_op jit(solution)/shard_map/convert_element_type | solution.py:54
  132.4 2.0 %collective-permute-done.14 = bf16[1024,256]{1,0:T(8,128)(2,1)S(1)} collective-permute-done((bf16[1024,256]{1,0:T(8,128)(2,1)}, bf16[1024,256]{1,0:T(8,128)(2,1)S(1)}, u32[]{:S(2)}, u32[]{:S(2)}) %collective-permute-start.14) | collective-permute-done | bytes 524320 | tf_op jit(solution)/shard_map/ppermute | solution.py:43
  134.5 12.4 %collective-permute-done.15 = bf16[1024,256]{1,0:T(8,128)(2,1)S(1)} collective-permute-done((bf16[1024,256]{1,0:T(8,128)(2,1)}, bf16[1024,256]{1,0:T(8,128)(2,1)S(1)}, u32[]{:S(2)}, u32[]{:S(2)}) %collective-permute-start.15) | collective-permute-done | bytes 524320 | tf_op jit(solution)/shard_map/ppermute | solution.py:43
  146.9 0.8 copy-done.9
  147.7 1.2 dynamic-slice_bitcast_fusion.3
  148.9 2.8 %collective-permute-start.21 = (bf16[2,512,256]{2,1,0:T(8,128)(2,1)}, bf16[2,512,256]{2,1,0:T(8,128)(2,1)}, u32[]{:S(2)}, u32[]{:S(2)}) collective-permute-start(bf16[2,512,256]{2,1,0:T(8,128)(2,1)} %get-tuple-element.67), channel_id=1, source_target_pairs={{0,64},{8,72},{16,80},{24,88},{32,96},{40,104},{48,112},{56,120},{... | collective-permute-start | bytes 1572872 | tf_op jit(solution)/shard_map/ppermute | solution.py:43
  152.1 1.5 add_convert_fusion.4
  153.6 5.1 %all-to-all-done = bf16[8,96,4096]{2,1,0:T(8,128)(2,1)} async-done(((bf16[8,96,4096]{2,1,0:T(8,128)(2,1)}), bf16[8,96,4096]{2,1,0:T(8,128)(2,1)}, u32[]{:S(2)}, u32[]{:S(2)}) %all-to-all-start) | async-done | bytes 6291488 | tf_op jit(solution)/shard_map/all_to_all | solution.py:504
  158.7 0.7 fusion.3
  159.4 0.9 collective-permute-start.17
  160.3 4.7 %fusion = bf16[96,4096]{1,0:T(8,128)(2,1)} fusion(bf16[8,96,4096]{2,1,0:T(8,128)(2,1)} %all-to-all-done), kind=kLoop, calls=%fused_computation.5 | loop fusion | flops 6291456 | bytes 7077888 | tf_op jit(solution)/shard_map/convert_element_type | solution.py:54
  164.9 2.2 %collective-permute-done.17.rest_1_ = bf16[512,256]{1,0:T(8,128)(2,1)S(1)} collective-permute-done((bf16[512,256]{1,0:T(8,128)(2,1)S(1)}, bf16[512,256]{1,0:T(8,128)(2,1)S(1)}, u32[]{:S(2)}, u32[]{:S(2)}) %collective-permute-start.17) | collective-permute-done | bytes 262176 | tf_op jit(solution)/shard_map/ppermute | solution.py:43
  167.1 0.7 copy-done.11
  167.8 2.8 %settle.1 = bf16[4,2,96,256]{3,2,1,0:T(8,128)(2,1)} custom-call(s32[2]{0:T(128)} %pad_add_fusion.place, s32[42]{0:T(128)} %owner.7, s32[42]{0:T(128)} %offset.7, f32[768,256]{1,0:T(8,128)} %get-tuple-element.57.own_ref, bf16[512,256]{1,0:T(8,128)(2,1)} %get-tuple-element.73.rest_0_, bf16[512,256]{1,0:T(8,128)(2,1)} %copy-done.11), custom_call_target="tpu_custom_call" | custom-call | bytes 100000 | tf_op jit(solution)/shard_map/settle/pallas_call | solution.py:491
  170.6 4.3 %all-to-all-start.1 = ((bf16[4,2,96,256]{3,2,1,0:T(8,128)(2,1)}), bf16[4,2,96,256]{3,2,1,0:T(8,128)(2,1)S(1)}, u32[]{:S(2)}, u32[]{:S(2)}) async-start(bf16[4,2,96,256]{3,2,1,0:T(8,128)(2,1)} %settle.1), calls=%async_computation.1 | async-start | bytes 786432 | tf_op jit(solution)/shard_map/all_to_all | solution.py:504
  175.1 0.4 collective-permute-done.22
  175.5 1.6 add_convert_fusion.3
  177.4 4.9 %all-to-all-done.1 = bf16[4,2,96,256]{3,2,1,0:T(8,128)(2,1)S(1)} async-done(((bf16[4,2,96,256]{3,2,1,0:T(8,128)(2,1)}), bf16[4,2,96,256]{3,2,1,0:T(8,128)(2,1)S(1)}, u32[]{:S(2)}, u32[]{:S(2)}) %all-to-all-start.1) | async-done | bytes 393248 | tf_op jit(solution)/shard_map/all_to_all | solution.py:504
  182.4 2.2 %collective-permute-start.18 = (bf16[96,256]{1,0:T(8,128)(2,1)S(1)}, bf16[96,256]{1,0:T(8,128)(2,1)S(1)}, u32[]{:S(2)}, u32[]{:S(2)}) collective-permute-start(bf16[96,256]{1,0:T(8,128)(2,1)S(1)} %slice_bitcast_fusion.2), channel_id=1, source_target_pairs={{0,4},{1,5},{2,6},{3,7},{4,0},{5,1},{6,2},{7,3},{8,12},{9,13},{10,... | collective-permute-start | bytes 147464 | tf_op jit(solution)/shard_map/ppermute | solution.py:36
  184.8 0.8 fusion.1
  185.5 2.5 %collective-permute-done.18 = bf16[96,256]{1,0:T(8,128)(2,1)S(1)} collective-permute-done((bf16[96,256]{1,0:T(8,128)(2,1)S(1)}, bf16[96,256]{1,0:T(8,128)(2,1)S(1)}, u32[]{:S(2)}, u32[]{:S(2)}) %collective-permute-start.18) | collective-permute-done | bytes 49184 | tf_op jit(solution)/shard_map/ppermute | solution.py:36
  188.1 0.6 pad_maximum_fusion.2
  188.7 0.6 pad_maximum_fusion.1
  (46 shorter events, 1.6 us)
Async XLA Ops:
  0.6 20.9 %collective-permute-start.4 = (bf16[96,4096]{1,0:T(8,128)(2,1)}, bf16[96,4096]{1,0:T(8,128)(2,1)S(1)}, u32[]{:S(2)}, u32[]{:S(2)}) collective-permute-start(bf16[96,4096]{1,0:T(8,128)(2,1)} %rest_0_.3), channel_id=1, source_target_pairs={{0,1},{1,2},{2,3},{3,0},{4,5},{5,6},{6,7},{7,4},{8,9},{9,10},{10,1... | collective-permute-start | bytes 2359304 | tf_op jit(solution)/shard_map/ppermute | solution.py:36
  5.6 9.4 %collective-permute-start = (bf16[512,256]{1,0:T(8,128)(2,1)}, bf16[512,256]{1,0:T(8,128)(2,1)S(1)}, u32[]{:S(2)}, u32[]{:S(2)}) collective-permute-start(bf16[512,256]{1,0:T(8,128)(2,1)} %get-tuple-element.36), channel_id=1, source_target_pairs={{0,16},{8,24},{16,0},{24,8},{32,48},{40,56},{48,32},{56,40},{64,80... | collective-permute-start | bytes 786440 | tf_op jit(solution)/shard_map/ppermute | solution.py:43
  7.1 18.9 %collective-permute-start.6 = (bf16[96,4096]{1,0:T(8,128)(2,1)}, bf16[96,4096]{1,0:T(8,128)(2,1)S(1)}, u32[]{:S(2)}, u32[]{:S(2)}) collective-permute-start(bf16[96,4096]{1,0:T(8,128)(2,1)} %rest_0_.3), channel_id=1, source_target_pairs={{0,3},{1,0},{2,1},{3,2},{4,7},{5,4},{6,5},{7,6},{8,11},{9,8},{10,9... | collective-permute-start | bytes 2359304 | tf_op jit(solution)/shard_map/ppermute | solution.py:36
  8.7 35.8 %collective-permute-start.8 = (bf16[96,4096]{1,0:T(8,128)(2,1)}, bf16[96,4096]{1,0:T(8,128)(2,1)S(1)}, u32[]{:S(2)}, u32[]{:S(2)}) collective-permute-start(bf16[96,4096]{1,0:T(8,128)(2,1)} %rest_0_.3), channel_id=1, source_target_pairs={{0,4},{1,5},{2,6},{3,7},{4,0},{5,1},{6,2},{7,3},{8,12},{9,13},{10,... | collective-permute-start | bytes 2359304 | tf_op jit(solution)/shard_map/ppermute | solution.py:36
  15.8 24.1 %collective-permute-start.1 = (bf16[1024,256]{1,0:T(8,128)(2,1)}, bf16[1024,256]{1,0:T(8,128)(2,1)S(1)}, u32[]{:S(2)}, u32[]{:S(2)}) collective-permute-start(bf16[1024,256]{1,0:T(8,128)(2,1)} %get-tuple-element.74), channel_id=1, source_target_pairs={{0,96},{8,104},{16,112},{24,120},{32,0},{40,8},{48,16},{56,24},{64... | collective-permute-start | bytes 1572872 | tf_op jit(solution)/shard_map/ppermute | solution.py:43
  19.9 26.3 %collective-permute-start.2 = (bf16[1024,256]{1,0:T(8,128)(2,1)}, bf16[1024,256]{1,0:T(8,128)(2,1)S(1)}, u32[]{:S(2)}, u32[]{:S(2)}) collective-permute-start(bf16[1024,256]{1,0:T(8,128)(2,1)} %get-tuple-element.74), channel_id=1, source_target_pairs={{0,64},{8,72},{16,80},{24,88},{32,96},{40,104},{48,112},{56,120},{... | collective-permute-start | bytes 1572872 | tf_op jit(solution)/shard_map/ppermute | solution.py:43
  21.6 28.5 %copy-start.1 = (bf16[96,4096]{1,0:T(8,128)(2,1)}, bf16[96,4096]{1,0:T(8,128)(2,1)S(1)}, u32[]{:S(2)}) copy-start(bf16[96,4096]{1,0:T(8,128)(2,1)S(1)} %collective-permute-done.4.refs_3_.rest_3_) | copy-start | bytes 2359300
  21.6 26.7 %collective-permute-start.3 = (bf16[1024,256]{1,0:T(8,128)(2,1)}, bf16[1024,256]{1,0:T(8,128)(2,1)}, u32[]{:S(2)}, u32[]{:S(2)}) collective-permute-start(bf16[1024,256]{1,0:T(8,128)(2,1)} %get-tuple-element.74), channel_id=1, source_target_pairs={{0,32},{8,40},{16,48},{24,56},{32,64},{40,72},{48,80},{56,88},{64,... | collective-permute-start | bytes 1572872 | tf_op jit(solution)/shard_map/ppermute | solution.py:43
  26.0 25.3 %copy-start.2 = (bf16[96,4096]{1,0:T(8,128)(2,1)}, bf16[96,4096]{1,0:T(8,128)(2,1)S(1)}, u32[]{:S(2)}) copy-start(bf16[96,4096]{1,0:T(8,128)(2,1)S(1)} %collective-permute-done.6.refs_1_.rest_1_) | copy-start | bytes 2359300
  26.0 24.1 %collective-permute-start.5 = (bf16[48,4096]{1,0:T(8,128)(2,1)S(1)}, bf16[48,4096]{1,0:T(8,128)(2,1)}, u32[]{:S(2)}, u32[]{:S(2)}) collective-permute-start(bf16[48,4096]{1,0:T(8,128)(2,1)S(1)} %slice.118), channel_id=1, source_target_pairs={{0,1},{1,2},{2,3},{3,0},{4,5},{5,6},{6,7},{7,4},{8,9},{9,10},{10,1... | collective-permute-start | bytes 1179656 | tf_op jit(solution)/shard_map/ppermute | solution.py:36
  40.0 10.1 %collective-permute-start.7 = (bf16[48,4096]{1,0:T(8,128)(2,1)}, bf16[48,4096]{1,0:T(8,128)(2,1)}, u32[]{:S(2)}, u32[]{:S(2)}) collective-permute-start(bf16[48,4096]{1,0:T(8,128)(2,1)} %slice.119), channel_id=1, source_target_pairs={{0,3},{1,0},{2,1},{3,2},{4,7},{5,4},{6,5},{7,6},{8,11},{9,8},{10,9... | collective-permute-start | bytes 1179656 | tf_op jit(solution)/shard_map/ppermute | solution.py:36
  44.5 6.8 %copy-start.4 = (bf16[96,4096]{1,0:T(8,128)(2,1)}, bf16[96,4096]{1,0:T(8,128)(2,1)S(1)}, u32[]{:S(2)}) copy-start(bf16[96,4096]{1,0:T(8,128)(2,1)S(1)} %collective-permute-done.8.refs_4_.rest_4_) | copy-start | bytes 2359300
  44.5 12.0 %collective-permute-start.10 = (bf16[96,4096]{1,0:T(8,128)(2,1)S(1)}, bf16[96,4096]{1,0:T(8,128)(2,1)S(1)}, u32[]{:S(2)}, u32[]{:S(2)}) collective-permute-start(bf16[96,4096]{1,0:T(8,128)(2,1)S(1)} %collective-permute-done.8.refs_4_.rest_4_), channel_id=1, source_target_pairs={{0,3},{1,0},{2,1},{3,2},{4,7},{5,4},{6,5},{7,6},{8,11},{9,8},{10,9... | collective-permute-start | bytes 2359304 | tf_op jit(solution)/shard_map/ppermute | solution.py:36
  46.2 13.2 %collective-permute-start.9 = (bf16[96,4096]{1,0:T(8,128)(2,1)S(1)}, bf16[96,4096]{1,0:T(8,128)(2,1)S(1)}, u32[]{:S(2)}, u32[]{:S(2)}) collective-permute-start(bf16[96,4096]{1,0:T(8,128)(2,1)S(1)} %collective-permute-done.8.refs_4_.rest_4_), channel_id=1, source_target_pairs={{0,1},{1,2},{2,3},{3,0},{4,5},{5,6},{6,7},{7,4},{8,9},{9,10},{10,1... | collective-permute-start | bytes 2359304 | tf_op jit(solution)/shard_map/ppermute | solution.py:36
  51.3 20.3 %copy-start = (bf16[96,4096]{1,0:T(8,128)(2,1)}, bf16[96,4096]{1,0:T(8,128)(2,1)S(1)}, u32[]{:S(2)}) copy-start(bf16[96,4096]{1,0:T(8,128)(2,1)S(1)} %pad_maximum_fusion.refs_2_.rest_2_) | copy-start | bytes 2359300
  56.5 7.2 %copy-start.5 = (bf16[96,4096]{1,0:T(8,128)(2,1)}, bf16[96,4096]{1,0:T(8,128)(2,1)S(1)}, u32[]{:S(2)}) copy-start(bf16[96,4096]{1,0:T(8,128)(2,1)S(1)} %collective-permute-done.10.refs_5_.rest_5_) | copy-start | bytes 2359300
  59.4 4.4 %copy-start.6 = (bf16[96,4096]{1,0:T(8,128)(2,1)}, bf16[96,4096]{1,0:T(8,128)(2,1)S(1)}, u32[]{:S(2)}) copy-start(bf16[96,4096]{1,0:T(8,128)(2,1)S(1)} %collective-permute-done.9.refs_7_.rest_7_) | copy-start | bytes 2359300
  59.4 4.4 %collective-permute-start.11 = (bf16[4096,256]{1,0:T(8,128)(2,1)}, bf16[4096,256]{1,0:T(8,128)(2,1)S(1)}, u32[]{:S(2)}, u32[]{:S(2)}) collective-permute-start(bf16[4096,256]{1,0:T(8,128)(2,1)} %constant_dynamic-update-slice_fusion.2.elder_mine_ref), channel_id=1, source_target_pairs={{0,8},{8,0},{16,24},{24,16},{32,40},{40,32},{48,56},{56,48},{64,72... | collective-permute-start | bytes 6291464 | tf_op jit(solution)/shard_map/ppermute | solution.py:43
  59.4 21.5 %collective-permute-start.12 = (bf16[96,4096]{1,0:T(8,128)(2,1)S(1)}, bf16[96,4096]{1,0:T(8,128)(2,1)S(1)}, u32[]{:S(2)}, u32[]{:S(2)}) collective-permute-start(bf16[96,4096]{1,0:T(8,128)(2,1)S(1)} %pad_maximum_fusion.refs_2_.rest_2_), channel_id=1, source_target_pairs={{0,4},{1,5},{2,6},{3,7},{4,0},{5,1},{6,2},{7,3},{8,12},{9,13},{10,... | collective-permute-start | bytes 2359304 | tf_op jit(solution)/shard_map/ppermute | solution.py:36
  63.7 1.3 copy-start.3
  80.8 0.9 copy-start.7
  81.8 76.9 %all-to-all-start = ((bf16[8,96,4096]{2,1,0:T(8,128)(2,1)}), bf16[8,96,4096]{2,1,0:T(8,128)(2,1)}, u32[]{:S(2)}, u32[]{:S(2)}) async-start(bf16[8,96,4096]{2,1,0:T(8,128)(2,1)} %bitcast.29), calls=%async_computation | async-start | bytes 12582912 | tf_op jit(solution)/shard_map/all_to_all | solution.py:504
  104.0 9.0 %collective-permute-start.13 = (bf16[4096,256]{1,0:T(8,128)(2,1)}, bf16[4096,256]{1,0:T(8,128)(2,1)}, u32[]{:S(2)}, u32[]{:S(2)}) collective-permute-start(bf16[4096,256]{1,0:T(8,128)(2,1)} %get-tuple-element.52), channel_id=1, source_target_pairs={{0,8},{8,0},{16,24},{24,16},{32,40},{40,32},{48,56},{56,48},{64,72... | collective-permute-start | bytes 6291464 | tf_op jit(solution)/shard_map/ppermute | solution.py:43
  113.0 16.7 %collective-permute-start.19 = (bf16[8,512,256]{2,1,0:T(8,128)(2,1)}, bf16[8,512,256]{2,1,0:T(8,128)(2,1)}, u32[]{:S(2)}, u32[]{:S(2)}) collective-permute-start(bf16[8,512,256]{2,1,0:T(8,128)(2,1)} %weight_grad.2), channel_id=1, source_target_pairs={{0,8},{8,0},{16,24},{24,16},{32,40},{40,32},{48,56},{56,48},{64,72... | collective-permute-start | bytes 6291464 | tf_op jit(solution)/shard_map/ppermute | solution.py:43
  117.0 17.5 %collective-permute-start.14 = (bf16[1024,256]{1,0:T(8,128)(2,1)}, bf16[1024,256]{1,0:T(8,128)(2,1)S(1)}, u32[]{:S(2)}, u32[]{:S(2)}) collective-permute-start(bf16[1024,256]{1,0:T(8,128)(2,1)} %get-tuple-element.69), channel_id=1, source_target_pairs={{0,32},{8,40},{16,48},{24,56},{32,64},{40,72},{48,80},{56,88},{64,... | collective-permute-start | bytes 1572872 | tf_op jit(solution)/shard_map/ppermute | solution.py:43
  117.0 29.9 %collective-permute-start.15 = (bf16[1024,256]{1,0:T(8,128)(2,1)}, bf16[1024,256]{1,0:T(8,128)(2,1)S(1)}, u32[]{:S(2)}, u32[]{:S(2)}) collective-permute-start(bf16[1024,256]{1,0:T(8,128)(2,1)} %get-tuple-element.71), channel_id=1, source_target_pairs={{0,64},{8,72},{16,80},{24,88},{32,96},{40,104},{48,112},{56,120},{... | collective-permute-start | bytes 1572872 | tf_op jit(solution)/shard_map/ppermute | solution.py:43
  123.5 23.4 %collective-permute-start.16 = (bf16[1024,256]{1,0:T(8,128)(2,1)}, bf16[1024,256]{1,0:T(8,128)(2,1)}, u32[]{:S(2)}, u32[]{:S(2)}) collective-permute-start(bf16[1024,256]{1,0:T(8,128)(2,1)} %get-tuple-element.70), channel_id=1, source_target_pairs={{0,96},{8,104},{16,112},{24,120},{32,0},{40,8},{48,16},{56,24},{64... | collective-permute-start | bytes 1572872 | tf_op jit(solution)/shard_map/ppermute | solution.py:43
  134.5 14.4 %copy-start.8 = (bf16[1024,256]{1,0:T(8,128)(2,1)}, bf16[1024,256]{1,0:T(8,128)(2,1)S(1)}, u32[]{:S(2)}) copy-start(bf16[1024,256]{1,0:T(8,128)(2,1)S(1)} %collective-permute-done.14) | copy-start | bytes 1572868
  146.9 0.8 copy-start.9
  147.7 4.4 %copy-start.10 = (bf16[1024,256]{1,0:T(8,128)(2,1)S(1)}, bf16[1024,256]{1,0:T(8,128)(2,1)}, u32[]{:S(2)}) copy-start(bf16[1024,256]{1,0:T(8,128)(2,1)} %copy-done.9) | copy-start | bytes 1572868
  148.9 26.1 %collective-permute-start.20 = (bf16[2,512,256]{2,1,0:T(8,128)(2,1)}, bf16[2,512,256]{2,1,0:T(8,128)(2,1)}, u32[]{:S(2)}, u32[]{:S(2)}) collective-permute-start(bf16[2,512,256]{2,1,0:T(8,128)(2,1)} %get-tuple-element.68), channel_id=1, source_target_pairs={{0,32},{8,40},{16,48},{24,56},{32,64},{40,72},{48,80},{56,88},{64,... | collective-permute-start | bytes 1572872 | tf_op jit(solution)/shard_map/ppermute | solution.py:43
  148.9 26.2 %collective-permute-start.21 = (bf16[2,512,256]{2,1,0:T(8,128)(2,1)}, bf16[2,512,256]{2,1,0:T(8,128)(2,1)}, u32[]{:S(2)}, u32[]{:S(2)}) collective-permute-start(bf16[2,512,256]{2,1,0:T(8,128)(2,1)} %get-tuple-element.67), channel_id=1, source_target_pairs={{0,64},{8,72},{16,80},{24,88},{32,96},{40,104},{48,112},{56,120},{... | collective-permute-start | bytes 1572872 | tf_op jit(solution)/shard_map/ppermute | solution.py:43
  151.7 23.8 %collective-permute-start.22 = (bf16[2,512,256]{2,1,0:T(8,128)(2,1)}, bf16[2,512,256]{2,1,0:T(8,128)(2,1)}, u32[]{:S(2)}, u32[]{:S(2)}) collective-permute-start(bf16[2,512,256]{2,1,0:T(8,128)(2,1)} %get-tuple-element.66), channel_id=1, source_target_pairs={{0,96},{8,104},{16,112},{24,120},{32,0},{40,8},{48,16},{56,24},{64... | collective-permute-start | bytes 1572872 | tf_op jit(solution)/shard_map/ppermute | solution.py:43
  159.4 7.7 %collective-permute-start.17 = (bf16[512,256]{1,0:T(8,128)(2,1)S(1)}, bf16[512,256]{1,0:T(8,128)(2,1)S(1)}, u32[]{:S(2)}, u32[]{:S(2)}) collective-permute-start(bf16[512,256]{1,0:T(8,128)(2,1)S(1)} %get-tuple-element.72), channel_id=1, source_target_pairs={{0,16},{8,24},{16,0},{24,8},{32,48},{40,56},{48,32},{56,40},{64,80... | collective-permute-start | bytes 786440 | tf_op jit(solution)/shard_map/ppermute | solution.py:43
  167.1 0.7 copy-start.11
  170.6 11.7 %all-to-all-start.1 = ((bf16[4,2,96,256]{3,2,1,0:T(8,128)(2,1)}), bf16[4,2,96,256]{3,2,1,0:T(8,128)(2,1)S(1)}, u32[]{:S(2)}, u32[]{:S(2)}) async-start(bf16[4,2,96,256]{3,2,1,0:T(8,128)(2,1)} %settle.1), calls=%async_computation.1 | async-start | bytes 786432 | tf_op jit(solution)/shard_map/all_to_all | solution.py:504
  177.1 7.6 %collective-permute-start.23 = (bf16[512,256]{1,0:T(8,128)(2,1)S(1)}, bf16[512,256]{1,0:T(8,128)(2,1)S(1)}, u32[]{:S(2)}, u32[]{:S(2)}) collective-permute-start(bf16[512,256]{1,0:T(8,128)(2,1)S(1)} %slice_bitcast_fusion), channel_id=1, source_target_pairs={{0,16},{8,24},{16,0},{24,8},{32,48},{40,56},{48,32},{56,40},{64,80... | collective-permute-start | bytes 786440 | tf_op jit(solution)/shard_map/ppermute | solution.py:43
  182.4 5.7 %collective-permute-start.18 = (bf16[96,256]{1,0:T(8,128)(2,1)S(1)}, bf16[96,256]{1,0:T(8,128)(2,1)S(1)}, u32[]{:S(2)}, u32[]{:S(2)}) collective-permute-start(bf16[96,256]{1,0:T(8,128)(2,1)S(1)} %slice_bitcast_fusion.2), channel_id=1, source_target_pairs={{0,4},{1,5},{2,6},{3,7},{4,0},{5,1},{6,2},{7,3},{8,12},{9,13},{10,... | collective-permute-start | bytes 147464 | tf_op jit(solution)/shard_map/ppermute | solution.py:36

commit v4 on v3

--- a/solution.py
+++ b/solution.py
@@ -23,7 +23,6 @@
 F32 = jnp.float32
 BF16 = jnp.bfloat16
 
-Y_GROUPS = [[0, 1, 2, 3], [4, 5, 6, 7]]
 Z_GROUPS = [[0, 4, 8, 12], [1, 5, 9, 13], [2, 6, 10, 14], [3, 7, 11, 15]]
 DOWN = (((0,), (0,)), ((), ()))
 ANY_SPEC = pl.BlockSpec(memory_space=pl.ANY)
@@ -471,7 +470,7 @@
 
 def settle_kernel(place, owner, offset, own_ref, *rest):
     parts, out_ref, total = rest[:2], rest[2], rest[3]
-    leaf, head = place[0], place[1]
+    leaf = place[0]
     total[...] = own_ref[...]
 
     def find(i, start):
@@ -481,16 +480,14 @@
     start = lax.fori_loop(0, owner.shape[0], find, jnp.int32(0))
     spot = pl.ds(pl.multiple_of(start, WIN), ELDER)
     total[spot, :] += sum(part[...].astype(F32) for part in parts)
-    for y in range(4):
-        for side in range(2):
-            first = pl.multiple_of(((head // 4 + side) % 2 * 4 + y) * 96, 32)
-            out_ref[y, side] = total[pl.ds(first, 96), :].astype(BF16)
+    for h in range(8):
+        out_ref[h] = total[h * 96 : (h + 1) * 96, :].astype(BF16)
 
 
 def settle(place, owner, offset, own, parts):
     return pl.pallas_call(
         settle_kernel,
-        out_shape=jax.ShapeDtypeStruct((4, 2, 96, 2 * HD), BF16),
+        out_shape=jax.ShapeDtypeStruct((8, 96, 2 * HD), BF16),
         in_specs=[SMEM_SPEC] * 3 + [VMEM_SPEC] * 3,
         out_specs=VMEM_SPEC,
         scratch_shapes=[pltpu.VMEM((ROWS, 2 * HD), F32)],
@@ -521,7 +518,6 @@
     seg_length,
 ):
     place = jnp.stack([lax.axis_index("leaf"), lax.axis_index("head")]).astype(jnp.int32)
-    side = lax.axis_index("head") // 4
     segs = (seg_owner, seg_parent, seg_offset, seg_length)
     own, elder = pack(place, seg_owner, seg_offset, key_rows, value_rows)
     pair = jnp.concatenate([elder, leaf_perm(elder, 0, 1, 0)], axis=0)
@@ -563,21 +559,19 @@
     pair_parts = [pair_blocks[0], *[leaf_perm(pair_blocks[d], d, 0, 0) for d in range(1, 4)]]
     mine_weight = weight_grad_of(place, after(attn, pair_joined), pieces, 0)
     weight_joined = add(mine_weight, weight_recv)
-    weight_joined = after(weight_joined, *pair_parts)
+    weight_joined = after(weight_joined, pair_parts[1])
     weight_parts = spread_depth(weight_joined.reshape(4, 2, *weight_joined.shape[1:]))
     pair_sum = add(*pair_parts)
     pair_sum, layer_parts = lax.optimization_barrier((pair_sum, layer_parts))
     pair_last = leaf_perm(pair_sum[ELDER:], 0, 1, 0)
     layer_out = sum_blocks(layer_parts)
     blocks = settle(place, seg_owner, seg_offset, own_grad, [pair_sum[:ELDER], pair_last])
-    weight_parts = [after(part, blocks) for part in weight_parts]
+    weight_parts = [after(part, pair_last) for part in weight_parts]
     weight_sum = add(*weight_parts)
     weight_grad = add(weight_sum[0], leaf_perm(weight_sum[1], 0, 1, 0))
-    total = sum_blocks(exchange(blocks, "head", Y_GROUPS))
-    near = total[0]
-    far = head_perm(total[1], 1, 0)
-    first = jnp.where(side == 0, near, far)
-    second = jnp.where(side == 0, far, near)
+    terms = exchange(blocks, "head")
+    first = add(*[terms[h] for h in range(4)])
+    second = add(*[terms[h] for h in range(4, 8)])
     key_grads = jnp.concatenate([first[:, :HD], second[:, :HD]], axis=1)
     value_grads = jnp.concatenate([first[:, HD:], second[:, HD:]], axis=1)
     return layer_out, query_grads, key_grads, value_grads, weight_grad

time: 190 us -> 195 us (1.026); the launches traced: 189 us -> 192 us
  Pallas kernels: 51.8 us -> 56 us
    all_to_all x2, waiting for transfers between devices: 9.99 us -> 14.8 us  [exchange(): return lax.all_to_all(blocks, axis, 0, 0, axis_index_groups=groups)]
    ppermute x9 -> x8, waiting for transfers between devices: 16.5 us -> 12.2 us  [head_perm(): return lax.ppermute(array, 'head', pairs)]
    all_to_all x2, starting transfers between devices: 9.22 us -> 12 us  [exchange(): return lax.all_to_all(blocks, axis, 0, 0, axis_index_groups=groups)]
    ppermute x9 -> x8, starting transfers between devices: 16.8 us -> 14.6 us  [head_perm(): return lax.ppermute(array, 'head', pairs)]
    pallas_call x1, Pallas kernels: 9.07 us -> 11.3 us  [backward(): pl.pallas_call(backward_kernel, out_shape=(jax.ShapeDtypeStruct((ROWS, HE...]
    unnamed x27 -> x23, local copies, waits for them, and re-layouts: 7.25 us -> 5.81 us
  transfers between devices with their start and end apart: 26 -> 25, of which waited for: 17 -> 12; matrix products, arithmetic and copies ran while one was open for 14% -> 13% of each run, Pallas kernels for 27% -> 29%
where the time goes in v4:
time: 195 us; the launch traced here: 192 us
  waiting for transfers between devices  57.8 us (30%)
  Pallas kernels  56 us (29%)
  starting transfers between devices  47.8 us (25%)
  other arithmetic  17.1 us (9%)
  local copies, waits for them, and re-layouts  12.4 us (6%)
    ppermute x15, waiting for transfers between devices, leaf_perm(): return lax.ppermute(array, 'leaf', pairs)  30.8 us
    ppermute x15, starting transfers between devices, leaf_perm(): return lax.ppermute(array, 'leaf', pairs)  21.2 us
    all_to_all x2, waiting for transfers between devices, exchange(): return lax.all_to_all(blocks, axis, 0, 0, axis_index_groups=groups)  14.8 us
    ppermute x8, starting transfers between devices, head_perm(): return lax.ppermute(array, 'head', pairs)  14.6 us
    convert_element_type x6, other arithmetic, add(): return total.astype(BF16)  14.1 us
    pallas_call x2, Pallas kernels, weight_grad_of(): pl.pallas_call(functools.partial(weight_grad_kernel, flip), grid=(2,), in...  12.4 us
    ppermute x8, waiting for transfers between devices, head_perm(): return lax.ppermute(array, 'head', pairs)  12.2 us
    all_to_all x2, starting transfers between devices, exchange(): return lax.all_to_all(blocks, axis, 0, 0, axis_index_groups=groups)  12 us
  transfers between devices with their start and end apart: 25, of which 12 were waited for; matrix products, arithmetic and copies ran while one was open for 13% of the time, Pallas kernels for 29%

profile of v4, /device:TPU:0, one launch (start us, length us, event | category | flops | bytes accessed | tf_op | source)
XLA Modules:
  0.0 192.0 jit_solution(2930972045468795475)
XLA Ops:
  0.6 1.7 collective-permute-start.4
  2.4 0.6 pad_add_fusion.place
  2.9 2.6 %pack_keys.1 = (bf16[768,256]{1,0:T(8,128)(2,1)}, bf16[512,256]{1,0:T(8,128)(2,1)}) custom-call(s32[2]{0:T(128)} %pad_add_fusion.place, s32[42]{0:T(128)} %owner.7, s32[42]{0:T(128)} %offset.7, bf16[768,256]{1,0:T(8,128)(2,1)} %key_ref.1, bf16[768,256]{1,0:T(8,128)(2,1)} %value_ref.1), custom_call_target="tpu_custom_call" | custom-call | bytes 100000 | tf_op jit(solution)/shard_map/pack_keys/pallas_call | solution.py:78
  5.5 1.5 collective-permute-start
  7.0 1.7 collective-permute-start.6
  8.7 2.7 %collective-permute-start.8 = (bf16[96,4096]{1,0:T(8,128)(2,1)}, bf16[96,4096]{1,0:T(8,128)(2,1)S(1)}, u32[]{:S(2)}, u32[]{:S(2)}) collective-permute-start(bf16[96,4096]{1,0:T(8,128)(2,1)} %rest_0_.3), channel_id=1, source_target_pairs={{0,4},{1,5},{2,6},{3,7},{4,0},{5,1},{6,2},{7,3},{8,12},{9,13},{10,... | collective-permute-start | bytes 2359304 | tf_op jit(solution)/shard_map/ppermute | solution.py:35
  11.4 1.8 constant_dynamic-update-slice_fusion.1
  13.2 1.8 collective-permute-done
  15.0 0.8 constant_dynamic-update-slice_fusion
  15.8 4.0 %collective-permute-start.1 = (bf16[1024,256]{1,0:T(8,128)(2,1)}, bf16[1024,256]{1,0:T(8,128)(2,1)S(1)}, u32[]{:S(2)}, u32[]{:S(2)}) collective-permute-start(bf16[1024,256]{1,0:T(8,128)(2,1)} %get-tuple-element.76), channel_id=1, source_target_pairs={{0,96},{8,104},{16,112},{24,120},{32,0},{40,8},{48,16},{56,24},{64... | collective-permute-start | bytes 1572872 | tf_op jit(solution)/shard_map/ppermute | solution.py:42
  19.8 1.7 collective-permute-done.4.refs_3_.rest_3_
  21.6 1.9 collective-permute-start.3
  23.5 2.4 %collective-permute-done.6.refs_1_.rest_1_ = bf16[96,4096]{1,0:T(8,128)(2,1)S(1)} collective-permute-done((bf16[96,4096]{1,0:T(8,128)(2,1)}, bf16[96,4096]{1,0:T(8,128)(2,1)S(1)}, u32[]{:S(2)}, u32[]{:S(2)}) %collective-permute-start.6) | collective-permute-done | bytes 786464 | tf_op jit(solution)/shard_map/ppermute | solution.py:35
  25.9 1.6 collective-permute-start.5
  27.5 0.8 slice.125
  28.3 11.6 %collective-permute-done.1 = bf16[1024,256]{1,0:T(8,128)(2,1)S(1)} collective-permute-done((bf16[1024,256]{1,0:T(8,128)(2,1)}, bf16[1024,256]{1,0:T(8,128)(2,1)S(1)}, u32[]{:S(2)}, u32[]{:S(2)}) %collective-permute-start.1) | collective-permute-done | bytes 524320 | tf_op jit(solution)/shard_map/ppermute | solution.py:42
  39.9 1.8 collective-permute-start.7
  41.7 2.7 %empty_elders.1 = (bf16[4096,256]{1,0:T(8,128)(2,1)}, bf16[4096,256]{1,0:T(8,128)(2,1)}) custom-call(s32[2]{0:T(128)} %pad_add_fusion.place), custom_call_target="tpu_custom_call" | custom-call | bytes 100000 | tf_op jit(solution)/shard_map/empty_elders/pallas_call | solution.py:99
  44.5 1.6 collective-permute-start.10
  46.1 0.4 collective-permute-start.9
  46.5 0.8 constant_dynamic-update-slice_fusion.4
  47.4 0.8 constant_dynamic-update-slice_fusion.3
  48.2 1.9 constant_dynamic-update-slice_fusion.2.elder_mine_ref
  50.1 1.2 pad_maximum_fusion.refs_2_.rest_2_
  51.3 5.2 %collective-permute-done.10.refs_5_.rest_5_ = bf16[96,4096]{1,0:T(8,128)(2,1)S(1)} collective-permute-done((bf16[96,4096]{1,0:T(8,128)(2,1)S(1)}, bf16[96,4096]{1,0:T(8,128)(2,1)S(1)}, u32[]{:S(2)}, u32[]{:S(2)}) %collective-permute-start.10) | collective-permute-done | bytes 786464 | tf_op jit(solution)/shard_map/ppermute | solution.py:35
  56.5 2.8 %collective-permute-done.9.refs_7_.rest_7_ = bf16[96,4096]{1,0:T(8,128)(2,1)S(1)} collective-permute-done((bf16[96,4096]{1,0:T(8,128)(2,1)S(1)}, bf16[96,4096]{1,0:T(8,128)(2,1)S(1)}, u32[]{:S(2)}, u32[]{:S(2)}) %collective-permute-start.9) | collective-permute-done | bytes 786464 | tf_op jit(solution)/shard_map/ppermute | solution.py:35
  59.3 3.0 %collective-permute-start.12 = (bf16[96,4096]{1,0:T(8,128)(2,1)S(1)}, bf16[96,4096]{1,0:T(8,128)(2,1)S(1)}, u32[]{:S(2)}, u32[]{:S(2)}) collective-permute-start(bf16[96,4096]{1,0:T(8,128)(2,1)S(1)} %pad_maximum_fusion.refs_2_.rest_2_), channel_id=1, source_target_pairs={{0,4},{1,5},{2,6},{3,7},{4,0},{5,1},{6,2},{7,3},{8,12},{9,13},{10,... | collective-permute-start | bytes 2359304 | tf_op jit(solution)/shard_map/ppermute | solution.py:35
  62.4 1.3 collective-permute-done.11.elder_other_ref
  63.7 1.3 copy-done.3
  65.0 8.5 %attention.1 = (bf16[768,512]{1,0:T(8,128)(2,1)}, f32[6,8,512]{2,1,0:T(8,128)}) custom-call(s32[2]{0:T(128)} %pad_add_fusion.place, s32[42]{0:T(128)} %owner.7, s32[42]{0:T(128)} %parent.3, s32[42]{0:T(128)} %offset.7, s32[42]{0:T(128)} %length.3, bf16[768,512]{1,0:T(8,128)(2,1)} %query_ref.3, bf16[768,256]{1,0:T(8,128)(2,1)} %get-tuple-element.35.own_ref, ...), custom_call_target="tpu_custom_call" | custom-call | bytes 100000 | tf_op jit(solution)/shard_map/attention/pallas_call | solution.py:258
  73.5 7.5 %project.1 = bf16[768,4096]{1,0:T(8,128)(2,1)} custom-call(bf16[768,512]{1,0:T(8,128)(2,1)} %get-tuple-element.59.attn_ref, bf16[512,4096]{1,0:T(8,128)(2,1)} %weight_ref.2), custom_call_target="tpu_custom_call" | custom-call | bytes 100000 | tf_op jit(solution)/shard_map/project/pallas_call | solution.py:288
  81.0 0.9 copy-done.7
  81.9 4.9 %all-to-all-start = ((bf16[8,96,4096]{2,1,0:T(8,128)(2,1)}), bf16[8,96,4096]{2,1,0:T(8,128)(2,1)}, u32[]{:S(2)}, u32[]{:S(2)}) async-start(bf16[8,96,4096]{2,1,0:T(8,128)(2,1)} %bitcast.25), calls=%async_computation | async-start | bytes 12582912 | tf_op jit(solution)/shard_map/all_to_all | solution.py:501
  86.9 8.3 %attn_grad.1.grad_ref = bf16[768,512]{1,0:T(8,128)(2,1)} custom-call(s32[2]{0:T(128)} %pad_add_fusion.place, bf16[512,4096]{1,0:T(8,128)(2,1)} %weight_ref.2, bf16[96,4096]{1,0:T(8,128)(2,1)} %rest_0_.3, bf16[96,4096]{1,0:T(8,128)(2,1)} %copy-done.2, bf16[96,4096]{1,0:T(8,128)(2,1)} %copy-done, bf16[96,4096]{1,0:T(8,128)(2,1)} %copy-done.1, ...), custom_call_target="tpu_custom_call" | custom-call | bytes 100000 | tf_op jit(solution)/shard_map/attn_grad/pallas_call | solution.py:327
  95.1 11.3 %attention_back.1 = (bf16[768,512]{1,0:T(8,128)(2,1)}, f32[768,256]{1,0:T(8,128)}, bf16[4096,256]{1,0:T(8,128)(2,1)}, bf16[4096,256]{1,0:T(8,128)(2,1)}) custom-call(s32[2]{0:T(128)} %pad_add_fusion.place, s32[42]{0:T(128)} %owner.7, s32[42]{0:T(128)} %parent.3, s32[42]{0:T(128)} %offset.7, ...), custom_call_target="tpu_custom_call", output_to_operand_aliasing={{2}: (12, {}), {3}: (13, {})} | custom-call | bytes 100000 | tf_op jit(solution)/shard_map/attention_back/pallas_call | solution.py:446
  106.4 0.1 collective-permute-start.13
  106.6 6.2 %weight_grad.2 = bf16[8,512,256]{2,1,0:T(8,128)(2,1)} custom-call(s32[2]{0:T(128)} %pad_add_fusion.place, bf16[768,512]{1,0:T(8,128)(2,1)} %get-tuple-element.59.attn_ref, bf16[96,4096]{1,0:T(8,128)(2,1)} %rest_0_.3, bf16[96,4096]{1,0:T(8,128)(2,1)} %copy-done.2, bf16[96,4096]{1,0:T(8,128)(2,1)} %copy-done, bf16[96,4096]{1,0:T(8,128)(2,1)} %copy-done.1, ...), custom_call_target="tpu_custom_call" | custom-call | bytes 100000 | tf_op jit(solution)/shard_map/weight_grad/pallas_call | solution.py:369
  112.8 0.4 collective-permute-start.18
  113.3 2.8 %add_convert_fusion.1 = bf16[4096,256]{1,0:T(8,128)(2,1)S(1)} fusion(bf16[4096,256]{1,0:T(8,128)(2,1)} %collective-permute-done.13, bf16[4096,256]{1,0:T(8,128)(2,1)} %get-tuple-element.54), kind=kLoop, calls=%fused_computation.1 | loop fusion | flops 4194304 | bytes 6291456 | tf_op jit(solution)/shard_map/convert_element_type | solution.py:53
  116.0 1.1 fusion.4
  117.1 5.0 %collective-permute-start.15 = (bf16[1024,256]{1,0:T(8,128)(2,1)}, bf16[1024,256]{1,0:T(8,128)(2,1)S(1)}, u32[]{:S(2)}, u32[]{:S(2)}) collective-permute-start(bf16[1024,256]{1,0:T(8,128)(2,1)} %get-tuple-element.71), channel_id=1, source_target_pairs={{0,64},{8,72},{16,80},{24,88},{32,96},{40,104},{48,112},{56,120},{... | collective-permute-start | bytes 1572872 | tf_op jit(solution)/shard_map/ppermute | solution.py:42
  122.1 6.2 %weight_grad.3 = bf16[8,512,256]{2,1,0:T(8,128)(2,1)} custom-call(s32[2]{0:T(128)} %pad_add_fusion.place, bf16[768,512]{1,0:T(8,128)(2,1)} %get-tuple-element.59.attn_ref, bf16[96,4096]{1,0:T(8,128)(2,1)} %rest_0_.3, bf16[96,4096]{1,0:T(8,128)(2,1)} %copy-done.2, bf16[96,4096]{1,0:T(8,128)(2,1)} %copy-done, bf16[96,4096]{1,0:T(8,128)(2,1)} %copy-done.1, ...), custom_call_target="tpu_custom_call" | custom-call | bytes 100000 | tf_op jit(solution)/shard_map/weight_grad/pallas_call | solution.py:369
  128.3 2.7 %add_convert_fusion = bf16[8,512,256]{2,1,0:T(8,128)(2,1)S(1)} fusion(bf16[8,512,256]{2,1,0:T(8,128)(2,1)} %collective-permute-done.18, bf16[8,512,256]{2,1,0:T(8,128)(2,1)} %weight_grad.3), kind=kLoop, calls=%fused_computation | loop fusion | flops 4194304 | bytes 6291456 | tf_op jit(solution)/shard_map/convert_element_type | solution.py:53
  131.0 1.7 collective-permute-done.14
  132.8 1.2 dynamic-slice_bitcast_fusion.3
  134.0 0.1 copy-done.8
  134.1 0.3 collective-permute-start.19
  134.4 3.8 %collective-permute-start.20 = (bf16[2,512,256]{2,1,0:T(8,128)(2,1)}, bf16[2,512,256]{2,1,0:T(8,128)(2,1)}, u32[]{:S(2)}, u32[]{:S(2)}) collective-permute-start(bf16[2,512,256]{2,1,0:T(8,128)(2,1)} %get-tuple-element.67), channel_id=1, source_target_pairs={{0,64},{8,72},{16,80},{24,88},{32,96},{40,104},{48,112},{56,120},{... | collective-permute-start | bytes 1572872 | tf_op jit(solution)/shard_map/ppermute | solution.py:42
  138.2 0.1 collective-permute-start.21
  138.4 7.8 %collective-permute-done.15 = bf16[1024,256]{1,0:T(8,128)(2,1)S(1)} collective-permute-done((bf16[1024,256]{1,0:T(8,128)(2,1)}, bf16[1024,256]{1,0:T(8,128)(2,1)S(1)}, u32[]{:S(2)}, u32[]{:S(2)}) %collective-permute-start.15) | collective-permute-done | bytes 524320 | tf_op jit(solution)/shard_map/ppermute | solution.py:42
  146.1 1.5 add_convert_fusion.4
  147.6 11.0 %all-to-all-done = bf16[8,96,4096]{2,1,0:T(8,128)(2,1)} async-done(((bf16[8,96,4096]{2,1,0:T(8,128)(2,1)}), bf16[8,96,4096]{2,1,0:T(8,128)(2,1)}, u32[]{:S(2)}, u32[]{:S(2)}) %all-to-all-start) | async-done | bytes 6291488 | tf_op jit(solution)/shard_map/all_to_all | solution.py:501
  158.6 0.7 fusion.5
  159.4 2.1 %collective-permute-start.17 = (bf16[512,256]{1,0:T(8,128)(2,1)S(1)}, bf16[512,256]{1,0:T(8,128)(2,1)S(1)}, u32[]{:S(2)}, u32[]{:S(2)}) collective-permute-start(bf16[512,256]{1,0:T(8,128)(2,1)S(1)} %get-tuple-element.72), channel_id=1, source_target_pairs={{0,16},{8,24},{16,0},{24,8},{32,48},{40,56},{48,32},{56,40},{64,80... | collective-permute-start | bytes 786440 | tf_op jit(solution)/shard_map/ppermute | solution.py:42
  161.4 6.5 %collective-permute-done.17.rest_1_ = bf16[512,256]{1,0:T(8,128)(2,1)S(1)} collective-permute-done((bf16[512,256]{1,0:T(8,128)(2,1)S(1)}, bf16[512,256]{1,0:T(8,128)(2,1)S(1)}, u32[]{:S(2)}, u32[]{:S(2)}) %collective-permute-start.17) | collective-permute-done | bytes 262176 | tf_op jit(solution)/shard_map/ppermute | solution.py:42
  167.9 1.7 add_convert_fusion.3
  169.7 1.8 collective-permute-start.22
  171.5 2.8 %settle.1 = bf16[8,96,256]{2,1,0:T(8,128)(2,1)} custom-call(s32[2]{0:T(128)} %pad_add_fusion.place, s32[42]{0:T(128)} %owner.7, s32[42]{0:T(128)} %offset.7, f32[768,256]{1,0:T(8,128)} %get-tuple-element.57.own_ref, bf16[512,256]{1,0:T(8,128)(2,1)} %get-tuple-element.73.rest_0_, bf16[512,256]{1,0:T(8,128)(2,1)} %copy-done.9), custom_call_target="tpu_custom_call" | custom-call | bytes 100000 | tf_op jit(solution)/shard_map/settle/pallas_call | solution.py:488
  174.3 7.1 %all-to-all-start.1 = ((bf16[8,96,256]{2,1,0:T(8,128)(2,1)}), bf16[8,96,256]{2,1,0:T(8,128)(2,1)S(1)}, u32[]{:S(2)}, u32[]{:S(2)}) async-start(bf16[8,96,256]{2,1,0:T(8,128)(2,1)} %settle.1), calls=%async_computation.1 | async-start | bytes 786432 | tf_op jit(solution)/shard_map/all_to_all | solution.py:501
  181.4 4.7 %fusion = bf16[96,4096]{1,0:T(8,128)(2,1)} fusion(bf16[8,96,4096]{2,1,0:T(8,128)(2,1)} %all-to-all-done), kind=kLoop, calls=%fused_computation.5 | loop fusion | flops 6291456 | bytes 7077888 | tf_op jit(solution)/shard_map/convert_element_type | solution.py:53
  186.1 0.8 fusion.1
  186.8 3.8 %all-to-all-done.1 = bf16[8,96,256]{2,1,0:T(8,128)(2,1)S(1)} async-done(((bf16[8,96,256]{2,1,0:T(8,128)(2,1)}), bf16[8,96,256]{2,1,0:T(8,128)(2,1)S(1)}, u32[]{:S(2)}, u32[]{:S(2)}) %all-to-all-start.1) | async-done | bytes 393248 | tf_op jit(solution)/shard_map/all_to_all | solution.py:501
  190.7 0.6 pad_maximum_fusion.2
  191.3 0.6 pad_maximum_fusion.1
  (38 shorter events, 0.2 us)
Async XLA Ops:
  0.6 20.9 %collective-permute-start.4 = (bf16[96,4096]{1,0:T(8,128)(2,1)}, bf16[96,4096]{1,0:T(8,128)(2,1)S(1)}, u32[]{:S(2)}, u32[]{:S(2)}) collective-permute-start(bf16[96,4096]{1,0:T(8,128)(2,1)} %rest_0_.3), channel_id=1, source_target_pairs={{0,1},{1,2},{2,3},{3,0},{4,5},{5,6},{6,7},{7,4},{8,9},{9,10},{10,1... | collective-permute-start | bytes 2359304 | tf_op jit(solution)/shard_map/ppermute | solution.py:35
  5.5 9.4 %collective-permute-start = (bf16[512,256]{1,0:T(8,128)(2,1)}, bf16[512,256]{1,0:T(8,128)(2,1)S(1)}, u32[]{:S(2)}, u32[]{:S(2)}) collective-permute-start(bf16[512,256]{1,0:T(8,128)(2,1)} %get-tuple-element.36), channel_id=1, source_target_pairs={{0,16},{8,24},{16,0},{24,8},{32,48},{40,56},{48,32},{56,40},{64,80... | collective-permute-start | bytes 786440 | tf_op jit(solution)/shard_map/ppermute | solution.py:42
  7.0 18.9 %collective-permute-start.6 = (bf16[96,4096]{1,0:T(8,128)(2,1)}, bf16[96,4096]{1,0:T(8,128)(2,1)S(1)}, u32[]{:S(2)}, u32[]{:S(2)}) collective-permute-start(bf16[96,4096]{1,0:T(8,128)(2,1)} %rest_0_.3), channel_id=1, source_target_pairs={{0,3},{1,0},{2,1},{3,2},{4,7},{5,4},{6,5},{7,6},{8,11},{9,8},{10,9... | collective-permute-start | bytes 2359304 | tf_op jit(solution)/shard_map/ppermute | solution.py:35
  8.7 35.8 %collective-permute-start.8 = (bf16[96,4096]{1,0:T(8,128)(2,1)}, bf16[96,4096]{1,0:T(8,128)(2,1)S(1)}, u32[]{:S(2)}, u32[]{:S(2)}) collective-permute-start(bf16[96,4096]{1,0:T(8,128)(2,1)} %rest_0_.3), channel_id=1, source_target_pairs={{0,4},{1,5},{2,6},{3,7},{4,0},{5,1},{6,2},{7,3},{8,12},{9,13},{10,... | collective-permute-start | bytes 2359304 | tf_op jit(solution)/shard_map/ppermute | solution.py:35
  15.8 24.1 %collective-permute-start.1 = (bf16[1024,256]{1,0:T(8,128)(2,1)}, bf16[1024,256]{1,0:T(8,128)(2,1)S(1)}, u32[]{:S(2)}, u32[]{:S(2)}) collective-permute-start(bf16[1024,256]{1,0:T(8,128)(2,1)} %get-tuple-element.76), channel_id=1, source_target_pairs={{0,96},{8,104},{16,112},{24,120},{32,0},{40,8},{48,16},{56,24},{64... | collective-permute-start | bytes 1572872 | tf_op jit(solution)/shard_map/ppermute | solution.py:42
  19.8 26.3 %collective-permute-start.2 = (bf16[1024,256]{1,0:T(8,128)(2,1)}, bf16[1024,256]{1,0:T(8,128)(2,1)S(1)}, u32[]{:S(2)}, u32[]{:S(2)}) collective-permute-start(bf16[1024,256]{1,0:T(8,128)(2,1)} %get-tuple-element.76), channel_id=1, source_target_pairs={{0,64},{8,72},{16,80},{24,88},{32,96},{40,104},{48,112},{56,120},{... | collective-permute-start | bytes 1572872 | tf_op jit(solution)/shard_map/ppermute | solution.py:42
  21.6 28.5 %copy-start.1 = (bf16[96,4096]{1,0:T(8,128)(2,1)}, bf16[96,4096]{1,0:T(8,128)(2,1)S(1)}, u32[]{:S(2)}) copy-start(bf16[96,4096]{1,0:T(8,128)(2,1)S(1)} %collective-permute-done.4.refs_3_.rest_3_) | copy-start | bytes 2359300
  21.6 26.6 %collective-permute-start.3 = (bf16[1024,256]{1,0:T(8,128)(2,1)}, bf16[1024,256]{1,0:T(8,128)(2,1)}, u32[]{:S(2)}, u32[]{:S(2)}) collective-permute-start(bf16[1024,256]{1,0:T(8,128)(2,1)} %get-tuple-element.76), channel_id=1, source_target_pairs={{0,32},{8,40},{16,48},{24,56},{32,64},{40,72},{48,80},{56,88},{64,... | collective-permute-start | bytes 1572872 | tf_op jit(solution)/shard_map/ppermute | solution.py:42
  25.9 25.3 %copy-start.2 = (bf16[96,4096]{1,0:T(8,128)(2,1)}, bf16[96,4096]{1,0:T(8,128)(2,1)S(1)}, u32[]{:S(2)}) copy-start(bf16[96,4096]{1,0:T(8,128)(2,1)S(1)} %collective-permute-done.6.refs_1_.rest_1_) | copy-start | bytes 2359300
  25.9 24.1 %collective-permute-start.5 = (bf16[48,4096]{1,0:T(8,128)(2,1)S(1)}, bf16[48,4096]{1,0:T(8,128)(2,1)}, u32[]{:S(2)}, u32[]{:S(2)}) collective-permute-start(bf16[48,4096]{1,0:T(8,128)(2,1)S(1)} %slice.124), channel_id=1, source_target_pairs={{0,1},{1,2},{2,3},{3,0},{4,5},{5,6},{6,7},{7,4},{8,9},{9,10},{10,1... | collective-permute-start | bytes 1179656 | tf_op jit(solution)/shard_map/ppermute | solution.py:35
  39.9 10.2 %collective-permute-start.7 = (bf16[48,4096]{1,0:T(8,128)(2,1)}, bf16[48,4096]{1,0:T(8,128)(2,1)}, u32[]{:S(2)}, u32[]{:S(2)}) collective-permute-start(bf16[48,4096]{1,0:T(8,128)(2,1)} %slice.125), channel_id=1, source_target_pairs={{0,3},{1,0},{2,1},{3,2},{4,7},{5,4},{6,5},{7,6},{8,11},{9,8},{10,9... | collective-permute-start | bytes 1179656 | tf_op jit(solution)/shard_map/ppermute | solution.py:35
  44.5 6.8 %copy-start.4 = (bf16[96,4096]{1,0:T(8,128)(2,1)}, bf16[96,4096]{1,0:T(8,128)(2,1)S(1)}, u32[]{:S(2)}) copy-start(bf16[96,4096]{1,0:T(8,128)(2,1)S(1)} %collective-permute-done.8.refs_4_.rest_4_) | copy-start | bytes 2359300
  44.5 12.0 %collective-permute-start.10 = (bf16[96,4096]{1,0:T(8,128)(2,1)S(1)}, bf16[96,4096]{1,0:T(8,128)(2,1)S(1)}, u32[]{:S(2)}, u32[]{:S(2)}) collective-permute-start(bf16[96,4096]{1,0:T(8,128)(2,1)S(1)} %collective-permute-done.8.refs_4_.rest_4_), channel_id=1, source_target_pairs={{0,3},{1,0},{2,1},{3,2},{4,7},{5,4},{6,5},{7,6},{8,11},{9,8},{10,9... | collective-permute-start | bytes 2359304 | tf_op jit(solution)/shard_map/ppermute | solution.py:35
  46.1 13.2 %collective-permute-start.9 = (bf16[96,4096]{1,0:T(8,128)(2,1)S(1)}, bf16[96,4096]{1,0:T(8,128)(2,1)S(1)}, u32[]{:S(2)}, u32[]{:S(2)}) collective-permute-start(bf16[96,4096]{1,0:T(8,128)(2,1)S(1)} %collective-permute-done.8.refs_4_.rest_4_), channel_id=1, source_target_pairs={{0,1},{1,2},{2,3},{3,0},{4,5},{5,6},{6,7},{7,4},{8,9},{9,10},{10,1... | collective-permute-start | bytes 2359304 | tf_op jit(solution)/shard_map/ppermute | solution.py:35
  51.3 22.3 %copy-start = (bf16[96,4096]{1,0:T(8,128)(2,1)}, bf16[96,4096]{1,0:T(8,128)(2,1)S(1)}, u32[]{:S(2)}) copy-start(bf16[96,4096]{1,0:T(8,128)(2,1)S(1)} %pad_maximum_fusion.refs_2_.rest_2_) | copy-start | bytes 2359300
  56.5 7.2 %copy-start.5 = (bf16[96,4096]{1,0:T(8,128)(2,1)}, bf16[96,4096]{1,0:T(8,128)(2,1)S(1)}, u32[]{:S(2)}) copy-start(bf16[96,4096]{1,0:T(8,128)(2,1)S(1)} %collective-permute-done.10.refs_5_.rest_5_) | copy-start | bytes 2359300
  59.3 4.4 %copy-start.6 = (bf16[96,4096]{1,0:T(8,128)(2,1)}, bf16[96,4096]{1,0:T(8,128)(2,1)S(1)}, u32[]{:S(2)}) copy-start(bf16[96,4096]{1,0:T(8,128)(2,1)S(1)} %collective-permute-done.9.refs_7_.rest_7_) | copy-start | bytes 2359300
  59.3 4.4 %collective-permute-start.11 = (bf16[4096,256]{1,0:T(8,128)(2,1)}, bf16[4096,256]{1,0:T(8,128)(2,1)S(1)}, u32[]{:S(2)}, u32[]{:S(2)}) collective-permute-start(bf16[4096,256]{1,0:T(8,128)(2,1)} %constant_dynamic-update-slice_fusion.2.elder_mine_ref), channel_id=1, source_target_pairs={{0,8},{8,0},{16,24},{24,16},{32,40},{40,32},{48,56},{56,48},{64,72... | collective-permute-start | bytes 6291464 | tf_op jit(solution)/shard_map/ppermute | solution.py:42
  59.3 21.7 %collective-permute-start.12 = (bf16[96,4096]{1,0:T(8,128)(2,1)S(1)}, bf16[96,4096]{1,0:T(8,128)(2,1)S(1)}, u32[]{:S(2)}, u32[]{:S(2)}) collective-permute-start(bf16[96,4096]{1,0:T(8,128)(2,1)S(1)} %pad_maximum_fusion.refs_2_.rest_2_), channel_id=1, source_target_pairs={{0,4},{1,5},{2,6},{3,7},{4,0},{5,1},{6,2},{7,3},{8,12},{9,13},{10,... | collective-permute-start | bytes 2359304 | tf_op jit(solution)/shard_map/ppermute | solution.py:35
  63.7 1.3 copy-start.3
  81.0 0.9 copy-start.7
  81.9 76.7 %all-to-all-start = ((bf16[8,96,4096]{2,1,0:T(8,128)(2,1)}), bf16[8,96,4096]{2,1,0:T(8,128)(2,1)}, u32[]{:S(2)}, u32[]{:S(2)}) async-start(bf16[8,96,4096]{2,1,0:T(8,128)(2,1)} %bitcast.25), calls=%async_computation | async-start | bytes 12582912 | tf_op jit(solution)/shard_map/all_to_all | solution.py:501
  106.4 6.8 %collective-permute-start.13 = (bf16[4096,256]{1,0:T(8,128)(2,1)}, bf16[4096,256]{1,0:T(8,128)(2,1)}, u32[]{:S(2)}, u32[]{:S(2)}) collective-permute-start(bf16[4096,256]{1,0:T(8,128)(2,1)} %get-tuple-element.52), channel_id=1, source_target_pairs={{0,8},{8,0},{16,24},{24,16},{32,40},{40,32},{48,56},{56,48},{64,72... | collective-permute-start | bytes 6291464 | tf_op jit(solution)/shard_map/ppermute | solution.py:42
  112.8 15.5 %collective-permute-start.18 = (bf16[8,512,256]{2,1,0:T(8,128)(2,1)}, bf16[8,512,256]{2,1,0:T(8,128)(2,1)}, u32[]{:S(2)}, u32[]{:S(2)}) collective-permute-start(bf16[8,512,256]{2,1,0:T(8,128)(2,1)} %weight_grad.2), channel_id=1, source_target_pairs={{0,8},{8,0},{16,24},{24,16},{32,40},{40,32},{48,56},{56,48},{64,72... | collective-permute-start | bytes 6291464 | tf_op jit(solution)/shard_map/ppermute | solution.py:42
  117.1 15.6 %collective-permute-start.14 = (bf16[1024,256]{1,0:T(8,128)(2,1)S(1)}, bf16[1024,256]{1,0:T(8,128)(2,1)S(1)}, u32[]{:S(2)}, u32[]{:S(2)}) collective-permute-start(bf16[1024,256]{1,0:T(8,128)(2,1)S(1)} %get-tuple-element.69), channel_id=1, source_target_pairs={{0,32},{8,40},{16,48},{24,56},{32,64},{40,72},{48,80},{56,88},{64,... | collective-permute-start | bytes 1572872 | tf_op jit(solution)/shard_map/ppermute | solution.py:42
  117.1 29.0 %collective-permute-start.15 = (bf16[1024,256]{1,0:T(8,128)(2,1)}, bf16[1024,256]{1,0:T(8,128)(2,1)S(1)}, u32[]{:S(2)}, u32[]{:S(2)}) collective-permute-start(bf16[1024,256]{1,0:T(8,128)(2,1)} %get-tuple-element.71), channel_id=1, source_target_pairs={{0,64},{8,72},{16,80},{24,88},{32,96},{40,104},{48,112},{56,120},{... | collective-permute-start | bytes 1572872 | tf_op jit(solution)/shard_map/ppermute | solution.py:42
  122.1 24.0 %collective-permute-start.16 = (bf16[1024,256]{1,0:T(8,128)(2,1)}, bf16[1024,256]{1,0:T(8,128)(2,1)}, u32[]{:S(2)}, u32[]{:S(2)}) collective-permute-start(bf16[1024,256]{1,0:T(8,128)(2,1)} %get-tuple-element.70), channel_id=1, source_target_pairs={{0,96},{8,104},{16,112},{24,120},{32,0},{40,8},{48,16},{56,24},{64... | collective-permute-start | bytes 1572872 | tf_op jit(solution)/shard_map/ppermute | solution.py:42
  132.8 1.3 copy-start.8
  134.1 33.9 %collective-permute-start.19 = (bf16[2,512,256]{2,1,0:T(8,128)(2,1)}, bf16[2,512,256]{2,1,0:T(8,128)(2,1)}, u32[]{:S(2)}, u32[]{:S(2)}) collective-permute-start(bf16[2,512,256]{2,1,0:T(8,128)(2,1)} %get-tuple-element.68), channel_id=1, source_target_pairs={{0,32},{8,40},{16,48},{24,56},{32,64},{40,72},{48,80},{56,88},{64,... | collective-permute-start | bytes 1572872 | tf_op jit(solution)/shard_map/ppermute | solution.py:42
  134.4 33.6 %collective-permute-start.20 = (bf16[2,512,256]{2,1,0:T(8,128)(2,1)}, bf16[2,512,256]{2,1,0:T(8,128)(2,1)}, u32[]{:S(2)}, u32[]{:S(2)}) collective-permute-start(bf16[2,512,256]{2,1,0:T(8,128)(2,1)} %get-tuple-element.67), channel_id=1, source_target_pairs={{0,64},{8,72},{16,80},{24,88},{32,96},{40,104},{48,112},{56,120},{... | collective-permute-start | bytes 1572872 | tf_op jit(solution)/shard_map/ppermute | solution.py:42
  138.2 29.7 %collective-permute-start.21 = (bf16[2,512,256]{2,1,0:T(8,128)(2,1)}, bf16[2,512,256]{2,1,0:T(8,128)(2,1)}, u32[]{:S(2)}, u32[]{:S(2)}) collective-permute-start(bf16[2,512,256]{2,1,0:T(8,128)(2,1)} %get-tuple-element.66), channel_id=1, source_target_pairs={{0,96},{8,104},{16,112},{24,120},{32,0},{40,8},{48,16},{56,24},{64... | collective-permute-start | bytes 1572872 | tf_op jit(solution)/shard_map/ppermute | solution.py:42
  159.4 8.6 %collective-permute-start.17 = (bf16[512,256]{1,0:T(8,128)(2,1)S(1)}, bf16[512,256]{1,0:T(8,128)(2,1)S(1)}, u32[]{:S(2)}, u32[]{:S(2)}) collective-permute-start(bf16[512,256]{1,0:T(8,128)(2,1)S(1)} %get-tuple-element.72), channel_id=1, source_target_pairs={{0,16},{8,24},{16,0},{24,8},{32,48},{40,56},{48,32},{56,40},{64,80... | collective-permute-start | bytes 786440 | tf_op jit(solution)/shard_map/ppermute | solution.py:42
  167.9 3.6 %copy-start.9 = (bf16[512,256]{1,0:T(8,128)(2,1)}, bf16[512,256]{1,0:T(8,128)(2,1)S(1)}, u32[]{:S(2)}) copy-start(bf16[512,256]{1,0:T(8,128)(2,1)S(1)} %collective-permute-done.17.rest_1_) | copy-start | bytes 786436
  169.7 16.4 %collective-permute-start.22 = (bf16[512,256]{1,0:T(8,128)(2,1)S(1)}, bf16[512,256]{1,0:T(8,128)(2,1)S(1)}, u32[]{:S(2)}, u32[]{:S(2)}) collective-permute-start(bf16[512,256]{1,0:T(8,128)(2,1)S(1)} %slice_bitcast_fusion), channel_id=1, source_target_pairs={{0,16},{8,24},{16,0},{24,8},{32,48},{40,56},{48,32},{56,40},{64,80... | collective-permute-start | bytes 786440 | tf_op jit(solution)/shard_map/ppermute | solution.py:42
  174.3 16.3 %all-to-all-start.1 = ((bf16[8,96,256]{2,1,0:T(8,128)(2,1)}), bf16[8,96,256]{2,1,0:T(8,128)(2,1)S(1)}, u32[]{:S(2)}, u32[]{:S(2)}) async-start(bf16[8,96,256]{2,1,0:T(8,128)(2,1)} %settle.1), calls=%async_computation.1 | async-start | bytes 786432 | tf_op jit(solution)/shard_map/all_to_all | solution.py:501
